TPU v7x, 512 devices: a whole 4x4x16 slice. The times are simulated.
512 devices in a mesh: span: 64 (over y, z), chord: 8 (over x, core).
Axes of the slice: x: 4, y: 4, z: 16, core: 2. Of those that a mesh axis runs over, the one named last changes fastest.
Arguments:
- schur: bfloat16 [64, 8, 1536, 1536], P('span', 'chord'), may hold values from -1 to 5, as said below
- loads: bfloat16 [64, 8, 64, 1536], P('span', 'chord'), may hold values from -24 to 24
- interface_rows: int32 [64, 8, 4, 384], P('span', 'chord'), may hold values from 0 to 1535, as said below
- edge_rows: int32 [64, 8, 4], P('span', 'chord'), may hold values from 0 to 384, as said below
- corner_rows: int32 [64, 8, 128], P('span', 'chord'), may hold values from 0 to 1535, as said below
- corner_map: int32 [64, 8, 128], P('span', 'chord'), may hold values from 0 to 383
- coarse_inverse: float32 [64, 384, 384], P('span', 'chord'), may hold values from -1 to 2, as said below
Outputs:
- solution: bfloat16 [64, 8, 64, 1536], P('span', 'chord')
Inputs may be any that keep to these rules, and one draw needn't show every extreme that they name: `schur`: each subdomain's matrix is symmetric positive definite. `interface_rows`: the 1536 entries of one subdomain are distinct. `edge_rows`: entry d is the number of live rows shared with the neighbour on side d; it equals that neighbour's entry for the opposite side, is 0 exactly where side d lies outside the grid, and some pairs of neighbours share all 384 rows. `corner_rows`: the 128 entries of one subdomain are distinct. `coarse_inverse`: each span index's matrix is symmetric positive definite.
All inputs are finite; a program needn't handle non-finite values.
Results may differ from a plain program's by a relative error of at most 0.0029.
Values may be sent and summed in bfloat16 or wider, within the bound.
No kernel may reach another device: no remote copies, remote signals or barrier semaphores. Data moves between devices by JAX's collectives and lax.ppermute only.
A program may use at most 64 MiB of HBM per device.

v0:
```python
import jax
import jax.numpy as jnp
from jax import lax
from jax.sharding import PartitionSpec as P

ITERS = 5


def with_halo(block, sides, width):
    for axis, dim in sides:
        count = lax.axis_size(axis)
        forward = [(i, i + 1) for i in range(count - 1)]
        backward = [(target, source) for source, target in forward]
        low = lax.ppermute(
            lax.slice_in_dim(block, block.shape[dim] - width, None, axis=dim), axis, forward
        )
        high = lax.ppermute(lax.slice_in_dim(block, 0, width, axis=dim), axis, backward)
        block = jnp.concatenate([low, block, high], axis=dim)
    return block


def case_sum(first, second):
    return lax.psum(jnp.sum(first * second, axis=1), ("span", "chord"))


def curve_sum(first, second):
    return lax.psum(jnp.sum(first * second, axis=1), ("span", "chord"))


def shards(schur, loads, interface_rows, edge_rows, corner_rows, corner_map, coarse_inverse):
    matrix = schur[0, 0]
    rows = interface_rows[0, 0]
    counts = edge_rows[0, 0]
    corners = corner_rows[0, 0]
    block = coarse_inverse[0]
    width = rows.shape[1]
    unknowns = matrix.shape[0]
    total_rows = block.shape[1]
    live = (jnp.arange(width, dtype=jnp.int32)[None, :] < counts[:, None]).astype(jnp.bfloat16)
    flat_rows = rows.reshape(-1)
    inv_diag = 1.0 / jnp.diagonal(matrix).astype(jnp.float32)
    onehot = (corner_map[0, 0][:, None] == jnp.arange(total_rows, dtype=jnp.int32)[None, :]).astype(
        jnp.float32
    )
    highest = lax.Precision.HIGHEST

    def precondition(resid):
        term = jnp.dot(resid[:, corners], onehot, precision=highest)
        summed = lax.psum(term, "chord")
        own_rows = jnp.dot(summed, block.T, precision=highest)
        lifted = lax.all_gather(own_rows, "chord", axis=1, tiled=True)
        back = jnp.dot(lifted, onehot.T, precision=highest)
        return (resid * inv_diag[None, :]).at[:, corners].add(back)

    resid = loads[0, 0].astype(jnp.float32)
    solution = jnp.zeros_like(resid)
    precond = precondition(resid)
    direction = precond
    norm_now = case_sum(resid, precond)
    for step in range(ITERS):
        rounded = direction.astype(jnp.bfloat16)
        picks = [rounded[:, rows[side]] * live[side][None, :] for side in range(4)]
        span_ext = with_halo(jnp.stack([picks[0], picks[1]]), (("span", 0),), 1)
        chord_ext = with_halo(jnp.stack([picks[2], picks[3]]), (("chord", 0),), 1)
        local = jnp.dot(rounded, matrix, preferred_element_type=jnp.float32)
        arrived = jnp.concatenate([span_ext[0], span_ext[3], chord_ext[0], chord_ext[3]], axis=1)
        coupled = (
            jnp.zeros((direction.shape[0], unknowns), jnp.float32)
            .at[:, flat_rows]
            .add(arrived.astype(jnp.float32))
        )
        image = local - coupled
        alpha = norm_now / curve_sum(direction, image)
        solution = solution + alpha[:, None] * direction
        resid = resid - alpha[:, None] * image
        if step + 1 < ITERS:
            precond = precondition(resid)
            norm_next = case_sum(resid, precond)
            direction = precond + (norm_next / norm_now)[:, None] * direction
            norm_now = norm_next
    return solution.astype(jnp.bfloat16)[None, None]


def solution(mesh):
    return jax.shard_map(
        shards,
        mesh=mesh,
        in_specs=(
            P("span", "chord", None, None),
            P("span", "chord", None, None),
            P("span", "chord", None, None),
            P("span", "chord", None),
            P("span", "chord", None),
            P("span", "chord", None),
            P("span", "chord", None),
        ),
        out_specs=P("span", "chord", None, None),
        check_vma=False,
    )
```

profile of v0, /device:TPU:1, one launch (start us, length us, event | category | flops | bytes accessed | tf_op | source)
XLA Modules:
  0.0 1566.5 jit_solution(3201410268036607082)
XLA Ops:
  10.9 23.8 %gather_fusion = bf16[1536]{0:T(1024)(128)(2,1)S(1)} fusion(bf16[1536,1536]{1,0:T(8,128)(2,1)} %bitcast.189, s32[1536]{0:T(1024)S(1)} %or_reduce_fusion), kind=kCustom, calls=%fused_computation | custom fusion | bytes 18432 | tf_op jit(solution)/shard_map/jit(diagonal)/cond/branch_0_fun/gather | solution.py:41
  35.2 52.7 %all-reduce.7.cloned.1.call-done = f32[64,384]{1,0:T(8,128)} async-done(((f32[64,384]{1,0:T(8,128)}), f32[64,384]{1,0:T(8,128)}) %all-reduce.7.cloned.1.call-update) | async-done | bytes 98320 | tf_op jit(solution)/shard_map/psum | solution.py:49
  89.1 15.4 all_gather.15
  108.0 2.2 collective-permute-start
  114.6 1.9 collective-permute-start.2
  118.2 2.4 collective-permute-start.3
  120.9 3.2 collective-permute-done.3
  124.1 11.6 scatter_custom_fusion.1
  136.0 3.4 multiply_reduce_fusion.7
  139.4 105.7 %all-reduce = (f32[64]{0:T(128)S(1)}, f32[64]{0:T(128)S(1)}) all-reduce(f32[64]{0:T(128)S(1)} %get-tuple-element.6, f32[64]{0:T(128)S(1)} %get-tuple-element.5), channel_id=1, replica_groups=mesh['span'=64,'chord'=8] {'span','chord'}, use_global_device_ids=true, to_apply=%region_3.4 | all-reduce | flops 128 | bytes 1024 | tf_op jit(solution)/shard_map/psum | solution.py:23
  247.4 66.9 %all-reduce.9.cloned.1.call-done = f32[64,384]{1,0:T(8,128)} async-done(((f32[64,384]{1,0:T(8,128)}), f32[64,384]{1,0:T(8,128)}) %all-reduce.9.cloned.1.call-update) | async-done | bytes 98320 | tf_op jit(solution)/shard_map/psum | solution.py:49
  315.5 15.9 %all_gather.16 = f32[64,384]{0,1:T(8,128)S(1)} all-gather(f32[64,48]{0,1:T(8,128)S(1)} %fusion.85), channel_id=1, replica_groups=mesh['span'=64,'chord'=8] {'chord'}, dimensions={1}, use_global_device_ids=true | all-gather | bytes 110592 | tf_op jit(solution)/shard_map/all_gather | solution.py:51
  333.6 103.1 %psum.109 = f32[64]{0:T(128)S(1)} all-reduce(f32[64]{0:T(128)S(1)} %multiply_reduce_fusion.6), channel_id=1, replica_groups=mesh['span'=64,'chord'=8] {'span','chord'}, use_global_device_ids=true, to_apply=%region_10.11 | all-reduce | flops 64 | bytes 512 | tf_op jit(solution)/shard_map/psum | solution.py:23
  446.3 3.6 collective-permute-start.6
  450.0 1.9 collective-permute-start.7
  452.0 4.0 collective-permute-done.7
  456.0 11.6 scatter_custom_fusion.3
  467.9 3.4 multiply_reduce_fusion.5
  471.3 103.0 %psum.110 = f32[64]{0:T(128)S(1)} all-reduce(f32[64]{0:T(128)S(1)} %get-tuple-element.32), channel_id=1, replica_groups=mesh['span'=64,'chord'=8] {'span','chord'}, use_global_device_ids=true, to_apply=%region_13.14 | all-reduce | flops 64 | bytes 512 | tf_op jit(solution)/shard_map/psum | solution.py:27
  576.6 65.9 %all-reduce.11.cloned.1.call-done = f32[64,384]{1,0:T(8,128)} async-done(((f32[64,384]{1,0:T(8,128)}), f32[64,384]{1,0:T(8,128)}) %all-reduce.11.cloned.1.call-update) | async-done | bytes 98320 | tf_op jit(solution)/shard_map/psum | solution.py:49
  643.6 15.4 all_gather.17
  661.5 103.1 %psum.112 = f32[64]{0:T(128)S(1)} all-reduce(f32[64]{0:T(128)S(1)} %multiply_reduce_fusion.4), channel_id=1, replica_groups=mesh['span'=64,'chord'=8] {'span','chord'}, use_global_device_ids=true, to_apply=%region_17.18 | all-reduce | flops 64 | bytes 512 | tf_op jit(solution)/shard_map/psum | solution.py:23
  774.2 3.6 collective-permute-start.10
  777.9 1.9 collective-permute-start.11
  779.9 4.0 collective-permute-done.11
  783.9 11.6 scatter_custom_fusion.5
  795.8 3.4 multiply_reduce_fusion.3
  799.1 103.0 %psum.113 = f32[64]{0:T(128)S(1)} all-reduce(f32[64]{0:T(128)S(1)} %get-tuple-element.34), channel_id=1, replica_groups=mesh['span'=64,'chord'=8] {'span','chord'}, use_global_device_ids=true, to_apply=%region_20.21 | all-reduce | flops 64 | bytes 512 | tf_op jit(solution)/shard_map/psum | solution.py:27
  904.4 65.9 %all-reduce.13.cloned.1.call-done = f32[64,384]{1,0:T(8,128)} async-done(((f32[64,384]{1,0:T(8,128)}), f32[64,384]{1,0:T(8,128)}) %all-reduce.13.cloned.1.call-update) | async-done | bytes 98320 | tf_op jit(solution)/shard_map/psum | solution.py:49
  971.5 15.4 all_gather.18
  989.1 103.3 %psum.115 = f32[64]{0:T(128)S(1)} all-reduce(f32[64]{0:T(128)S(1)} %multiply_reduce_fusion.2), channel_id=1, replica_groups=mesh['span'=64,'chord'=8] {'span','chord'}, use_global_device_ids=true, to_apply=%region_24.25 | all-reduce | flops 64 | bytes 512 | tf_op jit(solution)/shard_map/psum | solution.py:23
  1098.7 1.8 collective-permute-start.12
  1102.1 3.6 collective-permute-start.14
  1105.8 1.9 collective-permute-start.15
  1107.8 4.0 collective-permute-done.15
  1111.7 11.6 scatter_custom_fusion.7
  1123.6 3.4 multiply_reduce_fusion.1
  1127.0 103.0 %psum.116 = f32[64]{0:T(128)S(1)} all-reduce(f32[64]{0:T(128)S(1)} %get-tuple-element.36), channel_id=1, replica_groups=mesh['span'=64,'chord'=8] {'span','chord'}, use_global_device_ids=true, to_apply=%region_27.28 | all-reduce | flops 64 | bytes 512 | tf_op jit(solution)/shard_map/psum | solution.py:27
  1234.0 64.9 %all-reduce.15.cloned.1.call-done = f32[64,384]{1,0:T(8,128)} async-done(((f32[64,384]{1,0:T(8,128)}), f32[64,384]{1,0:T(8,128)}) %all-reduce.15.cloned.1.call-update) | async-done | bytes 98320 | tf_op jit(solution)/shard_map/psum | solution.py:49
  1300.0 15.4 all_gather.19
  1317.7 103.3 %psum.118 = f32[64]{0:T(128)S(1)} all-reduce(f32[64]{0:T(128)S(1)} %multiply_reduce_fusion), channel_id=1, replica_groups=mesh['span'=64,'chord'=8] {'span','chord'}, use_global_device_ids=true, to_apply=%region_31.32 | all-reduce | flops 64 | bytes 512 | tf_op jit(solution)/shard_map/psum | solution.py:23
  1427.3 1.8 collective-permute-start.16
  1430.6 3.6 collective-permute-start.18
  1434.4 1.9 collective-permute-start.19
  1436.3 4.0 collective-permute-done.19
  1440.3 11.6 scatter_custom_fusion.9
  1452.2 3.4 fusion.1
  1455.6 103.0 %psum.119 = f32[64]{0:T(128)S(1)} all-reduce(f32[64]{0:T(128)S(1)} %fusion.1), channel_id=1, replica_groups=mesh['span'=64,'chord'=8] {'span','chord'}, use_global_device_ids=true, to_apply=%region_34.35 | all-reduce | flops 64 | bytes 512 | tf_op jit(solution)/shard_map/psum | solution.py:27
  (166 shorter events, 77.3 us)
Async XLA Ops:
  6.5 81.4 %copy-start = (f32[1,48,384]{2,1,0:T(8,128)S(1)}, f32[1,48,384]{2,1,0:T(8,128)}, u32[]{:S(2)}) copy-start(f32[1,48,384]{2,1,0:T(8,128)} %param.13) | copy-start | bytes 221188
  6.5 28.2 %copy-start.1 = (bf16[1,1,64,1536]{3,2,1,0:T(8,128)(2,1)S(1)}, bf16[1,1,64,1536]{3,2,1,0:T(8,128)(2,1)}, u32[]{:S(2)}) copy-start(bf16[1,1,64,1536]{3,2,1,0:T(8,128)(2,1)} %param.8) | copy-start | bytes 589828
  6.5 98.0 %copy-start.2 = (s32[1,1,128]{2,1,0:T(1,128)S(1)}, s32[1,1,128]{2,1,0:T(1,128)}, u32[]{:S(2)}) copy-start(s32[1,1,128]{2,1,0:T(1,128)} %param.12) | copy-start | bytes 1540
  6.5 28.2 %copy-start.3 = (s32[1,1,4,384]{3,2,1,0:T(4,128)S(1)}, s32[1,1,4,384]{3,2,1,0:T(4,128)}, u32[]{:S(2)}) copy-start(s32[1,1,4,384]{3,2,1,0:T(4,128)} %param.9) | copy-start | bytes 18436
  6.5 28.2 %copy-start.4 = (s32[1,1,4]{2,1,0:T(1,128)S(1)}, s32[1,1,4]{2,1,0:T(1,128)}, u32[]{:S(2)}) copy-start(s32[1,1,4]{2,1,0:T(1,128)} %param.10) | copy-start | bytes 52
  6.5 81.4 %all-reduce.7.cloned.1.call-start = ((), (), s32[]{:S(2)}) async-start(), calls=%async_computation | async-start | bytes 196608 | tf_op jit(solution)/shard_map/psum | solution.py:49
  10.8 303.5 %all-reduce.9.cloned.1.call-start = ((), (), s32[]{:S(2)}) async-start(), calls=%async_computation.1 | async-start | bytes 196608 | tf_op jit(solution)/shard_map/psum | solution.py:49
  108.0 12.9 collective-permute-start
  111.8 9.1 collective-permute-start.1
  114.6 6.2 collective-permute-start.2
  118.2 5.9 collective-permute-start.3
  247.1 395.3 %all-reduce.11.cloned.1.call-start = ((), (), s32[]{:S(2)}) async-start(), calls=%async_computation.2 | async-start | bytes 196608 | tf_op jit(solution)/shard_map/psum | solution.py:49
  443.0 9.0 collective-permute-start.4
  444.9 7.1 collective-permute-start.5
  446.3 5.7 collective-permute-start.6
  450.0 5.9 collective-permute-start.7
  576.2 394.1 %all-reduce.13.cloned.1.call-start = ((), (), s32[]{:S(2)}) async-start(), calls=%async_computation.3 | async-start | bytes 196608 | tf_op jit(solution)/shard_map/psum | solution.py:49
  770.8 9.0 collective-permute-start.8
  772.7 7.1 collective-permute-start.9
  774.2 5.7 collective-permute-start.10
  777.9 5.9 collective-permute-start.11
  904.1 394.7 %all-reduce.15.cloned.1.call-start = ((), (), s32[]{:S(2)}) async-start(), calls=%async_computation.4 | async-start | bytes 196608 | tf_op jit(solution)/shard_map/psum | solution.py:49
  1098.7 9.0 collective-permute-start.12
  1100.6 7.1 collective-permute-start.13
  1102.1 5.7 collective-permute-start.14
  1105.8 5.9 collective-permute-start.15
  1427.3 9.0 collective-permute-start.16
  1429.2 7.1 collective-permute-start.17
  1430.6 5.7 collective-permute-start.18
  1434.4 5.9 collective-permute-start.19
Sparse Core Ops, SparseCore 0:
  10.9 77.0 all-reduce.6
  247.3 67.0 all-reduce.8
  576.4 66.0 all-reduce.10
  904.2 66.0 all-reduce.12
  1232.9 65.9 all-reduce.14
where the time goes:
time: 1580 us; the launch traced here: 1570 us
  blocking collectives  1010 us (64%)
  waiting for transfers between devices  335 us (21%)
  other arithmetic  72.7 us (5%)
  local copies, waits for them, and re-layouts  64 us (4%)
  starting transfers between devices  42.5 us (3%)
  matrix products  29.3 us (2%)
    psum x5, blocking collectives, case_sum(): return lax.psum(jnp.sum(first * second, axis=1), ('span', 'chord'))  518 us
    psum x4, blocking collectives, curve_sum(): return lax.psum(jnp.sum(first * second, axis=1), ('span', 'chord'))  412 us
    psum x5, waiting for transfers between devices, precondition(): summed = lax.psum(term, 'chord')  316 us
    all_gather x5, blocking collectives, precondition(): lifted = lax.all_gather(own_rows, 'chord', axis=1, tiled=True)  77.5 us
    scatter-add x5, other arithmetic, shards(): coupled = jnp.zeros((direction.shape[0], unknowns), jnp.float32).at[:, fl...  58.2 us
  transfers between devices with their start and end apart: 25, of which 10 were waited for; matrix products, arithmetic and copies ran while one was open for 2% of the time, Pallas kernels for 0%

commit v1 on v0

v1 whole, which is shorter than its diff:
```python
import functools

import jax
import jax.numpy as jnp
from jax import lax
from jax.experimental import pallas as pl
from jax.experimental.pallas import tpu as pltpu
from jax.sharding import PartitionSpec as P

ITERS = 5
F32 = jnp.float32
BF16 = jnp.bfloat16
PIVOT_FLOOR = 2e-5
GRAM_ROWS = 16


def with_halo(block, sides, width):
    for axis, dim in sides:
        count = lax.axis_size(axis)
        forward = [(i, i + 1) for i in range(count - 1)]
        backward = [(target, source) for source, target in forward]
        low = lax.ppermute(
            lax.slice_in_dim(block, block.shape[dim] - width, None, axis=dim), axis, forward
        )
        high = lax.ppermute(lax.slice_in_dim(block, 0, width, axis=dim), axis, backward)
        block = jnp.concatenate([low, block, high], axis=dim)
    return block


def case_sum(first, second):
    return lax.psum(jnp.sum(first * second, axis=1), ("span", "chord"))


def plain_recurrence(
    schur, loads, interface_rows, edge_rows, corner_rows, corner_map, coarse_inverse
):
    matrix = schur[0, 0]
    rows = interface_rows[0, 0]
    counts = edge_rows[0, 0]
    corners = corner_rows[0, 0]
    block = coarse_inverse[0]
    width = rows.shape[1]
    unknowns = matrix.shape[0]
    total_rows = block.shape[1]
    live = (jnp.arange(width, dtype=jnp.int32)[None, :] < counts[:, None]).astype(BF16)
    flat_rows = rows.reshape(-1)
    inv_diag = 1.0 / jnp.diagonal(matrix).astype(F32)
    onehot = (
        corner_map[0, 0][:, None] == jnp.arange(total_rows, dtype=jnp.int32)[None, :]
    ).astype(F32)
    highest = lax.Precision.HIGHEST

    def precondition(resid):
        term = jnp.dot(resid[:, corners], onehot, precision=highest)
        summed = lax.psum(term, "chord")
        own_rows = jnp.dot(summed, block.T, precision=highest)
        lifted = lax.all_gather(own_rows, "chord", axis=1, tiled=True)
        back = jnp.dot(lifted, onehot.T, precision=highest)
        return (resid * inv_diag[None, :]).at[:, corners].add(back)

    def apply_operator(direction):
        rounded = direction.astype(BF16)
        picks = [rounded[:, rows[side]] * live[side][None, :] for side in range(4)]
        span_ext = with_halo(jnp.stack([picks[0], picks[1]]), (("span", 0),), 1)
        chord_ext = with_halo(jnp.stack([picks[2], picks[3]]), (("chord", 0),), 1)
        local = jnp.dot(rounded, matrix, preferred_element_type=F32)
        arrived = jnp.concatenate([span_ext[0], span_ext[3], chord_ext[0], chord_ext[3]], axis=1)
        coupled = (
            jnp.zeros((direction.shape[0], unknowns), F32)
            .at[:, flat_rows]
            .add(arrived.astype(F32))
        )
        return local - coupled

    resid = loads[0, 0].astype(F32)
    result = jnp.zeros_like(resid)
    direction = precondition(resid)
    norm_now = case_sum(resid, direction)

    def step(_, carry):
        result, resid, direction, norm_now = carry
        image = apply_operator(direction)
        alpha = norm_now / case_sum(direction, image)
        result = result + alpha[:, None] * direction
        resid = resid - alpha[:, None] * image
        precond = precondition(resid)
        norm_next = case_sum(resid, precond)
        direction = precond + (norm_next / norm_now)[:, None] * direction
        return result, resid, direction, norm_next

    result, resid, direction, norm_now = lax.fori_loop(
        0, ITERS - 1, step, (result, resid, direction, norm_now)
    )
    alpha = norm_now / case_sum(direction, apply_operator(direction))
    return (result + alpha[:, None] * direction).astype(BF16)


NN = (((1,), (0,)), ((), ()))
NT = (((1,), (1,)), ((), ()))
TN = (((0,), (0,)), ((), ()))


def mm(first, second, dims=NN):
    return lax.dot_general(first, second, dims, preferred_element_type=F32)


def halves(value):
    high = value.astype(BF16)
    return high, (value - high.astype(F32)).astype(BF16)


def stacked(value):
    return jnp.concatenate(halves(value), axis=0)


def folded(value):
    half = value.shape[0] // 2
    return value[:half] + value[half:]


def whole(ref, cols=slice(None)):
    half = ref.shape[0] // 2
    return ref[:half, cols].astype(F32) + ref[half:, cols].astype(F32)


def call(body, outs, scratch=(), limit=28, flops=10**8):
    return pl.pallas_call(
        body,
        out_shape=outs,
        scratch_shapes=list(scratch),
        compiler_params=pltpu.CompilerParams(vmem_limit_bytes=limit * 2**20),
        cost_estimate=pl.CostEstimate(flops=flops, bytes_accessed=10**6, transcendentals=0),
    )


def shape(dims, dtype):
    return jax.ShapeDtypeStruct(dims, dtype)


def setup_kernel(
    schur, loads, rows, corners, slots, coarse, pick_ref, corner_ref, inv_ref, send_ref
):
    unknowns = schur.shape[0]
    lanes = corners.shape[1]
    tile = 128
    eye = lax.broadcasted_iota(jnp.int32, (tile, tile), 0) == lax.broadcasted_iota(
        jnp.int32, (tile, tile), 1
    )
    for start in range(0, unknowns, tile):
        block = schur[start : start + tile, start : start + tile].astype(F32)
        diag = jnp.sum(jnp.where(eye, block, 0.0), axis=0, keepdims=True)
        inv_ref[:, start : start + tile] = 1.0 / diag

    def build(step, _):
        start = pl.multiple_of(step * tile, tile)
        index = lax.broadcasted_iota(jnp.int32, (tile, unknowns), 0) + start
        pick_ref[pl.ds(start, tile), :] = (index == rows[...]).astype(F32).astype(BF16)
        index = lax.broadcasted_iota(jnp.int32, (tile, lanes), 0) + start
        corner_ref[pl.ds(start, tile), :] = (index == corners[...]).astype(F32).astype(BF16)
        return 0

    lax.fori_loop(0, unknowns // tile, build, 0)
    picked = mm(loads[...], corner_ref[...])
    cases = picked.shape[0]
    own, total = coarse.shape
    for peer in range(send_ref.shape[0]):
        send_ref[peer, :cases, :] = picked
        for part in range(total // lanes):
            send_ref[peer, cases + part * own : cases + (part + 1) * own, :] = coarse[
                :, part * lanes : (part + 1) * lanes
            ]
        send_ref[peer, cases + own * (total // lanes) :, :] = jnp.broadcast_to(
            slots[...].astype(F32), (8, lanes)
        )


def lift_kernel(slots, got, lift_ref, *, cases, own):
    peers, _, lanes = got.shape
    total = own * peers
    parts = total // lanes
    index = lax.broadcasted_iota(jnp.int32, (total, lanes), 0)
    mine = (index == slots[...]).astype(F32).astype(BF16)
    inverse = jnp.concatenate(
        [
            jnp.concatenate(
                [got[p, cases + q * own : cases + (q + 1) * own, :] for q in range(parts)], axis=1
            )
            for p in range(peers)
        ],
        axis=0,
    )
    high = inverse.astype(BF16)
    rest = inverse - high.astype(F32)
    middle, low = halves(rest)
    cols = (mm(high, mine) + mm(middle, mine)) + mm(low, mine)
    cols = jnp.concatenate(halves(cols), axis=1)
    base = cases + own * parts
    for peer in range(peers):
        theirs = got[peer, base : base + 1, :].astype(jnp.int32)
        theirs = (index == theirs).astype(F32).astype(BF16)
        lift_ref[peer * lanes : (peer + 1) * lanes, :] = mm(theirs, cols, TN).astype(BF16)


def precondition_kernel(got, lift, corner, pick, resid, inv, field_ref, *send_refs):
    peers = got.shape[0]
    cases = resid.shape[0]
    lanes = corner.shape[1]
    corners = jnp.concatenate([got[p, :cases, :] for p in range(peers)], axis=1)
    product = mm(stacked(corners), lift[...])
    back = folded(product[:, :lanes]) + product[:cases, lanes:]
    back = stacked(back)
    unknowns = resid.shape[1]
    width = unknowns // 4
    for side in range(4):
        cols = slice(side * width, (side + 1) * width)
        added = folded(mm(back, corner[cols, :], NT))
        value = resid[:, cols].astype(F32) * inv[:, cols] + added
        high, low = halves(value)
        field_ref[:cases, cols] = high
        field_ref[cases:, cols] = low
    for pair in range(2):
        cols = slice(2 * pair * width, 2 * (pair + 1) * width)
        sent = mm(field_ref[...], pick[:, cols]).astype(BF16)
        send_refs[2 * pair][...] = sent[:, :width]
        send_refs[2 * pair + 1][...] = sent[:, width:]


def gram_slot(row, col):
    return col * (col + 1) // 2 + row + 5 if row >= 0 else col


def local_kernel(*refs, step):
    field, matrix, loads, acc = refs[:4]
    last = step == ITERS - 1
    before = refs[4] if step else None
    images = refs[5 : 5 + step] if step else ()
    out_acc = refs[-1]
    cases = loads.shape[0]
    lane = lax.broadcasted_iota(jnp.int32, (cases, 128), 1)
    total = acc[...] if step else jnp.zeros((cases, 128), F32)

    def put(total, slot, value):
        return jnp.where(lane == slot, value, total)

    def product(first, second):
        return jnp.sum(first * second, axis=1, keepdims=True)

    local = folded(mm(field[...], matrix[...]))
    value = whole(field)
    if last:
        total = put(total, gram_slot(step, step), product(value, local))
    else:
        refs[-2][...] = local
    total = put(total, gram_slot(-1, step), product(value, loads[...].astype(F32)))
    for row in range(step):
        total = put(total, gram_slot(row, step), product(value, images[row][...]))
    if step:
        total = put(total, gram_slot(step - 1, step - 1), product(whole(before), images[-1][...]))
    out_acc[...] = total


def image_kernel(from0, from1, from2, from3, pick, corner, local, image_ref, send_ref, joined):
    width = from0.shape[1]
    for side, came in enumerate((from0, from1, from2, from3)):
        joined[:, side * width : (side + 1) * width] = came[...]
    unknowns = local.shape[1]
    chunk = 512
    for start in range(0, unknowns, chunk):
        cols = slice(start, start + chunk)
        image_ref[:, cols] = local[:, cols] - folded(mm(joined[...], pick[cols, :], NT))
    picked = folded(mm(stacked(image_ref[...]), corner[...]))
    for peer in range(send_ref.shape[0]):
        send_ref[peer] = picked


def gram_kernel(acc, sent0, from0, sent2, from2, send_ref):
    total = acc[...]
    lane = lax.broadcasted_iota(jnp.int32, total.shape, 1)
    pairs = whole(sent0) * whole(from0) + whole(sent2) * whole(from2)
    coupled = 2.0 * jnp.sum(pairs, axis=1, keepdims=True)
    slot = gram_slot(ITERS - 1, ITERS - 1)
    total = jnp.where(lane == slot, total - coupled, total).T
    packed = jnp.concatenate([total[:GRAM_ROWS], total[GRAM_ROWS : 2 * GRAM_ROWS]], axis=1)
    for peer in range(send_ref.shape[0]):
        send_ref[peer] = packed


def tree_sum(parts):
    while len(parts) > 1:
        parts = [a + b for a, b in zip(parts[::2], parts[1::2])] + parts[len(parts) & ~1 :]
    return parts[0]


def relay_kernel(got, send_ref):
    total = tree_sum([got[p] for p in range(got.shape[0])])
    for peer in range(send_ref.shape[0]):
        send_ref[peer] = total


def solve_kernel(got, *refs):
    fields = refs[:ITERS]
    out_ref, fault_ref = refs[ITERS:]
    total = tree_sum([got[p] for p in range(got.shape[0])])
    cases = out_ref.shape[0]

    def entry(row, col):
        slot = gram_slot(row, col)
        half, at = divmod(slot, GRAM_ROWS)
        return total[at : at + 1, half * cases : (half + 1) * cases]

    n = ITERS
    scale = [lax.rsqrt(entry(k, k)) for k in range(n)]
    rhs = [entry(-1, k) * scale[k] for k in range(n)]
    lower, pivots, solved = {}, [], []
    fault = jnp.zeros_like(rhs[0])
    for k in range(n):
        for j in range(k):
            value = (entry(j, k) * scale[j]) * scale[k]
            for m in range(j):
                value = value - (lower[k, m] * pivots[m]) * lower[j, m]
            lower[k, j] = value / pivots[j]
        pivot = jnp.ones_like(rhs[0])
        value = rhs[k]
        for m in range(k):
            pivot = pivot - (lower[k, m] * pivots[m]) * lower[k, m]
            value = value - lower[k, m] * solved[m]
        pivots.append(pivot)
        solved.append(value)
        good = (pivot > PIVOT_FLOOR) & (scale[k] > 0.0) & (scale[k] < 1e30)
        fault = jnp.maximum(fault, jnp.where(good, 0.0, 1.0))
    coeffs = [solved[k] / pivots[k] for k in range(n)]
    for k in reversed(range(n)):
        for m in range(k + 1, n):
            coeffs[k] = coeffs[k] - lower[m, k] * coeffs[m]
    coeffs = [coeffs[k] * scale[k] for k in range(n)]
    for k in range(n):
        good = jnp.abs(coeffs[k]) < 1e37
        fault = jnp.maximum(fault, jnp.where(good, 0.0, 1.0))
    fault_ref[0, 0] = jnp.max(fault)
    spread = jnp.concatenate(coeffs + [jnp.zeros_like(coeffs[0])] * (8 - n), axis=0)
    spread = jnp.concatenate([spread, jnp.zeros_like(spread)], axis=1).T[:cases]
    width = out_ref.shape[1] // 4
    for part in range(4):
        cols = slice(part * width, (part + 1) * width)
        value = spread[:, 0:1] * whole(fields[0], cols)
        for k in range(1, n):
            value = value + spread[:, k : k + 1] * whole(fields[k], cols)
        out_ref[:, cols] = value.astype(BF16)


def ring(axis, shift):
    count = lax.axis_size(axis)
    return [(i, (i + shift) % count) for i in range(count)]


def exchange(send, axis, groups=None):
    return lax.all_to_all(send, axis, 0, 0, axis_index_groups=groups)


def sum_groups(span, chord, inner):
    outer = span // inner
    first = [
        [(o * inner + i) * chord + c for o in range(outer) for c in range(chord)]
        for i in range(inner)
    ]
    second = [[o * inner + i for i in range(inner)] for o in range(outer)]
    return first, second


def shards(schur, loads, interface_rows, edge_rows, corner_rows, corner_map, coarse_inverse):
    originals = (
        schur, loads, interface_rows, edge_rows, corner_rows, corner_map, coarse_inverse
    )
    span, chord = lax.axis_size("span"), lax.axis_size("chord")
    matrix, rhs, block = schur[0, 0], loads[0, 0], coarse_inverse[0]
    unknowns = matrix.shape[0]
    cases = rhs.shape[0]
    rows, counts = interface_rows[0, 0], edge_rows[0, 0]
    width = rows.shape[1]
    lanes = corner_rows.shape[2]
    own, total = block.shape
    live = jnp.arange(width, dtype=jnp.int32)[None, :] < counts[:, None]
    live_rows = jnp.where(live, rows, -1).reshape(1, unknowns)
    slots = corner_map[0]

    pick, corner, inv, send = call(
        setup_kernel,
        (
            shape((unknowns, unknowns), BF16),
            shape((unknowns, lanes), BF16),
            shape((1, unknowns), F32),
            shape((chord, cases + own * (total // lanes) + 8, lanes), F32),
        ),
    )(matrix, rhs, live_rows, corner_rows[0], slots, block)
    got = exchange(send, "chord")
    lift = call(
        functools.partial(lift_kernel, cases=cases, own=own),
        shape((chord * lanes, 2 * lanes), BF16),
    )(slots, got)

    resid = rhs
    fields, images = [], []
    acc = jnp.zeros((cases, 128), F32)
    for step in range(ITERS):
        field, *sends = call(
            precondition_kernel,
            (shape((2 * cases, unknowns), BF16),) + (shape((2 * cases, width), BF16),) * 4,
        )(got, lift, corner, pick, resid, inv)
        last = step == ITERS - 1
        came = [
            lax.ppermute(sends[1], "span", ring("span", 1)),
            None if last else lax.ppermute(sends[0], "span", ring("span", -1)),
            lax.ppermute(sends[3], "chord", ring("chord", 1)),
            None if last else lax.ppermute(sends[2], "chord", ring("chord", -1)),
        ]
        out = (shape((cases, 128), F32),)
        if not last:
            out = (shape((cases, unknowns), F32),) + out
        before = (fields[-1],) if step else ()
        result = call(functools.partial(local_kernel, step=step), out)(
            field, matrix, rhs, acc, *before, *images
        )
        acc = result[-1]
        fields.append(field)
        if not last:
            resid, send = call(
                image_kernel,
                (shape((cases, unknowns), F32), shape((chord, cases, lanes), F32)),
                scratch=[pltpu.VMEM((2 * cases, unknowns), BF16)],
            )(*came, pick, corner, result[0])
            images.append(resid)
            got = exchange(send, "chord")

    inner = 16 if span % 16 == 0 else span
    first, second = sum_groups(span, chord, inner)
    send = call(gram_kernel, shape((len(first[0]), GRAM_ROWS, 128), F32))(
        acc, sends[0], came[0], sends[2], came[2]
    )
    got = exchange(send, ("span", "chord"), first)
    send = call(relay_kernel, shape((inner, GRAM_ROWS, 128), F32))(got)
    got = exchange(send, "span", second)
    answer, fault = pl.pallas_call(
        solve_kernel,
        out_shape=(shape((cases, unknowns), BF16), shape((1, 1), F32)),
        out_specs=(
            pl.BlockSpec(memory_space=pltpu.VMEM),
            pl.BlockSpec(memory_space=pltpu.SMEM),
        ),
        compiler_params=pltpu.CompilerParams(vmem_limit_bytes=28 * 2**20),
    )(got, *fields)
    answer = lax.cond(
        fault[0, 0] > 0.0,
        lambda answer, *arrays: plain_recurrence(*arrays),
        lambda answer, *arrays: answer,
        answer,
        *originals,
    )
    return answer[None, None]


def solution(mesh):
    return jax.shard_map(
        shards,
        mesh=mesh,
        in_specs=(
            P("span", "chord", None, None),
            P("span", "chord", None, None),
            P("span", "chord", None, None),
            P("span", "chord", None),
            P("span", "chord", None),
            P("span", "chord", None),
            P("span", "chord", None),
        ),
        out_specs=P("span", "chord", None, None),
        check_vma=False,
    )
```

time: 1580 us -> 207 us (0.13)
  blocking collectives: 1010 us -> 81.7 us
  waiting for transfers between devices: 335 us -> 30.7 us
  other arithmetic: 72.7 us -> 0.78 us
  local copies, waits for them, and re-layouts: 64 us -> 1.41 us
  matrix products: 29.3 us -> 0 us
  Pallas kernels: 0 us -> 25.1 us
    psum x9 -> x0, blocking collectives: 930 us -> none  [the longest x5 518 us: case_sum(): return lax.psum(jnp.sum(first * second, axis=1), ('span', 'chord'))]
    psum x5 -> x0, waiting for transfers between devices: 316 us -> none  [precondition(): summed = lax.psum(term, 'chord')]
    all_to_all x0 -> x6, blocking collectives: none -> 81.7 us  [exchange(): return lax.all_to_all(send, axis, 0, 0, axis_index_groups=groups)]
    all_gather x5 -> x0, blocking collectives: 77.5 us -> none  [precondition(): lifted = lax.all_gather(own_rows, 'chord', axis=1, tiled=True)]
    scatter-add x10 -> x0, other arithmetic: 66.2 us -> none  [the longest x5 58.2 us: shards(): coupled = jnp.zeros((direction.shape[0], unknowns), jnp.float32).at[:, fl...]
    gather x26 -> x0, local copies, waits for them, and re-layouts: 56.1 us -> none  [the longest x20 28.9 us: shards(): picks = [rounded[:, rows[side]] * live[side][None, :] for side in range(4)]]
    dot_general x20 -> x0, matrix products: 29.3 us -> none  [the longest x5 17 us: shards(): local = jnp.dot(rounded, matrix, preferred_element_type=jnp.float32)]
    pallas_call x0 -> x19, Pallas kernels: none -> 25.1 us  [the longest x4 7.15 us: shards(): call(image_kernel, (shape((cases, unknowns), F32), shape((chord, cases, l...]
  transfers between devices with their start and end apart: 25 -> 19, of which waited for: 10 -> 10; matrix products, arithmetic and copies ran while one was open for 2% -> 0% of each run, Pallas kernels for 0% -> 2%
where the time goes in v1:
time: 207 us; the launch traced here: 205 us
  blocking collectives  81.7 us (39%)
  starting transfers between devices  51.1 us (25%)
  waiting for transfers between devices  30.7 us (15%)
  Pallas kernels  25.1 us (12%)
  between operations  14.3 us (7%)
    all_to_all x6, blocking collectives, exchange(): return lax.all_to_all(send, axis, 0, 0, axis_index_groups=groups)  81.7 us
    ppermute x4, starting transfers between devices, shards(): lax.ppermute(sends[0], 'span', ring('span', -1))  30.1 us
    all_to_all x1, waiting for transfers between devices, exchange(): return lax.all_to_all(send, axis, 0, 0, axis_index_groups=groups)  12.4 us
    ppermute x4, waiting for transfers between devices, shards(): lax.ppermute(sends[2], 'chord', ring('chord', -1))  10.8 us
    ppermute x5, starting transfers between devices, shards(): lax.ppermute(sends[1], 'span', ring('span', 1))  9.6 us
    ppermute x5, starting transfers between devices, shards(): lax.ppermute(sends[3], 'chord', ring('chord', 1))  7.84 us
    pallas_call x4, Pallas kernels, shards(): call(image_kernel, (shape((cases, unknowns), F32), shape((chord, cases, l...  7.15 us
    pallas_call x5, Pallas kernels, shards(): call(precondition_kernel, (shape((2 * cases, unknowns), BF16),) + (shape(...  6.22 us
  transfers between devices with their start and end apart: 19, of which 10 were waited for; matrix products, arithmetic and copies ran while one was open for 0% of the time, Pallas kernels for 2%

profile of v1, /device:TPU:1, one launch (start us, length us, event | category | flops | bytes accessed | tf_op | source)
XLA Modules:
  0.0 205.4 jit_solution(6175362506021261286)
XLA Ops:
  6.5 0.8 fusion.52
  8.0 3.8 %shard_map.75 = (bf16[1536,1536]{1,0:T(8,128)(2,1)S(1)}, bf16[1536,128]{1,0:T(8,128)(2,1)S(1)}, f32[1,1536]{1,0:T(1,128)S(1)}, f32[8,216,128]{2,1,0:T(8,128)S(1)}) custom-call(bf16[1536,1536]{1,0:T(8,128)(2,1)} %bitcast.155, bf16[64,1536]{1,0:T(8,128)(2,1)} %bitcast.166, s32[1,1536]{1,0:T(1,128)S(1)} %broadcast_select_fusion.rows, ...), custom_call_target="tpu_custom_call" | custom-call | flops 100000000 | bytes 1000000 | tf_op jit(solution)/shard_map/pallas_call | solution.py:386
  11.9 22.8 %all_to_all.35.got = f32[8,216,128]{2,1,0:T(8,128)S(1)} all-to-all(f32[8,216,128]{2,1,0:T(8,128)S(1)} %get-tuple-element.148), channel_id=1, replica_groups=mesh['span'=64,'chord'=8] {'chord'}, dimensions={0} | all-to-all | bytes 1769472 | tf_op jit(solution)/shard_map/all_to_all | solution.py:357
  34.6 1.5 shard_map.76.lift
  36.1 1.2 shard_map.77
  37.4 1.9 collective-permute-start.8
  39.3 9.9 %collective-permute-start.9 = (bf16[128,384]{1,0:T(8,128)(2,1)S(1)}, bf16[128,384]{1,0:T(8,128)(2,1)S(1)}, u32[]{:S(2)}, u32[]{:S(2)}) collective-permute-start(bf16[128,384]{1,0:T(8,128)(2,1)S(1)} %get-tuple-element.153), channel_id=1, source_target_pairs={{0,504},{8,0},{16,8},{24,16},{32,24},{40,32},{48,40},{56,48},{64,5... | collective-permute-start | bytes 294920 | tf_op jit(solution)/shard_map/ppermute | solution.py:412
  49.2 1.3 collective-permute-start.10
  50.5 0.8 shard_map.78
  51.4 0.8 collective-permute-done.10.from2
  52.2 2.7 %collective-permute-done.11.from3 = bf16[128,384]{1,0:T(8,128)(2,1)S(1)} collective-permute-done((bf16[128,384]{1,0:T(8,128)(2,1)S(1)}, bf16[128,384]{1,0:T(8,128)(2,1)S(1)}, u32[]{:S(2)}, u32[]{:S(2)}) %collective-permute-start.11) | collective-permute-done | bytes 98336 | tf_op jit(solution)/shard_map/ppermute | solution.py:414
  54.9 1.8 shard_map.79
  56.7 11.3 %all_to_all.36.got = f32[8,64,128]{2,1,0:T(8,128)S(1)} all-to-all(f32[8,64,128]{2,1,0:T(8,128)S(1)} %get-tuple-element.158), channel_id=1, replica_groups=mesh['span'=64,'chord'=8] {'chord'}, dimensions={0} | all-to-all | bytes 524288 | tf_op jit(solution)/shard_map/all_to_all | solution.py:357
  67.9 1.2 shard_map.80
  69.2 1.9 collective-permute-start.12
  71.1 6.7 %collective-permute-start.13 = (bf16[128,384]{1,0:T(8,128)(2,1)S(1)}, bf16[128,384]{1,0:T(8,128)(2,1)S(1)}, u32[]{:S(2)}, u32[]{:S(2)}) collective-permute-start(bf16[128,384]{1,0:T(8,128)(2,1)S(1)} %get-tuple-element.161), channel_id=1, source_target_pairs={{0,504},{8,0},{16,8},{24,16},{32,24},{40,32},{48,40},{56,48},{64,5... | collective-permute-start | bytes 294920 | tf_op jit(solution)/shard_map/ppermute | solution.py:412
  77.8 1.8 collective-permute-start.14
  79.6 0.9 shard_map.81
  80.4 0.8 collective-permute-done.14.from2
  81.2 2.7 %collective-permute-done.15.from3 = bf16[128,384]{1,0:T(8,128)(2,1)S(1)} collective-permute-done((bf16[128,384]{1,0:T(8,128)(2,1)S(1)}, bf16[128,384]{1,0:T(8,128)(2,1)S(1)}, u32[]{:S(2)}, u32[]{:S(2)}) %collective-permute-start.15) | collective-permute-done | bytes 98336 | tf_op jit(solution)/shard_map/ppermute | solution.py:414
  83.9 1.8 shard_map.82
  85.7 11.3 %all_to_all.37.got = f32[8,64,128]{2,1,0:T(8,128)S(1)} all-to-all(f32[8,64,128]{2,1,0:T(8,128)S(1)} %get-tuple-element.167), channel_id=1, replica_groups=mesh['span'=64,'chord'=8] {'chord'}, dimensions={0} | all-to-all | bytes 524288 | tf_op jit(solution)/shard_map/all_to_all | solution.py:357
  97.0 1.2 shard_map.83
  98.2 1.9 collective-permute-start.16
  100.2 6.7 %collective-permute-start.17 = (bf16[128,384]{1,0:T(8,128)(2,1)S(1)}, bf16[128,384]{1,0:T(8,128)(2,1)S(1)}, u32[]{:S(2)}, u32[]{:S(2)}) collective-permute-start(bf16[128,384]{1,0:T(8,128)(2,1)S(1)} %get-tuple-element.170), channel_id=1, source_target_pairs={{0,504},{8,0},{16,8},{24,16},{32,24},{40,32},{48,40},{56,48},{64,5... | collective-permute-start | bytes 294920 | tf_op jit(solution)/shard_map/ppermute | solution.py:412
  106.9 1.8 collective-permute-start.18
  108.6 0.9 shard_map.84
  109.5 0.7 collective-permute-done.18.from2
  110.3 2.7 %collective-permute-done.19.from3 = bf16[128,384]{1,0:T(8,128)(2,1)S(1)} collective-permute-done((bf16[128,384]{1,0:T(8,128)(2,1)S(1)}, bf16[128,384]{1,0:T(8,128)(2,1)S(1)}, u32[]{:S(2)}, u32[]{:S(2)}) %collective-permute-start.19) | collective-permute-done | bytes 98336 | tf_op jit(solution)/shard_map/ppermute | solution.py:414
  113.0 1.8 shard_map.85
  114.8 11.3 %all_to_all.38.got = f32[8,64,128]{2,1,0:T(8,128)S(1)} all-to-all(f32[8,64,128]{2,1,0:T(8,128)S(1)} %get-tuple-element.176), channel_id=1, replica_groups=mesh['span'=64,'chord'=8] {'chord'}, dimensions={0} | all-to-all | bytes 524288 | tf_op jit(solution)/shard_map/all_to_all | solution.py:357
  126.0 1.2 shard_map.86
  127.3 1.9 collective-permute-start.20
  129.2 6.9 %collective-permute-start.21 = (bf16[128,384]{1,0:T(8,128)(2,1)S(1)}, bf16[128,384]{1,0:T(8,128)(2,1)S(1)}, u32[]{:S(2)}, u32[]{:S(2)}) collective-permute-start(bf16[128,384]{1,0:T(8,128)(2,1)S(1)} %get-tuple-element.179), channel_id=1, source_target_pairs={{0,504},{8,0},{16,8},{24,16},{32,24},{40,32},{48,40},{56,48},{64,5... | collective-permute-start | bytes 294920 | tf_op jit(solution)/shard_map/ppermute | solution.py:412
  136.1 1.8 collective-permute-start.22
  137.9 0.9 shard_map.87
  139.5 2.7 %collective-permute-done.23.from3 = bf16[128,384]{1,0:T(8,128)(2,1)S(1)} collective-permute-done((bf16[128,384]{1,0:T(8,128)(2,1)S(1)}, bf16[128,384]{1,0:T(8,128)(2,1)S(1)}, u32[]{:S(2)}, u32[]{:S(2)}) %collective-permute-start.23) | collective-permute-done | bytes 98336 | tf_op jit(solution)/shard_map/ppermute | solution.py:414
  142.2 1.8 shard_map.88
  144.0 11.3 %all_to_all.39.got = f32[8,64,128]{2,1,0:T(8,128)S(1)} all-to-all(f32[8,64,128]{2,1,0:T(8,128)S(1)} %get-tuple-element.185), channel_id=1, replica_groups=mesh['span'=64,'chord'=8] {'chord'}, dimensions={0} | all-to-all | bytes 524288 | tf_op jit(solution)/shard_map/all_to_all | solution.py:357
  155.3 1.2 shard_map.89
  156.5 1.9 collective-permute-start.24
  158.5 1.2 collective-permute-start.25
  159.7 1.0 shard_map.90.acc
  160.7 4.5 %collective-permute-done.24.from0 = bf16[128,384]{1,0:T(8,128)(2,1)S(1)} collective-permute-done((bf16[128,384]{1,0:T(8,128)(2,1)S(1)}, bf16[128,384]{1,0:T(8,128)(2,1)S(1)}, u32[]{:S(2)}, u32[]{:S(2)}) %collective-permute-start.24) | collective-permute-done | bytes 98336 | tf_op jit(solution)/shard_map/ppermute | solution.py:411
  165.5 13.8 %all_to_all.40.got = f32[32,16,128]{2,1,0:T(8,128)S(1)} all-to-all(f32[32,16,128]{2,1,0:T(8,128)S(1)} %shard_map.91), channel_id=1, replica_groups={{0,1,2,3,4,5,6,7,128,129,130,131,132,133,134,135,256,257,258,259,260,26..., dimensions={0} | all-to-all | bytes 524288 | tf_op jit(solution)/shard_map/all_to_all | solution.py:357
  180.0 3.5 %all-to-all-start.6 = ((f32[16,16,128]{2,1,0:T(8,128)}), f32[16,16,128]{2,1,0:T(8,128)S(1)}, u32[]{:S(2)}, u32[]{:S(2)}) async-start(f32[16,16,128]{2,1,0:T(8,128)} %shard_map.92), calls=%async_computation.6 | async-start | bytes 262144 | tf_op jit(solution)/shard_map/all_to_all | solution.py:357
  183.5 12.4 %all-to-all-done.6.got = f32[16,16,128]{2,1,0:T(8,128)S(1)} async-done(((f32[16,16,128]{2,1,0:T(8,128)}), f32[16,16,128]{2,1,0:T(8,128)S(1)}, u32[]{:S(2)}, u32[]{:S(2)}) %all-to-all-start.6) | async-done | bytes 131104 | tf_op jit(solution)/shard_map/all_to_all | solution.py:357
  195.9 1.0 shard_map.93
  (34 shorter events, 3.4 us)
Async XLA Ops:
  6.5 29.6 %copy-start.1 = (bf16[1,1,64,1536]{3,2,1,0:T(8,128)(2,1)S(1)}, bf16[1,1,64,1536]{3,2,1,0:T(8,128)(2,1)}, u32[]{:S(2)}) copy-start(bf16[1,1,64,1536]{3,2,1,0:T(8,128)(2,1)} %param.12) | copy-start | bytes 589828
  8.0 42.5 %slice-start = ((s8[4718592]{0:T(1024)(128)(4,1)}), s8[4194304]{0:T(1024)(128)(4,1)S(1)}, s32[]{:S(2)}) async-start(s8[4718592]{0:T(1024)(128)(4,1)} %bitcast.156), calls=%async_computation.9 | async-start | bytes 8388608
  34.6 15.9 %slice-start.1 = ((s8[4718592]{0:T(1024)(128)(4,1)}), s8[524288]{0:T(1024)(128)(4,1)S(1)}, s32[]{:S(2)}) async-start(s8[4718592]{0:T(1024)(128)(4,1)} %bitcast.156), calls=%async_computation.10 | async-start | bytes 1048576
  37.4 13.9 %collective-permute-start.8 = (bf16[128,384]{1,0:T(8,128)(2,1)S(1)}, bf16[128,384]{1,0:T(8,128)(2,1)S(1)}, u32[]{:S(2)}, u32[]{:S(2)}) collective-permute-start(bf16[128,384]{1,0:T(8,128)(2,1)S(1)} %get-tuple-element.152), channel_id=1, source_target_pairs={{0,8},{8,16},{16,24},{24,32},{32,40},{40,48},{48,56},{56,64},{64,7... | collective-permute-start | bytes 294920 | tf_op jit(solution)/shard_map/ppermute | solution.py:411
  39.3 12.0 %collective-permute-start.9 = (bf16[128,384]{1,0:T(8,128)(2,1)S(1)}, bf16[128,384]{1,0:T(8,128)(2,1)S(1)}, u32[]{:S(2)}, u32[]{:S(2)}) collective-permute-start(bf16[128,384]{1,0:T(8,128)(2,1)S(1)} %get-tuple-element.153), channel_id=1, source_target_pairs={{0,504},{8,0},{16,8},{24,16},{32,24},{40,32},{48,40},{56,48},{64,5... | collective-permute-start | bytes 294920 | tf_op jit(solution)/shard_map/ppermute | solution.py:412
  49.2 2.9 %collective-permute-start.10 = (bf16[128,384]{1,0:T(8,128)(2,1)S(1)}, bf16[128,384]{1,0:T(8,128)(2,1)S(1)}, u32[]{:S(2)}, u32[]{:S(2)}) collective-permute-start(bf16[128,384]{1,0:T(8,128)(2,1)S(1)} %get-tuple-element.154), channel_id=1, source_target_pairs={{0,1},{1,2},{2,3},{3,4},{4,5},{5,6},{6,7},{7,0},{8,9},{9,10},{10,1... | collective-permute-start | bytes 294920 | tf_op jit(solution)/shard_map/ppermute | solution.py:413
  50.5 4.3 %collective-permute-start.11 = (bf16[128,384]{1,0:T(8,128)(2,1)S(1)}, bf16[128,384]{1,0:T(8,128)(2,1)S(1)}, u32[]{:S(2)}, u32[]{:S(2)}) collective-permute-start(bf16[128,384]{1,0:T(8,128)(2,1)S(1)} %get-tuple-element.155), channel_id=1, source_target_pairs={{0,7},{1,0},{2,1},{3,2},{4,3},{5,4},{6,5},{7,6},{8,15},{9,8},{10,9... | collective-permute-start | bytes 294920 | tf_op jit(solution)/shard_map/ppermute | solution.py:414
  69.2 11.3 %collective-permute-start.12 = (bf16[128,384]{1,0:T(8,128)(2,1)S(1)}, bf16[128,384]{1,0:T(8,128)(2,1)S(1)}, u32[]{:S(2)}, u32[]{:S(2)}) collective-permute-start(bf16[128,384]{1,0:T(8,128)(2,1)S(1)} %get-tuple-element.160), channel_id=1, source_target_pairs={{0,8},{8,16},{16,24},{24,32},{32,40},{40,48},{48,56},{56,64},{64,7... | collective-permute-start | bytes 294920 | tf_op jit(solution)/shard_map/ppermute | solution.py:411
  71.1 9.3 %collective-permute-start.13 = (bf16[128,384]{1,0:T(8,128)(2,1)S(1)}, bf16[128,384]{1,0:T(8,128)(2,1)S(1)}, u32[]{:S(2)}, u32[]{:S(2)}) collective-permute-start(bf16[128,384]{1,0:T(8,128)(2,1)S(1)} %get-tuple-element.161), channel_id=1, source_target_pairs={{0,504},{8,0},{16,8},{24,16},{32,24},{40,32},{48,40},{56,48},{64,5... | collective-permute-start | bytes 294920 | tf_op jit(solution)/shard_map/ppermute | solution.py:412
  77.8 3.4 %collective-permute-start.14 = (bf16[128,384]{1,0:T(8,128)(2,1)S(1)}, bf16[128,384]{1,0:T(8,128)(2,1)S(1)}, u32[]{:S(2)}, u32[]{:S(2)}) collective-permute-start(bf16[128,384]{1,0:T(8,128)(2,1)S(1)} %get-tuple-element.162), channel_id=1, source_target_pairs={{0,1},{1,2},{2,3},{3,4},{4,5},{5,6},{6,7},{7,0},{8,9},{9,10},{10,1... | collective-permute-start | bytes 294920 | tf_op jit(solution)/shard_map/ppermute | solution.py:413
  79.6 4.3 %collective-permute-start.15 = (bf16[128,384]{1,0:T(8,128)(2,1)S(1)}, bf16[128,384]{1,0:T(8,128)(2,1)S(1)}, u32[]{:S(2)}, u32[]{:S(2)}) collective-permute-start(bf16[128,384]{1,0:T(8,128)(2,1)S(1)} %get-tuple-element.163), channel_id=1, source_target_pairs={{0,7},{1,0},{2,1},{3,2},{4,3},{5,4},{6,5},{7,6},{8,15},{9,8},{10,9... | collective-permute-start | bytes 294920 | tf_op jit(solution)/shard_map/ppermute | solution.py:414
  98.2 11.3 %collective-permute-start.16 = (bf16[128,384]{1,0:T(8,128)(2,1)S(1)}, bf16[128,384]{1,0:T(8,128)(2,1)S(1)}, u32[]{:S(2)}, u32[]{:S(2)}) collective-permute-start(bf16[128,384]{1,0:T(8,128)(2,1)S(1)} %get-tuple-element.169), channel_id=1, source_target_pairs={{0,8},{8,16},{16,24},{24,32},{32,40},{40,48},{48,56},{56,64},{64,7... | collective-permute-start | bytes 294920 | tf_op jit(solution)/shard_map/ppermute | solution.py:411
  100.2 9.4 %collective-permute-start.17 = (bf16[128,384]{1,0:T(8,128)(2,1)S(1)}, bf16[128,384]{1,0:T(8,128)(2,1)S(1)}, u32[]{:S(2)}, u32[]{:S(2)}) collective-permute-start(bf16[128,384]{1,0:T(8,128)(2,1)S(1)} %get-tuple-element.170), channel_id=1, source_target_pairs={{0,504},{8,0},{16,8},{24,16},{32,24},{40,32},{48,40},{56,48},{64,5... | collective-permute-start | bytes 294920 | tf_op jit(solution)/shard_map/ppermute | solution.py:412
  106.9 3.4 %collective-permute-start.18 = (bf16[128,384]{1,0:T(8,128)(2,1)S(1)}, bf16[128,384]{1,0:T(8,128)(2,1)S(1)}, u32[]{:S(2)}, u32[]{:S(2)}) collective-permute-start(bf16[128,384]{1,0:T(8,128)(2,1)S(1)} %get-tuple-element.171), channel_id=1, source_target_pairs={{0,1},{1,2},{2,3},{3,4},{4,5},{5,6},{6,7},{7,0},{8,9},{9,10},{10,1... | collective-permute-start | bytes 294920 | tf_op jit(solution)/shard_map/ppermute | solution.py:413
  108.6 4.3 %collective-permute-start.19 = (bf16[128,384]{1,0:T(8,128)(2,1)S(1)}, bf16[128,384]{1,0:T(8,128)(2,1)S(1)}, u32[]{:S(2)}, u32[]{:S(2)}) collective-permute-start(bf16[128,384]{1,0:T(8,128)(2,1)S(1)} %get-tuple-element.172), channel_id=1, source_target_pairs={{0,7},{1,0},{2,1},{3,2},{4,3},{5,4},{6,5},{7,6},{8,15},{9,8},{10,9... | collective-permute-start | bytes 294920 | tf_op jit(solution)/shard_map/ppermute | solution.py:414
  127.3 11.5 %collective-permute-start.20 = (bf16[128,384]{1,0:T(8,128)(2,1)S(1)}, bf16[128,384]{1,0:T(8,128)(2,1)S(1)}, u32[]{:S(2)}, u32[]{:S(2)}) collective-permute-start(bf16[128,384]{1,0:T(8,128)(2,1)S(1)} %get-tuple-element.178), channel_id=1, source_target_pairs={{0,8},{8,16},{16,24},{24,32},{32,40},{40,48},{48,56},{56,64},{64,7... | collective-permute-start | bytes 294920 | tf_op jit(solution)/shard_map/ppermute | solution.py:411
  129.2 9.6 %collective-permute-start.21 = (bf16[128,384]{1,0:T(8,128)(2,1)S(1)}, bf16[128,384]{1,0:T(8,128)(2,1)S(1)}, u32[]{:S(2)}, u32[]{:S(2)}) collective-permute-start(bf16[128,384]{1,0:T(8,128)(2,1)S(1)} %get-tuple-element.179), channel_id=1, source_target_pairs={{0,504},{8,0},{16,8},{24,16},{32,24},{40,32},{48,40},{56,48},{64,5... | collective-permute-start | bytes 294920 | tf_op jit(solution)/shard_map/ppermute | solution.py:412
  136.1 3.4 %collective-permute-start.22 = (bf16[128,384]{1,0:T(8,128)(2,1)S(1)}, bf16[128,384]{1,0:T(8,128)(2,1)S(1)}, u32[]{:S(2)}, u32[]{:S(2)}) collective-permute-start(bf16[128,384]{1,0:T(8,128)(2,1)S(1)} %get-tuple-element.180), channel_id=1, source_target_pairs={{0,1},{1,2},{2,3},{3,4},{4,5},{5,6},{6,7},{7,0},{8,9},{9,10},{10,1... | collective-permute-start | bytes 294920 | tf_op jit(solution)/shard_map/ppermute | solution.py:413
  137.9 4.3 %collective-permute-start.23 = (bf16[128,384]{1,0:T(8,128)(2,1)S(1)}, bf16[128,384]{1,0:T(8,128)(2,1)S(1)}, u32[]{:S(2)}, u32[]{:S(2)}) collective-permute-start(bf16[128,384]{1,0:T(8,128)(2,1)S(1)} %get-tuple-element.181), channel_id=1, source_target_pairs={{0,7},{1,0},{2,1},{3,2},{4,3},{5,4},{6,5},{7,6},{8,15},{9,8},{10,9... | collective-permute-start | bytes 294920 | tf_op jit(solution)/shard_map/ppermute | solution.py:414
  156.5 8.7 %collective-permute-start.24 = (bf16[128,384]{1,0:T(8,128)(2,1)S(1)}, bf16[128,384]{1,0:T(8,128)(2,1)S(1)}, u32[]{:S(2)}, u32[]{:S(2)}) collective-permute-start(bf16[128,384]{1,0:T(8,128)(2,1)S(1)} %get-tuple-element.190), channel_id=1, source_target_pairs={{0,8},{8,16},{16,24},{24,32},{32,40},{40,48},{48,56},{56,64},{64,7... | collective-permute-start | bytes 294920 | tf_op jit(solution)/shard_map/ppermute | solution.py:411
  158.5 6.8 %collective-permute-start.25 = (bf16[128,384]{1,0:T(8,128)(2,1)S(1)}, bf16[128,384]{1,0:T(8,128)(2,1)S(1)}, u32[]{:S(2)}, u32[]{:S(2)}) collective-permute-start(bf16[128,384]{1,0:T(8,128)(2,1)S(1)} %get-tuple-element.192), channel_id=1, source_target_pairs={{0,1},{1,2},{2,3},{3,4},{4,5},{5,6},{6,7},{7,0},{8,9},{9,10},{10,1... | collective-permute-start | bytes 294920 | tf_op jit(solution)/shard_map/ppermute | solution.py:413
  159.7 37.9 %copy-start.2 = (s32[1,1,4,384]{3,2,1,0:T(4,128)S(1)}, s32[1,1,4,384]{3,2,1,0:T(4,128)}, u32[]{:S(2)}) copy-start(s32[1,1,4,384]{3,2,1,0:T(4,128)} %param.13) | copy-start | bytes 18436
  159.7 38.0 %copy-start.5 = (s32[1,1,4]{2,1,0:T(1,128)S(1)}, s32[1,1,4]{2,1,0:T(1,128)}, u32[]{:S(2)}) copy-start(s32[1,1,4]{2,1,0:T(1,128)} %param.14) | copy-start | bytes 52
  180.0 15.9 %all-to-all-start.6 = ((f32[16,16,128]{2,1,0:T(8,128)}), f32[16,16,128]{2,1,0:T(8,128)S(1)}, u32[]{:S(2)}, u32[]{:S(2)}) async-start(f32[16,16,128]{2,1,0:T(8,128)} %shard_map.92), calls=%async_computation.6 | async-start | bytes 262144 | tf_op jit(solution)/shard_map/all_to_all | solution.py:357
  197.9 0.7 copy-start.6

commit v2 on v1

--- a/solution.py
+++ b/solution.py
@@ -138,23 +138,22 @@
 
 
 def setup_kernel(
-    schur, loads, rows, corners, slots, coarse, pick_ref, corner_ref, inv_ref, send_ref
+    counts, loads, rows, corners, slots, coarse, pick_ref, corner_ref, send_ref
 ):
-    unknowns = schur.shape[0]
+    unknowns = loads.shape[1]
     lanes = corners.shape[1]
     tile = 128
-    eye = lax.broadcasted_iota(jnp.int32, (tile, tile), 0) == lax.broadcasted_iota(
-        jnp.int32, (tile, tile), 1
-    )
-    for start in range(0, unknowns, tile):
-        block = schur[start : start + tile, start : start + tile].astype(F32)
-        diag = jnp.sum(jnp.where(eye, block, 0.0), axis=0, keepdims=True)
-        inv_ref[:, start : start + tile] = 1.0 / diag
+
+    sides, width = rows.shape
+    lane = lax.broadcasted_iota(jnp.int32, (1, width), 1)
+    live = [jnp.where(lane < counts[side], rows[side : side + 1, :], -1) for side in range(sides)]
 
     def build(step, _):
         start = pl.multiple_of(step * tile, tile)
-        index = lax.broadcasted_iota(jnp.int32, (tile, unknowns), 0) + start
-        pick_ref[pl.ds(start, tile), :] = (index == rows[...]).astype(F32).astype(BF16)
+        index = lax.broadcasted_iota(jnp.int32, (tile, width), 0) + start
+        for side in range(sides):
+            cols = slice(side * width, (side + 1) * width)
+            pick_ref[pl.ds(start, tile), cols] = (index == live[side]).astype(F32).astype(BF16)
         index = lax.broadcasted_iota(jnp.int32, (tile, lanes), 0) + start
         corner_ref[pl.ds(start, tile), :] = (index == corners[...]).astype(F32).astype(BF16)
         return 0
@@ -174,7 +173,15 @@
         )
 
 
-def lift_kernel(slots, got, lift_ref, *, cases, own):
+def lift_kernel(schur, slots, got, lift_ref, inv_ref, *, cases, own):
+    tile = 128
+    eye = lax.broadcasted_iota(jnp.int32, (tile, tile), 0) == lax.broadcasted_iota(
+        jnp.int32, (tile, tile), 1
+    )
+    for start in range(0, schur.shape[0], tile):
+        block = schur[start : start + tile, start : start + tile].astype(F32)
+        diag = jnp.sum(jnp.where(eye, block, 0.0), axis=0, keepdims=True)
+        inv_ref[:, start : start + tile] = 1.0 / diag
     peers, _, lanes = got.shape
     total = own * peers
     parts = total // lanes
@@ -348,9 +355,10 @@
         out_ref[:, cols] = value.astype(BF16)
 
 
-def ring(axis, shift):
+def shifted(value, axis, shift, wrap):
     count = lax.axis_size(axis)
-    return [(i, (i + shift) % count) for i in range(count)]
+    pairs = [(i, (i + shift) % count) for i in range(count) if wrap or 0 <= i + shift < count]
+    return lax.ppermute(value, axis, pairs)
 
 
 def exchange(send, axis, groups=None):
@@ -379,24 +387,24 @@
     width = rows.shape[1]
     lanes = corner_rows.shape[2]
     own, total = block.shape
-    live = jnp.arange(width, dtype=jnp.int32)[None, :] < counts[:, None]
-    live_rows = jnp.where(live, rows, -1).reshape(1, unknowns)
     slots = corner_map[0]
 
-    pick, corner, inv, send = call(
+    pick, corner, send = pl.pallas_call(
         setup_kernel,
-        (
+        in_specs=[pl.BlockSpec(memory_space=pltpu.SMEM)]
+        + [pl.BlockSpec(memory_space=pltpu.VMEM)] * 5,
+        out_shape=(
             shape((unknowns, unknowns), BF16),
             shape((unknowns, lanes), BF16),
-            shape((1, unknowns), F32),
             shape((chord, cases + own * (total // lanes) + 8, lanes), F32),
         ),
-    )(matrix, rhs, live_rows, corner_rows[0], slots, block)
+        compiler_params=pltpu.CompilerParams(vmem_limit_bytes=28 * 2**20),
+    )(counts, rhs, rows, corner_rows[0], slots, block)
     got = exchange(send, "chord")
-    lift = call(
+    lift, inv = call(
         functools.partial(lift_kernel, cases=cases, own=own),
-        shape((chord * lanes, 2 * lanes), BF16),
-    )(slots, got)
+        (shape((chord * lanes, 2 * lanes), BF16), shape((1, unknowns), F32)),
+    )(matrix, slots, got)
 
     resid = rhs
     fields, images = [], []
@@ -408,10 +416,10 @@
         )(got, lift, corner, pick, resid, inv)
         last = step == ITERS - 1
         came = [
-            lax.ppermute(sends[1], "span", ring("span", 1)),
-            None if last else lax.ppermute(sends[0], "span", ring("span", -1)),
-            lax.ppermute(sends[3], "chord", ring("chord", 1)),
-            None if last else lax.ppermute(sends[2], "chord", ring("chord", -1)),
+            shifted(sends[1], "span", 1, False),
+            None if last else shifted(sends[0], "span", -1, False),
+            shifted(sends[3], "chord", 1, True),
+            None if last else shifted(sends[2], "chord", -1, True),
         ]
         out = (shape((cases, 128), F32),)
         if not last:

time: 207 us -> 202 us (0.976)
  blocking collectives: 81.7 us -> 96.6 us
  starting transfers between devices: 51.1 us -> 36.9 us
  waiting for transfers between devices: 30.7 us -> 26.7 us
    ppermute x18, starting transfers between devices: 47.6 us -> 31.8 us  [shifted(): return lax.ppermute(value, axis, pairs)]
    all_to_all x6, blocking collectives: 81.7 us -> 96.6 us  [exchange(): return lax.all_to_all(send, axis, 0, 0, axis_index_groups=groups)]
    ppermute x18, waiting for transfers between devices: 18.4 us -> 14.5 us  [shifted(): return lax.ppermute(value, axis, pairs)]
where the time goes in v2:
time: 202 us; the launch traced here: 201 us
  blocking collectives  96.6 us (48%)
  starting transfers between devices  36.9 us (18%)
  waiting for transfers between devices  26.7 us (13%)
  Pallas kernels  25.4 us (13%)
  between operations  14.3 us (7%)
    all_to_all x6, blocking collectives, exchange(): return lax.all_to_all(send, axis, 0, 0, axis_index_groups=groups)  96.6 us
    ppermute x18, starting transfers between devices, shifted(): return lax.ppermute(value, axis, pairs)  31.8 us
    ppermute x18, waiting for transfers between devices, shifted(): return lax.ppermute(value, axis, pairs)  14.5 us
    all_to_all x1, waiting for transfers between devices, exchange(): return lax.all_to_all(send, axis, 0, 0, axis_index_groups=groups)  12.2 us
    pallas_call x4, Pallas kernels, shards(): call(image_kernel, (shape((cases, unknowns), F32), shape((chord, cases, l...  7.13 us
    pallas_call x5, Pallas kernels, shards(): call(precondition_kernel, (shape((2 * cases, unknowns), BF16),) + (shape(...  6.28 us
    all_to_all x1, starting transfers between devices, exchange(): return lax.all_to_all(send, axis, 0, 0, axis_index_groups=groups)  5.09 us
    pallas_call x5, Pallas kernels, shards(): call(functools.partial(local_kernel, step=step), out)  4.43 us
  transfers between devices with their start and end apart: 19, of which 10 were waited for; matrix products, arithmetic and copies ran while one was open for 0% of the time, Pallas kernels for 2%

profile of v2, /device:TPU:1, one launch (start us, length us, event | category | flops | bytes accessed | tf_op | source)
XLA Modules:
  0.0 200.8 jit_solution(14136193839828428216)
XLA Ops:
  6.5 2.3 %shard_map.75 = (bf16[1536,1536]{1,0:T(8,128)(2,1)S(1)}, bf16[1536,128]{1,0:T(8,128)(2,1)S(1)}, f32[8,216,128]{2,1,0:T(8,128)S(1)}) custom-call(s32[4]{0:T(128)} %bitcast.179, bf16[64,1536]{1,0:T(8,128)(2,1)} %bitcast.160, s32[4,384]{1,0:T(4,128)} %bitcast.172, s32[1,128]{1,0:T(1,128)} %bitcast.31.corners, s32[1,128]{1,0:T(1,128)} %bitcast.32.slots, ...), custom_call_target="tpu_custom_call" | custom-call | tf_op jit(solution)/shard_map/pallas_call | solution.py:392
  8.8 23.0 %all_to_all.35.got = f32[8,216,128]{2,1,0:T(8,128)S(1)} all-to-all(f32[8,216,128]{2,1,0:T(8,128)S(1)} %get-tuple-element.149), channel_id=1, replica_groups=mesh['span'=64,'chord'=8] {'chord'}, dimensions={0} | all-to-all | bytes 1769472 | tf_op jit(solution)/shard_map/all_to_all | solution.py:365
  31.8 3.3 %shard_map.76 = (bf16[1024,256]{1,0:T(8,128)(2,1)S(1)}, f32[1,1536]{1,0:T(1,128)S(1)}) custom-call(bf16[1536,1536]{1,0:T(8,128)(2,1)} %bitcast.149, s32[1,128]{1,0:T(1,128)} %bitcast.32.slots, f32[8,216,128]{2,1,0:T(8,128)S(1)} %all_to_all.35.got), custom_call_target="tpu_custom_call" | custom-call | flops 100000000 | bytes 1000000 | tf_op jit(solution)/shard_map/pallas_call | solution.py:404
  35.1 1.3 shard_map.77
  36.4 1.3 collective-permute-start.8
  37.7 1.3 collective-permute-start.9
  39.0 1.0 collective-permute-start.10
  40.0 0.8 shard_map.78
  40.8 2.2 %collective-permute-done.9.from1 = bf16[128,384]{1,0:T(8,128)(2,1)S(1)} collective-permute-done((bf16[128,384]{1,0:T(8,128)(2,1)S(1)}, bf16[128,384]{1,0:T(8,128)(2,1)S(1)}, u32[]{:S(2)}, u32[]{:S(2)}) %collective-permute-start.9) | collective-permute-done | bytes 98336 | tf_op jit(solution)/shard_map/ppermute | solution.py:361
  43.1 1.3 collective-permute-done.11.from3
  44.4 1.8 shard_map.79
  46.1 11.3 %all_to_all.36.got = f32[8,64,128]{2,1,0:T(8,128)S(1)} all-to-all(f32[8,64,128]{2,1,0:T(8,128)S(1)} %get-tuple-element.160), channel_id=1, replica_groups=mesh['span'=64,'chord'=8] {'chord'}, dimensions={0} | all-to-all | bytes 524288 | tf_op jit(solution)/shard_map/all_to_all | solution.py:365
  57.4 1.3 shard_map.80
  58.7 4.3 %collective-permute-start.12 = (bf16[128,384]{1,0:T(8,128)(2,1)S(1)}, bf16[128,384]{1,0:T(8,128)(2,1)S(1)}, u32[]{:S(2)}, u32[]{:S(2)}) collective-permute-start(bf16[128,384]{1,0:T(8,128)(2,1)S(1)} %get-tuple-element.162), channel_id=1, source_target_pairs={{0,8},{8,16},{16,24},{24,32},{32,40},{40,48},{48,56},{56,64},{64,7... | collective-permute-start | bytes 294920 | tf_op jit(solution)/shard_map/ppermute | solution.py:361
  63.0 1.3 collective-permute-start.13
  64.3 1.5 collective-permute-start.14
  65.8 0.9 shard_map.81
  66.6 1.7 collective-permute-done.13.from1
  68.3 1.8 collective-permute-done.15.from3
  70.1 1.8 shard_map.82
  71.9 11.3 %all_to_all.37.got = f32[8,64,128]{2,1,0:T(8,128)S(1)} all-to-all(f32[8,64,128]{2,1,0:T(8,128)S(1)} %get-tuple-element.169), channel_id=1, replica_groups=mesh['span'=64,'chord'=8] {'chord'}, dimensions={0} | all-to-all | bytes 524288 | tf_op jit(solution)/shard_map/all_to_all | solution.py:365
  83.2 1.3 shard_map.83
  84.4 4.3 %collective-permute-start.16 = (bf16[128,384]{1,0:T(8,128)(2,1)S(1)}, bf16[128,384]{1,0:T(8,128)(2,1)S(1)}, u32[]{:S(2)}, u32[]{:S(2)}) collective-permute-start(bf16[128,384]{1,0:T(8,128)(2,1)S(1)} %get-tuple-element.171), channel_id=1, source_target_pairs={{0,8},{8,16},{16,24},{24,32},{32,40},{40,48},{48,56},{56,64},{64,7... | collective-permute-start | bytes 294920 | tf_op jit(solution)/shard_map/ppermute | solution.py:361
  88.7 1.3 collective-permute-start.17
  90.0 1.5 collective-permute-start.18
  91.5 0.9 shard_map.84
  92.4 1.7 collective-permute-done.17.from1
  94.1 1.7 collective-permute-done.19.from3
  95.9 1.8 shard_map.85
  97.7 11.3 %all_to_all.38.got = f32[8,64,128]{2,1,0:T(8,128)S(1)} all-to-all(f32[8,64,128]{2,1,0:T(8,128)S(1)} %get-tuple-element.178), channel_id=1, replica_groups=mesh['span'=64,'chord'=8] {'chord'}, dimensions={0} | all-to-all | bytes 524288 | tf_op jit(solution)/shard_map/all_to_all | solution.py:365
  108.9 1.3 shard_map.86
  110.2 4.3 %collective-permute-start.20 = (bf16[128,384]{1,0:T(8,128)(2,1)S(1)}, bf16[128,384]{1,0:T(8,128)(2,1)S(1)}, u32[]{:S(2)}, u32[]{:S(2)}) collective-permute-start(bf16[128,384]{1,0:T(8,128)(2,1)S(1)} %get-tuple-element.180), channel_id=1, source_target_pairs={{0,8},{8,16},{16,24},{24,32},{32,40},{40,48},{48,56},{56,64},{64,7... | collective-permute-start | bytes 294920 | tf_op jit(solution)/shard_map/ppermute | solution.py:361
  114.5 1.5 collective-permute-start.21
  116.0 1.5 collective-permute-start.22
  117.5 0.9 shard_map.87
  118.4 3.1 %collective-permute-done.21.from1 = bf16[128,384]{1,0:T(8,128)(2,1)S(1)} collective-permute-done((bf16[128,384]{1,0:T(8,128)(2,1)S(1)}, bf16[128,384]{1,0:T(8,128)(2,1)S(1)}, u32[]{:S(2)}, u32[]{:S(2)}) %collective-permute-start.21) | collective-permute-done | bytes 98336 | tf_op jit(solution)/shard_map/ppermute | solution.py:361
  121.8 1.8 shard_map.88
  123.6 11.3 %all_to_all.39.got = f32[8,64,128]{2,1,0:T(8,128)S(1)} all-to-all(f32[8,64,128]{2,1,0:T(8,128)S(1)} %get-tuple-element.187), channel_id=1, replica_groups=mesh['span'=64,'chord'=8] {'chord'}, dimensions={0} | all-to-all | bytes 524288 | tf_op jit(solution)/shard_map/all_to_all | solution.py:365
  134.9 1.3 shard_map.89
  136.1 5.3 %collective-permute-start.24 = (bf16[128,384]{1,0:T(8,128)(2,1)S(1)}, bf16[128,384]{1,0:T(8,128)(2,1)S(1)}, u32[]{:S(2)}, u32[]{:S(2)}) collective-permute-start(bf16[128,384]{1,0:T(8,128)(2,1)S(1)} %get-tuple-element.192), channel_id=1, source_target_pairs={{0,8},{8,16},{16,24},{24,32},{32,40},{40,48},{48,56},{56,64},{64,7... | collective-permute-start | bytes 294920 | tf_op jit(solution)/shard_map/ppermute | solution.py:361
  141.5 1.5 collective-permute-start.25
  143.0 1.0 shard_map.90.acc
  144.9 28.5 %all_to_all.40.got = f32[32,16,128]{2,1,0:T(8,128)S(1)} all-to-all(f32[32,16,128]{2,1,0:T(8,128)S(1)} %shard_map.91), channel_id=1, replica_groups={{0,1,2,3,4,5,6,7,128,129,130,131,132,133,134,135,256,257,258,259,260,26..., dimensions={0} | all-to-all | bytes 524288 | tf_op jit(solution)/shard_map/all_to_all | solution.py:365
  173.4 0.7 shard_map.92
  174.1 5.1 %all-to-all-start.6 = ((f32[16,16,128]{2,1,0:T(8,128)}), f32[16,16,128]{2,1,0:T(8,128)S(1)}, u32[]{:S(2)}, u32[]{:S(2)}) async-start(f32[16,16,128]{2,1,0:T(8,128)} %shard_map.92), calls=%async_computation.6 | async-start | bytes 262144 | tf_op jit(solution)/shard_map/all_to_all | solution.py:365
  179.2 12.2 %all-to-all-done.6.got = f32[16,16,128]{2,1,0:T(8,128)S(1)} async-done(((f32[16,16,128]{2,1,0:T(8,128)}), f32[16,16,128]{2,1,0:T(8,128)S(1)}, u32[]{:S(2)}, u32[]{:S(2)}) %all-to-all-start.6) | async-done | bytes 131104 | tf_op jit(solution)/shard_map/all_to_all | solution.py:365
  191.3 1.0 shard_map.93
  193.3 0.7 copy-done.6
  (30 shorter events, 1.6 us)
Async XLA Ops:
  6.5 28.6 %copy-start.1 = (bf16[1,1,64,1536]{3,2,1,0:T(8,128)(2,1)S(1)}, bf16[1,1,64,1536]{3,2,1,0:T(8,128)(2,1)}, u32[]{:S(2)}) copy-start(bf16[1,1,64,1536]{3,2,1,0:T(8,128)(2,1)} %param.12) | copy-start | bytes 589828
  8.8 31.2 %slice-start = ((s8[4718592]{0:T(1024)(128)(4,1)}), s8[4194304]{0:T(1024)(128)(4,1)S(1)}, s32[]{:S(2)}) async-start(s8[4718592]{0:T(1024)(128)(4,1)} %bitcast.150), calls=%async_computation.9 | async-start | bytes 8388608
  31.8 8.2 %slice-start.1 = ((s8[4718592]{0:T(1024)(128)(4,1)}), s8[524288]{0:T(1024)(128)(4,1)S(1)}, s32[]{:S(2)}) async-start(s8[4718592]{0:T(1024)(128)(4,1)} %bitcast.150), calls=%async_computation.10 | async-start | bytes 1048576
  36.4 4.5 %collective-permute-start.8 = (bf16[128,384]{1,0:T(8,128)(2,1)S(1)}, bf16[128,384]{1,0:T(8,128)(2,1)S(1)}, u32[]{:S(2)}, u32[]{:S(2)}) collective-permute-start(bf16[128,384]{1,0:T(8,128)(2,1)S(1)} %get-tuple-element.154), channel_id=1, source_target_pairs={{0,8},{8,16},{16,24},{24,32},{32,40},{40,48},{48,56},{56,64},{64,7... | collective-permute-start | bytes 294920 | tf_op jit(solution)/shard_map/ppermute | solution.py:361
  37.7 5.4 %collective-permute-start.9 = (bf16[128,384]{1,0:T(8,128)(2,1)S(1)}, bf16[128,384]{1,0:T(8,128)(2,1)S(1)}, u32[]{:S(2)}, u32[]{:S(2)}) collective-permute-start(bf16[128,384]{1,0:T(8,128)(2,1)S(1)} %get-tuple-element.155), channel_id=1, source_target_pairs={{8,0},{16,8},{24,16},{32,24},{40,32},{48,40},{56,48},{64,56},{72,6... | collective-permute-start | bytes 294920 | tf_op jit(solution)/shard_map/ppermute | solution.py:361
  39.0 4.1 %collective-permute-start.10 = (bf16[128,384]{1,0:T(8,128)(2,1)S(1)}, bf16[128,384]{1,0:T(8,128)(2,1)S(1)}, u32[]{:S(2)}, u32[]{:S(2)}) collective-permute-start(bf16[128,384]{1,0:T(8,128)(2,1)S(1)} %get-tuple-element.156), channel_id=1, source_target_pairs={{0,1},{1,2},{2,3},{3,4},{4,5},{5,6},{6,7},{7,0},{8,9},{9,10},{10,1... | collective-permute-start | bytes 294920 | tf_op jit(solution)/shard_map/ppermute | solution.py:361
  40.0 4.3 %collective-permute-start.11 = (bf16[128,384]{1,0:T(8,128)(2,1)S(1)}, bf16[128,384]{1,0:T(8,128)(2,1)S(1)}, u32[]{:S(2)}, u32[]{:S(2)}) collective-permute-start(bf16[128,384]{1,0:T(8,128)(2,1)S(1)} %get-tuple-element.157), channel_id=1, source_target_pairs={{0,7},{1,0},{2,1},{3,2},{4,3},{5,4},{6,5},{7,6},{8,15},{9,8},{10,9... | collective-permute-start | bytes 294920 | tf_op jit(solution)/shard_map/ppermute | solution.py:361
  58.7 8.0 %collective-permute-start.12 = (bf16[128,384]{1,0:T(8,128)(2,1)S(1)}, bf16[128,384]{1,0:T(8,128)(2,1)S(1)}, u32[]{:S(2)}, u32[]{:S(2)}) collective-permute-start(bf16[128,384]{1,0:T(8,128)(2,1)S(1)} %get-tuple-element.162), channel_id=1, source_target_pairs={{0,8},{8,16},{16,24},{24,32},{32,40},{40,48},{48,56},{56,64},{64,7... | collective-permute-start | bytes 294920 | tf_op jit(solution)/shard_map/ppermute | solution.py:361
  63.0 5.4 %collective-permute-start.13 = (bf16[128,384]{1,0:T(8,128)(2,1)S(1)}, bf16[128,384]{1,0:T(8,128)(2,1)S(1)}, u32[]{:S(2)}, u32[]{:S(2)}) collective-permute-start(bf16[128,384]{1,0:T(8,128)(2,1)S(1)} %get-tuple-element.163), channel_id=1, source_target_pairs={{8,0},{16,8},{24,16},{32,24},{40,32},{48,40},{56,48},{64,56},{72,6... | collective-permute-start | bytes 294920 | tf_op jit(solution)/shard_map/ppermute | solution.py:361
  64.3 4.1 %collective-permute-start.14 = (bf16[128,384]{1,0:T(8,128)(2,1)S(1)}, bf16[128,384]{1,0:T(8,128)(2,1)S(1)}, u32[]{:S(2)}, u32[]{:S(2)}) collective-permute-start(bf16[128,384]{1,0:T(8,128)(2,1)S(1)} %get-tuple-element.164), channel_id=1, source_target_pairs={{0,1},{1,2},{2,3},{3,4},{4,5},{5,6},{6,7},{7,0},{8,9},{9,10},{10,1... | collective-permute-start | bytes 294920 | tf_op jit(solution)/shard_map/ppermute | solution.py:361
  65.8 4.3 %collective-permute-start.15 = (bf16[128,384]{1,0:T(8,128)(2,1)S(1)}, bf16[128,384]{1,0:T(8,128)(2,1)S(1)}, u32[]{:S(2)}, u32[]{:S(2)}) collective-permute-start(bf16[128,384]{1,0:T(8,128)(2,1)S(1)} %get-tuple-element.165), channel_id=1, source_target_pairs={{0,7},{1,0},{2,1},{3,2},{4,3},{5,4},{6,5},{7,6},{8,15},{9,8},{10,9... | collective-permute-start | bytes 294920 | tf_op jit(solution)/shard_map/ppermute | solution.py:361
  84.4 8.0 %collective-permute-start.16 = (bf16[128,384]{1,0:T(8,128)(2,1)S(1)}, bf16[128,384]{1,0:T(8,128)(2,1)S(1)}, u32[]{:S(2)}, u32[]{:S(2)}) collective-permute-start(bf16[128,384]{1,0:T(8,128)(2,1)S(1)} %get-tuple-element.171), channel_id=1, source_target_pairs={{0,8},{8,16},{16,24},{24,32},{32,40},{40,48},{48,56},{56,64},{64,7... | collective-permute-start | bytes 294920 | tf_op jit(solution)/shard_map/ppermute | solution.py:361
  88.7 5.4 %collective-permute-start.17 = (bf16[128,384]{1,0:T(8,128)(2,1)S(1)}, bf16[128,384]{1,0:T(8,128)(2,1)S(1)}, u32[]{:S(2)}, u32[]{:S(2)}) collective-permute-start(bf16[128,384]{1,0:T(8,128)(2,1)S(1)} %get-tuple-element.172), channel_id=1, source_target_pairs={{8,0},{16,8},{24,16},{32,24},{40,32},{48,40},{56,48},{64,56},{72,6... | collective-permute-start | bytes 294920 | tf_op jit(solution)/shard_map/ppermute | solution.py:361
  90.0 4.1 %collective-permute-start.18 = (bf16[128,384]{1,0:T(8,128)(2,1)S(1)}, bf16[128,384]{1,0:T(8,128)(2,1)S(1)}, u32[]{:S(2)}, u32[]{:S(2)}) collective-permute-start(bf16[128,384]{1,0:T(8,128)(2,1)S(1)} %get-tuple-element.173), channel_id=1, source_target_pairs={{0,1},{1,2},{2,3},{3,4},{4,5},{5,6},{6,7},{7,0},{8,9},{9,10},{10,1... | collective-permute-start | bytes 294920 | tf_op jit(solution)/shard_map/ppermute | solution.py:361
  91.5 4.3 %collective-permute-start.19 = (bf16[128,384]{1,0:T(8,128)(2,1)S(1)}, bf16[128,384]{1,0:T(8,128)(2,1)S(1)}, u32[]{:S(2)}, u32[]{:S(2)}) collective-permute-start(bf16[128,384]{1,0:T(8,128)(2,1)S(1)} %get-tuple-element.174), channel_id=1, source_target_pairs={{0,7},{1,0},{2,1},{3,2},{4,3},{5,4},{6,5},{7,6},{8,15},{9,8},{10,9... | collective-permute-start | bytes 294920 | tf_op jit(solution)/shard_map/ppermute | solution.py:361
  110.2 8.2 %collective-permute-start.20 = (bf16[128,384]{1,0:T(8,128)(2,1)S(1)}, bf16[128,384]{1,0:T(8,128)(2,1)S(1)}, u32[]{:S(2)}, u32[]{:S(2)}) collective-permute-start(bf16[128,384]{1,0:T(8,128)(2,1)S(1)} %get-tuple-element.180), channel_id=1, source_target_pairs={{0,8},{8,16},{16,24},{24,32},{32,40},{40,48},{48,56},{56,64},{64,7... | collective-permute-start | bytes 294920 | tf_op jit(solution)/shard_map/ppermute | solution.py:361
  114.5 7.0 %collective-permute-start.21 = (bf16[128,384]{1,0:T(8,128)(2,1)S(1)}, bf16[128,384]{1,0:T(8,128)(2,1)S(1)}, u32[]{:S(2)}, u32[]{:S(2)}) collective-permute-start(bf16[128,384]{1,0:T(8,128)(2,1)S(1)} %get-tuple-element.181), channel_id=1, source_target_pairs={{8,0},{16,8},{24,16},{32,24},{40,32},{48,40},{56,48},{64,56},{72,6... | collective-permute-start | bytes 294920 | tf_op jit(solution)/shard_map/ppermute | solution.py:361
  116.0 5.5 %collective-permute-start.22 = (bf16[128,384]{1,0:T(8,128)(2,1)S(1)}, bf16[128,384]{1,0:T(8,128)(2,1)S(1)}, u32[]{:S(2)}, u32[]{:S(2)}) collective-permute-start(bf16[128,384]{1,0:T(8,128)(2,1)S(1)} %get-tuple-element.182), channel_id=1, source_target_pairs={{0,1},{1,2},{2,3},{3,4},{4,5},{5,6},{6,7},{7,0},{8,9},{9,10},{10,1... | collective-permute-start | bytes 294920 | tf_op jit(solution)/shard_map/ppermute | solution.py:361
  117.5 4.3 %collective-permute-start.23 = (bf16[128,384]{1,0:T(8,128)(2,1)S(1)}, bf16[128,384]{1,0:T(8,128)(2,1)S(1)}, u32[]{:S(2)}, u32[]{:S(2)}) collective-permute-start(bf16[128,384]{1,0:T(8,128)(2,1)S(1)} %get-tuple-element.183), channel_id=1, source_target_pairs={{0,7},{1,0},{2,1},{3,2},{4,3},{5,4},{6,5},{7,6},{8,15},{9,8},{10,9... | collective-permute-start | bytes 294920 | tf_op jit(solution)/shard_map/ppermute | solution.py:361
  136.1 7.8 %collective-permute-start.24 = (bf16[128,384]{1,0:T(8,128)(2,1)S(1)}, bf16[128,384]{1,0:T(8,128)(2,1)S(1)}, u32[]{:S(2)}, u32[]{:S(2)}) collective-permute-start(bf16[128,384]{1,0:T(8,128)(2,1)S(1)} %get-tuple-element.192), channel_id=1, source_target_pairs={{0,8},{8,16},{16,24},{24,32},{32,40},{40,48},{48,56},{56,64},{64,7... | collective-permute-start | bytes 294920 | tf_op jit(solution)/shard_map/ppermute | solution.py:361
  141.5 3.1 %collective-permute-start.25 = (bf16[128,384]{1,0:T(8,128)(2,1)S(1)}, bf16[128,384]{1,0:T(8,128)(2,1)S(1)}, u32[]{:S(2)}, u32[]{:S(2)}) collective-permute-start(bf16[128,384]{1,0:T(8,128)(2,1)S(1)} %get-tuple-element.194), channel_id=1, source_target_pairs={{0,1},{1,2},{2,3},{3,4},{4,5},{5,6},{6,7},{7,0},{8,9},{9,10},{10,1... | collective-permute-start | bytes 294920 | tf_op jit(solution)/shard_map/ppermute | solution.py:361
  143.0 50.1 %copy-start.2 = (s32[1,1,4,384]{3,2,1,0:T(4,128)S(1)}, s32[1,1,4,384]{3,2,1,0:T(4,128)}, u32[]{:S(2)}) copy-start(s32[1,1,4,384]{3,2,1,0:T(4,128)} %param.13) | copy-start | bytes 18436
  143.0 50.1 %copy-start.5 = (s32[1,1,4]{2,1,0:T(1,128)S(1)}, s32[1,1,4]{2,1,0:T(1,128)}, u32[]{:S(2)}) copy-start(s32[1,1,4]{2,1,0:T(1,128)} %param.14) | copy-start | bytes 52
  174.1 17.3 %all-to-all-start.6 = ((f32[16,16,128]{2,1,0:T(8,128)}), f32[16,16,128]{2,1,0:T(8,128)S(1)}, u32[]{:S(2)}, u32[]{:S(2)}) async-start(f32[16,16,128]{2,1,0:T(8,128)} %shard_map.92), calls=%async_computation.6 | async-start | bytes 262144 | tf_op jit(solution)/shard_map/all_to_all | solution.py:365
  193.3 0.7 copy-start.6

commit v3 on v2

--- a/solution.py
+++ b/solution.py
@@ -118,11 +118,6 @@
     return value[:half] + value[half:]
 
 
-def whole(ref, cols=slice(None)):
-    half = ref.shape[0] // 2
-    return ref[:half, cols].astype(F32) + ref[half:, cols].astype(F32)
-
-
 def call(body, outs, scratch=(), limit=28, flops=10**8):
     return pl.pallas_call(
         body,
@@ -138,11 +133,18 @@
 
 
 def setup_kernel(
-    counts, loads, rows, corners, slots, coarse, pick_ref, corner_ref, send_ref
+    counts, schur, loads, rows, corners, slots, coarse,
+    pick_ref, corner_ref, inv_ref, send_ref, blocks, sems,
 ):
     unknowns = loads.shape[1]
     lanes = corners.shape[1]
-    tile = 128
+    tile = blocks.shape[1]
+    copies = []
+    for part in range(unknowns // tile):
+        span = pl.ds(part * tile, tile)
+        copy = pltpu.make_async_copy(schur.at[span, span], blocks.at[part], sems.at[part])
+        copy.start()
+        copies.append(copy)
 
     sides, width = rows.shape
     lane = lax.broadcasted_iota(jnp.int32, (1, width), 1)
@@ -159,6 +161,14 @@
         return 0
 
     lax.fori_loop(0, unknowns // tile, build, 0)
+    eye = lax.broadcasted_iota(jnp.int32, (tile, tile), 0) == lax.broadcasted_iota(
+        jnp.int32, (tile, tile), 1
+    )
+    for part, copy in enumerate(copies):
+        copy.wait()
+        block = blocks[part].astype(F32)
+        diag = jnp.sum(jnp.where(eye, block, 0.0), axis=0, keepdims=True)
+        inv_ref[:, part * tile : (part + 1) * tile] = 1.0 / diag
     picked = mm(loads[...], corner_ref[...])
     cases = picked.shape[0]
     own, total = coarse.shape
@@ -173,15 +183,7 @@
         )
 
 
-def lift_kernel(schur, slots, got, lift_ref, inv_ref, *, cases, own):
-    tile = 128
-    eye = lax.broadcasted_iota(jnp.int32, (tile, tile), 0) == lax.broadcasted_iota(
-        jnp.int32, (tile, tile), 1
-    )
-    for start in range(0, schur.shape[0], tile):
-        block = schur[start : start + tile, start : start + tile].astype(F32)
-        diag = jnp.sum(jnp.where(eye, block, 0.0), axis=0, keepdims=True)
-        inv_ref[:, start : start + tile] = 1.0 / diag
+def lift_kernel(slots, got, lift_ref, *, cases, own):
     peers, _, lanes = got.shape
     total = own * peers
     parts = total // lanes
@@ -208,82 +210,141 @@
         lift_ref[peer * lanes : (peer + 1) * lanes, :] = mm(theirs, cols, TN).astype(BF16)
 
 
-def precondition_kernel(got, lift, corner, pick, resid, inv, field_ref, *send_refs):
+def corner_part(got, lift, cases, lanes):
     peers = got.shape[0]
-    cases = resid.shape[0]
-    lanes = corner.shape[1]
     corners = jnp.concatenate([got[p, :cases, :] for p in range(peers)], axis=1)
     product = mm(stacked(corners), lift[...])
-    back = folded(product[:, :lanes]) + product[:cases, lanes:]
-    back = stacked(back)
-    unknowns = resid.shape[1]
+    return stacked(folded(product[:, :lanes]) + product[:cases, lanes:])
+
+
+def begin_kernel(got, lift, corner, pick, loads, inv, field_ref, *send_refs):
+    cases, unknowns = loads.shape
+    back = corner_part(got, lift, cases, corner.shape[1])
     width = unknowns // 4
     for side in range(4):
         cols = slice(side * width, (side + 1) * width)
         added = folded(mm(back, corner[cols, :], NT))
-        value = resid[:, cols].astype(F32) * inv[:, cols] + added
-        high, low = halves(value)
-        field_ref[:cases, cols] = high
-        field_ref[cases:, cols] = low
+        field_ref[:, cols] = stacked(loads[:, cols].astype(F32) * inv[:, cols] + added)
     for pair in range(2):
         cols = slice(2 * pair * width, 2 * (pair + 1) * width)
-        sent = mm(field_ref[...], pick[:, cols]).astype(BF16)
+        sent = folded(mm(field_ref[...], pick[:, cols]))
         send_refs[2 * pair][...] = sent[:, :width]
         send_refs[2 * pair + 1][...] = sent[:, width:]
 
 
+def lifted_kernel(
+    got, lift, leave, ahead, inv_sent, from0, from1, from2, from3, back_ref, *send_refs
+):
+    cases = ahead.shape[0]
+    back = corner_part(got, lift, cases, leave.shape[0])
+    back_ref[...] = back
+    width = ahead.shape[1] // 4
+    for side, came in enumerate((from0, from1, from2, from3)):
+        cols = slice(side * width, (side + 1) * width)
+        value = ahead[:, cols] - came[...] * inv_sent[:, cols]
+        send_refs[side][...] = value + folded(mm(back, leave[:, cols]))
+
+
 def gram_slot(row, col):
     return col * (col + 1) // 2 + row + 5 if row >= 0 else col
 
 
+def put(total, slot, value):
+    lane = lax.broadcasted_iota(jnp.int32, total.shape, 1)
+    return jnp.where(lane == slot, value, total)
+
+
+def product(first, second):
+    return jnp.sum(first * second, axis=1, keepdims=True)
+
+
+def first_local_kernel(
+    field, matrix, corner, pick, inv, loads,
+    field_ref, acc_ref, local_ref, local_corner_ref, ahead_ref,
+    arrive_ref, leave_ref, corner_matrix_ref, inv_sent_ref,
+):
+    cases, unknowns = loads.shape
+    local = folded(mm(field[...], matrix[...]))
+    local_ref[...] = local
+    local_corner_ref[...] = folded(mm(stacked(local), corner[...]))
+    value = field[:cases, :].astype(F32) + field[cases:, :].astype(F32)
+    field_ref[...] = value
+    total = jnp.zeros(acc_ref.shape, F32)
+    acc_ref[...] = put(total, gram_slot(-1, 0), product(value, loads[...].astype(F32)))
+    scale = jnp.broadcast_to(inv[...], (8, unknowns))
+    high = scale.astype(BF16).astype(F32)
+    middle = (scale - high).astype(BF16).astype(F32)
+    pieces = jnp.concatenate(
+        [high, middle, scale - high - middle, jnp.zeros_like(scale)], axis=0
+    ).astype(BF16)
+    left = jnp.concatenate([stacked(local * inv[...]), pieces], axis=0)
+    wide = unknowns // 4
+    for start in range(0, unknowns, wide):
+        cols = slice(start, start + wide)
+        picked = mm(left, pick[:, cols])
+        ahead_ref[:, cols] = folded(picked[: 2 * cases])
+        parts = picked[2 * cases :]
+        inv_sent_ref[:, cols] = parts[0:1] + parts[8:9] + parts[16:17]
+        arrive_ref[cols, :] = mm(pick[:, cols], corner[...], TN).astype(BF16)
+        leave_ref[:, cols] = mm(corner[...], pick[:, cols], TN).astype(BF16)
+        corner_matrix_ref[:, cols] = mm(corner[...], matrix[:, cols], TN).astype(BF16)
+
+
 def local_kernel(*refs, step):
-    field, matrix, loads, acc = refs[:4]
+    from0, from1, from2, from3, back, before, local_before = refs[:7]
+    matrix, corner, corner_matrix, pick, inv, loads, acc = refs[7:14]
+    images = refs[14 : 13 + step]
+    outs = refs[13 + step : -2]
+    joined, scaled = refs[-2:]
     last = step == ITERS - 1
-    before = refs[4] if step else None
-    images = refs[5 : 5 + step] if step else ()
-    out_acc = refs[-1]
-    cases = loads.shape[0]
-    lane = lax.broadcasted_iota(jnp.int32, (cases, 128), 1)
-    total = acc[...] if step else jnp.zeros((cases, 128), F32)
-
-    def put(total, slot, value):
-        return jnp.where(lane == slot, value, total)
-
-    def product(first, second):
-        return jnp.sum(first * second, axis=1, keepdims=True)
-
-    local = folded(mm(field[...], matrix[...]))
-    value = whole(field)
+    cases, unknowns = loads.shape
+    image_ref, field_ref, acc_ref = outs[:3]
+    width = from0.shape[1]
+    for side, came in enumerate((from0, from1, from2, from3)):
+        joined[:, side * width : (side + 1) * width] = stacked(came[...])
+    chunk = 512
+    for start in range(0, unknowns, chunk):
+        cols = slice(start, start + chunk)
+        image = local_before[:, cols] - folded(mm(joined[...], pick[cols, :], NT))
+        image_ref[:, cols] = image
+        scaled[:, cols] = stacked(image * inv[:, cols])
+    added = folded(mm(back[...], corner[...], NT))
+    value = scaled[:cases, :].astype(F32) + scaled[cases:, :].astype(F32) + added
+    field_ref[...] = value
+    local = folded(mm(scaled[...], matrix[...])) + folded(mm(back[...], corner_matrix[...]))
+    total = put(acc[...], gram_slot(-1, step), product(value, loads[...].astype(F32)))
+    for row in range(step):
+        image = image_ref if row == step - 1 else images[row]
+        total = put(total, gram_slot(row, step), product(value, image[...]))
+    total = put(total, gram_slot(step - 1, step - 1), product(before[...], image_ref[...]))
     if last:
         total = put(total, gram_slot(step, step), product(value, local))
     else:
-        refs[-2][...] = local
-    total = put(total, gram_slot(-1, step), product(value, loads[...].astype(F32)))
-    for row in range(step):
-        total = put(total, gram_slot(row, step), product(value, images[row][...]))
-    if step:
-        total = put(total, gram_slot(step - 1, step - 1), product(whole(before), images[-1][...]))
-    out_acc[...] = total
-
-
-def image_kernel(from0, from1, from2, from3, pick, corner, local, image_ref, send_ref, joined):
+        local_ref, local_corner_ref, ahead_ref = outs[3:]
+        local_ref[...] = local
+        local_corner_ref[...] = folded(mm(stacked(local), corner[...]))
+        scaled[...] = stacked(local * inv[...])
+        half = unknowns // 2
+        for start in (0, half):
+            cols = slice(start, start + half)
+            ahead_ref[:, cols] = folded(mm(scaled[...], pick[:, cols]))
+    acc_ref[...] = total
+
+
+def corner_kernel(from0, from1, from2, from3, arrive, local_corner, send_ref):
     width = from0.shape[1]
+    total = local_corner[...]
     for side, came in enumerate((from0, from1, from2, from3)):
-        joined[:, side * width : (side + 1) * width] = came[...]
-    unknowns = local.shape[1]
-    chunk = 512
-    for start in range(0, unknowns, chunk):
-        cols = slice(start, start + chunk)
-        image_ref[:, cols] = local[:, cols] - folded(mm(joined[...], pick[cols, :], NT))
-    picked = folded(mm(stacked(image_ref[...]), corner[...]))
+        rows = slice(side * width, (side + 1) * width)
+        total = total - folded(mm(stacked(came[...]), arrive[rows, :]))
     for peer in range(send_ref.shape[0]):
-        send_ref[peer] = picked
+        send_ref[peer] = total
 
 
 def gram_kernel(acc, sent0, from0, sent2, from2, send_ref):
     total = acc[...]
     lane = lax.broadcasted_iota(jnp.int32, total.shape, 1)
-    pairs = whole(sent0) * whole(from0) + whole(sent2) * whole(from2)
+    pairs = sent0[...] * from0[...] + sent2[...] * from2[...]
     coupled = 2.0 * jnp.sum(pairs, axis=1, keepdims=True)
     slot = gram_slot(ITERS - 1, ITERS - 1)
     total = jnp.where(lane == slot, total - coupled, total).T
@@ -349,9 +410,9 @@
     width = out_ref.shape[1] // 4
     for part in range(4):
         cols = slice(part * width, (part + 1) * width)
-        value = spread[:, 0:1] * whole(fields[0], cols)
+        value = spread[:, 0:1] * fields[0][:, cols]
         for k in range(1, n):
-            value = value + spread[:, k : k + 1] * whole(fields[k], cols)
+            value = value + spread[:, k : k + 1] * fields[k][:, cols]
         out_ref[:, cols] = value.astype(BF16)
 
 
@@ -389,54 +450,82 @@
     own, total = block.shape
     slots = corner_map[0]
 
-    pick, corner, send = pl.pallas_call(
+    tile = 128
+    pick, corner, inv, send = pl.pallas_call(
         setup_kernel,
-        in_specs=[pl.BlockSpec(memory_space=pltpu.SMEM)]
+        in_specs=[pl.BlockSpec(memory_space=pltpu.SMEM), pl.BlockSpec(memory_space=pl.ANY)]
         + [pl.BlockSpec(memory_space=pltpu.VMEM)] * 5,
         out_shape=(
             shape((unknowns, unknowns), BF16),
             shape((unknowns, lanes), BF16),
+            shape((1, unknowns), F32),
             shape((chord, cases + own * (total // lanes) + 8, lanes), F32),
         ),
+        scratch_shapes=[
+            pltpu.VMEM((unknowns // tile, tile, tile), BF16),
+            pltpu.SemaphoreType.DMA((unknowns // tile,)),
+        ],
         compiler_params=pltpu.CompilerParams(vmem_limit_bytes=28 * 2**20),
-    )(counts, rhs, rows, corner_rows[0], slots, block)
+    )(counts, matrix, rhs, rows, corner_rows[0], slots, block)
     got = exchange(send, "chord")
-    lift, inv = call(
+    lift = call(
         functools.partial(lift_kernel, cases=cases, own=own),
-        (shape((chord * lanes, 2 * lanes), BF16), shape((1, unknowns), F32)),
-    )(matrix, slots, got)
-
-    resid = rhs
+        shape((chord * lanes, 2 * lanes), BF16),
+    )(slots, got)
+
+    full = shape((cases, unknowns), F32)
+    edges = (shape((cases, width), F32),) * 4
+    table = shape((cases, 128), F32)
+    corners = shape((cases, lanes), F32)
+    doubled = shape((2 * cases, unknowns), BF16)
     fields, images = [], []
-    acc = jnp.zeros((cases, 128), F32)
     for step in range(ITERS):
-        field, *sends = call(
-            precondition_kernel,
-            (shape((2 * cases, unknowns), BF16),) + (shape((2 * cases, width), BF16),) * 4,
-        )(got, lift, corner, pick, resid, inv)
         last = step == ITERS - 1
+        if step == 0:
+            first, *sends = call(begin_kernel, (doubled, *edges))(
+                got, lift, corner, pick, rhs, inv
+            )
+        else:
+            back, *sends = call(lifted_kernel, (shape((2 * cases, lanes), BF16), *edges))(
+                got, lift, leave, ahead, inv_sent, *came
+            )
+        earlier = came if step else ()
         came = [
             shifted(sends[1], "span", 1, False),
             None if last else shifted(sends[0], "span", -1, False),
             shifted(sends[3], "chord", 1, True),
             None if last else shifted(sends[2], "chord", -1, True),
         ]
-        out = (shape((cases, 128), F32),)
-        if not last:
-            out = (shape((cases, unknowns), F32),) + out
-        before = (fields[-1],) if step else ()
-        result = call(functools.partial(local_kernel, step=step), out)(
-            field, matrix, rhs, acc, *before, *images
-        )
-        acc = result[-1]
+        if step == 0:
+            field, acc, local, local_corner, ahead, arrive, leave, corner_matrix, inv_sent = call(
+                first_local_kernel,
+                (
+                    full, table, full, corners, full,
+                    shape((unknowns, lanes), BF16),
+                    shape((lanes, unknowns), BF16),
+                    shape((lanes, unknowns), BF16),
+                    shape((1, unknowns), F32),
+                ),
+                flops=10**9,
+            )(first, matrix, corner, pick, inv, rhs)
+        else:
+            image, field, acc, *rest = call(
+                functools.partial(local_kernel, step=step),
+                (full, full, table) + (() if last else (full, corners, full)),
+                scratch=[pltpu.VMEM(doubled.shape, BF16)] * 2,
+                flops=10**9,
+            )(
+                *earlier, back, fields[-1], local,
+                matrix, corner, corner_matrix, pick, inv, rhs, acc, *images,
+            )
+            images.append(image)
+            if not last:
+                local, local_corner, ahead = rest
         fields.append(field)
         if not last:
-            resid, send = call(
-                image_kernel,
-                (shape((cases, unknowns), F32), shape((chord, cases, lanes), F32)),
-                scratch=[pltpu.VMEM((2 * cases, unknowns), BF16)],
-            )(*came, pick, corner, result[0])
-            images.append(resid)
+            send = call(corner_kernel, shape((chord, cases, lanes), F32))(
+                *came, arrive, local_corner
+            )
             got = exchange(send, "chord")
 
     inner = 16 if span % 16 == 0 else span

time: 202 us -> 193 us (0.955)
  waiting for transfers between devices: 26.7 us -> 15.1 us
  Pallas kernels: 25.4 us -> 28.7 us
    ppermute x18, waiting for transfers between devices: 14.5 us -> 2.89 us  [shifted(): return lax.ppermute(value, axis, pairs)]
    pallas_call x15, Pallas kernels: 21.1 us -> 23.7 us  [the longest x4 12.7 us: shards(): call(functools.partial(local_kernel, step=step), (full, full, table) + ((...]
  transfers between devices with their start and end apart: 19 -> 19, of which waited for: 10 -> 5; matrix products, arithmetic and copies ran while one was open for 0% -> 0% of each run, Pallas kernels for 2% -> 9%
where the time goes in v3:
time: 193 us; the launch traced here: 192 us
  blocking collectives  95.7 us (50%)
  starting transfers between devices  36.9 us (19%)
  Pallas kernels  28.7 us (15%)
  waiting for transfers between devices  15.1 us (8%)
  between operations  14.4 us (7%)
    all_to_all x6, blocking collectives, exchange(): return lax.all_to_all(send, axis, 0, 0, axis_index_groups=groups)  95.7 us
    ppermute x18, starting transfers between devices, shifted(): return lax.ppermute(value, axis, pairs)  31.8 us
    pallas_call x4, Pallas kernels, shards(): call(functools.partial(local_kernel, step=step), (full, full, table) + ((...  12.7 us
    all_to_all x1, waiting for transfers between devices, exchange(): return lax.all_to_all(send, axis, 0, 0, axis_index_groups=groups)  12.2 us
    all_to_all x1, starting transfers between devices, exchange(): return lax.all_to_all(send, axis, 0, 0, axis_index_groups=groups)  5.06 us
    pallas_call x1, Pallas kernels, shards(): call(first_local_kernel, (full, table, full, corners, full, shape((unknow...  4.88 us
  transfers between devices with their start and end apart: 19, of which 5 were waited for; matrix products, arithmetic and copies ran while one was open for 0% of the time, Pallas kernels for 9%

profile of v3, /device:TPU:1, one launch (start us, length us, event | category | flops | bytes accessed | tf_op | source)
XLA Modules:
  0.0 191.7 jit_solution(11501867660208560739)
XLA Ops:
  6.5 3.0 %shard_map.75 = (bf16[1536,1536]{1,0:T(8,128)(2,1)S(1)}, bf16[1536,128]{1,0:T(8,128)(2,1)S(1)}, f32[1,1536]{1,0:T(1,128)S(1)}, f32[8,216,128]{2,1,0:T(8,128)S(1)}) custom-call(s32[4]{0:T(128)} %bitcast.179, bf16[1536,1536]{1,0:T(8,128)(2,1)} %bitcast.149, bf16[64,1536]{1,0:T(8,128)(2,1)} %bitcast.160, s32[4,384]{1,0:T(4,128)} %bitcast.172, ...), custom_call_target="tpu_custom_call" | custom-call | tf_op jit(solution)/shard_map/pallas_call | solution.py:454
  9.5 22.8 %all_to_all.35.got = f32[8,216,128]{2,1,0:T(8,128)S(1)} all-to-all(f32[8,216,128]{2,1,0:T(8,128)S(1)} %get-tuple-element.161), channel_id=1, replica_groups=mesh['span'=64,'chord'=8] {'chord'}, dimensions={0} | all-to-all | bytes 1769472 | tf_op jit(solution)/shard_map/all_to_all | solution.py:426
  32.3 1.5 shard_map.76.lift
  33.8 1.2 shard_map.77
  35.0 1.3 collective-permute-start.8
  36.3 1.3 collective-permute-start.9
  37.6 1.0 collective-permute-start.10
  38.7 4.9 %shard_map.78 = (f32[64,1536]{1,0:T(8,128)S(1)}, f32[64,128]{1,0:T(8,128)S(1)}, f32[64,1536]{1,0:T(8,128)S(1)}, f32[64,128]{1,0:T(8,128)S(1)}, f32[64,1536]{1,0:...) custom-call(bf16[128,1536]{1,0:T(8,128)(2,1)S(1)} %get-tuple-element, ...), custom_call_target="tpu_custom_call" | custom-call | flops 1000000000 | bytes 1000000 | tf_op jit(solution)/shard_map/pallas_call | solution.py:500
  43.6 0.3 shard_map.79
  43.9 11.7 %all_to_all.36.got = f32[8,64,128]{2,1,0:T(8,128)S(1)} all-to-all(f32[8,64,128]{2,1,0:T(8,128)S(1)} %shard_map.79), channel_id=1, replica_groups=mesh['span'=64,'chord'=8] {'chord'}, dimensions={0} | all-to-all | bytes 524288 | tf_op jit(solution)/shard_map/all_to_all | solution.py:426
  55.5 0.6 shard_map.80
  56.1 4.3 %collective-permute-start.12 = (f32[64,384]{1,0:T(8,128)S(1)}, f32[64,384]{1,0:T(8,128)S(1)}, u32[]{:S(2)}, u32[]{:S(2)}) collective-permute-start(f32[64,384]{1,0:T(8,128)S(1)} %get-tuple-element.175), channel_id=1, source_target_pairs={{0,8},{8,16},{16,24},{24,32},{32,40},{40,48},{48,56},{56,64},{64,7... | collective-permute-start | bytes 294920 | tf_op jit(solution)/shard_map/ppermute | solution.py:422
  60.4 1.3 collective-permute-start.13
  61.7 1.5 collective-permute-start.14
  63.2 3.3 %shard_map.81 = (f32[64,1536]{1,0:T(8,128)S(1)}, f32[64,1536]{1,0:T(8,128)S(1)}, f32[64,128]{1,0:T(8,128)S(1)}, f32[64,1536]{1,0:T(8,128)S(1)}, f32[64,128]{1,0:T(8,128)S(1)}, /*index=5*/f32[64,1536]{1,0:T(8,128)S(1)}) custom-call(f32[64,384]{1,0:T(8,128)S(1)} %collective-permute-done.8.from0.refs_0_, f32[64,384]{1,0:T(8,128)S(1)} %collective-permute-done.9.from1.refs_1_, ...), custom_call_target="tpu_custom_call" | custom-call | flops 1000000000 | bytes 1000000 | tf_op jit(solution)/shard_map/pallas_call | solution.py:512
  66.6 1.0 collective-permute-done.15.from3.refs_3_
  67.5 0.3 shard_map.82
  67.8 11.3 %all_to_all.37.got = f32[8,64,128]{2,1,0:T(8,128)S(1)} all-to-all(f32[8,64,128]{2,1,0:T(8,128)S(1)} %shard_map.82), channel_id=1, replica_groups=mesh['span'=64,'chord'=8] {'chord'}, dimensions={0} | all-to-all | bytes 524288 | tf_op jit(solution)/shard_map/all_to_all | solution.py:426
  79.1 0.6 shard_map.83
  79.7 4.3 %collective-permute-start.16 = (f32[64,384]{1,0:T(8,128)S(1)}, f32[64,384]{1,0:T(8,128)S(1)}, u32[]{:S(2)}, u32[]{:S(2)}) collective-permute-start(f32[64,384]{1,0:T(8,128)S(1)} %get-tuple-element.186), channel_id=1, source_target_pairs={{0,8},{8,16},{16,24},{24,32},{32,40},{40,48},{48,56},{56,64},{64,7... | collective-permute-start | bytes 294920 | tf_op jit(solution)/shard_map/ppermute | solution.py:422
  83.9 1.6 collective-permute-start.17
  85.5 1.5 collective-permute-start.18
  87.0 3.3 %shard_map.84 = (f32[64,1536]{1,0:T(8,128)S(1)}, f32[64,1536]{1,0:T(8,128)S(1)}, f32[64,128]{1,0:T(8,128)S(1)}, f32[64,1536]{1,0:T(8,128)S(1)}, f32[64,128]{1,0:T(8,128)S(1)}, /*index=5*/f32[64,1536]{1,0:T(8,128)S(1)}) custom-call(f32[64,384]{1,0:T(8,128)S(1)} %collective-permute-done.12.from0.refs_0_, f32[64,384]{1,0:T(8,128)S(1)} %collective-permute-done.13.from1.refs_1_, ...), custom_call_target="tpu_custom_call" | custom-call | flops 1000000000 | bytes 1000000 | tf_op jit(solution)/shard_map/pallas_call | solution.py:512
  90.4 1.0 collective-permute-done.19.from3.refs_3_
  91.4 0.3 shard_map.85
  91.6 11.3 %all_to_all.38.got = f32[8,64,128]{2,1,0:T(8,128)S(1)} all-to-all(f32[8,64,128]{2,1,0:T(8,128)S(1)} %shard_map.85), channel_id=1, replica_groups=mesh['span'=64,'chord'=8] {'chord'}, dimensions={0} | all-to-all | bytes 524288 | tf_op jit(solution)/shard_map/all_to_all | solution.py:426
  102.9 0.6 shard_map.86
  103.5 4.3 %collective-permute-start.20 = (f32[64,384]{1,0:T(8,128)S(1)}, f32[64,384]{1,0:T(8,128)S(1)}, u32[]{:S(2)}, u32[]{:S(2)}) collective-permute-start(f32[64,384]{1,0:T(8,128)S(1)} %get-tuple-element.197), channel_id=1, source_target_pairs={{0,8},{8,16},{16,24},{24,32},{32,40},{40,48},{48,56},{56,64},{64,7... | collective-permute-start | bytes 294920 | tf_op jit(solution)/shard_map/ppermute | solution.py:422
  107.8 1.3 collective-permute-start.21
  109.1 1.5 collective-permute-start.22
  110.6 3.4 %shard_map.87 = (f32[64,1536]{1,0:T(8,128)S(1)}, f32[64,1536]{1,0:T(8,128)S(1)}, f32[64,128]{1,0:T(8,128)S(1)}, f32[64,1536]{1,0:T(8,128)S(1)}, f32[64,128]{1,0:T(8,128)S(1)}, /*index=5*/f32[64,1536]{1,0:T(8,128)S(1)}) custom-call(f32[64,384]{1,0:T(8,128)S(1)} %collective-permute-done.16.from0.refs_0_, f32[64,384]{1,0:T(8,128)S(1)} %collective-permute-done.17.from1.refs_1_, ...), custom_call_target="tpu_custom_call" | custom-call | flops 1000000000 | bytes 1000000 | tf_op jit(solution)/shard_map/pallas_call | solution.py:512
  114.0 0.7 collective-permute-done.21.from1.refs_1_
  114.7 0.2 collective-permute-done.23.from3.refs_3_
  114.9 0.3 shard_map.88
  115.2 11.3 %all_to_all.39.got = f32[8,64,128]{2,1,0:T(8,128)S(1)} all-to-all(f32[8,64,128]{2,1,0:T(8,128)S(1)} %shard_map.88), channel_id=1, replica_groups=mesh['span'=64,'chord'=8] {'chord'}, dimensions={0} | all-to-all | bytes 524288 | tf_op jit(solution)/shard_map/all_to_all | solution.py:426
  126.5 0.6 shard_map.89
  127.0 5.3 %collective-permute-start.24 = (f32[64,384]{1,0:T(8,128)S(1)}, f32[64,384]{1,0:T(8,128)S(1)}, u32[]{:S(2)}, u32[]{:S(2)}) collective-permute-start(f32[64,384]{1,0:T(8,128)S(1)} %get-tuple-element.215), channel_id=1, source_target_pairs={{0,8},{8,16},{16,24},{24,32},{32,40},{40,48},{48,56},{56,64},{64,7... | collective-permute-start | bytes 294920 | tf_op jit(solution)/shard_map/ppermute | solution.py:422
  132.3 1.5 collective-permute-start.25
  133.8 2.7 %shard_map.90 = (f32[64,1536]{1,0:T(8,128)}, f32[64,1536]{1,0:T(8,128)S(1)}, f32[64,128]{1,0:T(8,128)S(1)}) custom-call(f32[64,384]{1,0:T(8,128)S(1)} %collective-permute-done.20.from0.refs_0_, f32[64,384]{1,0:T(8,128)S(1)} %collective-permute-done.21.from1.refs_1_, f32[64,384]{1,0:T(8,128)S(1)} %collective-permute-done.22.from2.refs_2_, ...), custom_call_target="tpu_custom_call" | custom-call | flops 1000000000 | bytes 1000000 | tf_op jit(solution)/shard_map/pallas_call | solution.py:512
  136.5 0.2 shard_map.91
  136.8 27.5 %all_to_all.40.got = f32[32,16,128]{2,1,0:T(8,128)S(1)} all-to-all(f32[32,16,128]{2,1,0:T(8,128)S(1)} %shard_map.91), channel_id=1, replica_groups={{0,1,2,3,4,5,6,7,128,129,130,131,132,133,134,135,256,257,258,259,260,26..., dimensions={0} | all-to-all | bytes 524288 | tf_op jit(solution)/shard_map/all_to_all | solution.py:426
  164.3 0.7 shard_map.92
  164.9 5.1 %all-to-all-start.6 = ((f32[16,16,128]{2,1,0:T(8,128)}), f32[16,16,128]{2,1,0:T(8,128)S(1)}, u32[]{:S(2)}, u32[]{:S(2)}) async-start(f32[16,16,128]{2,1,0:T(8,128)} %shard_map.92), calls=%async_computation.6 | async-start | bytes 262144 | tf_op jit(solution)/shard_map/all_to_all | solution.py:426
  170.0 12.2 %all-to-all-done.6.got = f32[16,16,128]{2,1,0:T(8,128)S(1)} async-done(((f32[16,16,128]{2,1,0:T(8,128)}), f32[16,16,128]{2,1,0:T(8,128)S(1)}, u32[]{:S(2)}, u32[]{:S(2)}) %all-to-all-start.6) | async-done | bytes 131104 | tf_op jit(solution)/shard_map/all_to_all | solution.py:426
  182.2 1.0 shard_map.93
  183.9 0.2 conditional.1
  184.1 0.0 copy-start.6
  184.1 0.7 copy-done.6
  (29 shorter events, 0.1 us)
Async XLA Ops:
  6.5 27.2 %copy-start.1 = (bf16[1,1,64,1536]{3,2,1,0:T(8,128)(2,1)S(1)}, bf16[1,1,64,1536]{3,2,1,0:T(8,128)(2,1)}, u32[]{:S(2)}) copy-start(bf16[1,1,64,1536]{3,2,1,0:T(8,128)(2,1)} %param.12) | copy-start | bytes 589828
  6.5 32.1 %slice-start = ((s8[4718592]{0:T(1024)(128)(4,1)}), s8[4194304]{0:T(1024)(128)(4,1)S(1)}, s32[]{:S(2)}) async-start(s8[4718592]{0:T(1024)(128)(4,1)} %bitcast.150), calls=%async_computation.9 | async-start | bytes 8388608
  32.3 6.4 %slice-start.1 = ((s8[4718592]{0:T(1024)(128)(4,1)}), s8[524288]{0:T(1024)(128)(4,1)S(1)}, s32[]{:S(2)}) async-start(s8[4718592]{0:T(1024)(128)(4,1)} %bitcast.150), calls=%async_computation.10 | async-start | bytes 1048576
  35.0 8.5 %collective-permute-start.8 = (f32[64,384]{1,0:T(8,128)S(1)}, f32[64,384]{1,0:T(8,128)S(1)}, u32[]{:S(2)}, u32[]{:S(2)}) collective-permute-start(f32[64,384]{1,0:T(8,128)S(1)} %get-tuple-element.165), channel_id=1, source_target_pairs={{0,8},{8,16},{16,24},{24,32},{32,40},{40,48},{48,56},{56,64},{64,7... | collective-permute-start | bytes 294920 | tf_op jit(solution)/shard_map/ppermute | solution.py:422
  36.3 7.2 %collective-permute-start.9 = (f32[64,384]{1,0:T(8,128)S(1)}, f32[64,384]{1,0:T(8,128)S(1)}, u32[]{:S(2)}, u32[]{:S(2)}) collective-permute-start(f32[64,384]{1,0:T(8,128)S(1)} %get-tuple-element.166), channel_id=1, source_target_pairs={{8,0},{16,8},{24,16},{32,24},{40,32},{48,40},{56,48},{64,56},{72,6... | collective-permute-start | bytes 294920 | tf_op jit(solution)/shard_map/ppermute | solution.py:422
  37.6 5.9 %collective-permute-start.10 = (f32[64,384]{1,0:T(8,128)S(1)}, f32[64,384]{1,0:T(8,128)S(1)}, u32[]{:S(2)}, u32[]{:S(2)}) collective-permute-start(f32[64,384]{1,0:T(8,128)S(1)} %get-tuple-element.167), channel_id=1, source_target_pairs={{0,1},{1,2},{2,3},{3,4},{4,5},{5,6},{6,7},{7,0},{8,9},{9,10},{10,1... | collective-permute-start | bytes 294920 | tf_op jit(solution)/shard_map/ppermute | solution.py:422
  38.7 4.9 %collective-permute-start.11 = (f32[64,384]{1,0:T(8,128)S(1)}, f32[64,384]{1,0:T(8,128)S(1)}, u32[]{:S(2)}, u32[]{:S(2)}) collective-permute-start(f32[64,384]{1,0:T(8,128)S(1)} %get-tuple-element.168), channel_id=1, source_target_pairs={{0,7},{1,0},{2,1},{3,2},{4,3},{5,4},{6,5},{7,6},{8,15},{9,8},{10,9... | collective-permute-start | bytes 294920 | tf_op jit(solution)/shard_map/ppermute | solution.py:422
  56.1 10.4 %collective-permute-start.12 = (f32[64,384]{1,0:T(8,128)S(1)}, f32[64,384]{1,0:T(8,128)S(1)}, u32[]{:S(2)}, u32[]{:S(2)}) collective-permute-start(f32[64,384]{1,0:T(8,128)S(1)} %get-tuple-element.175), channel_id=1, source_target_pairs={{0,8},{8,16},{16,24},{24,32},{32,40},{40,48},{48,56},{56,64},{64,7... | collective-permute-start | bytes 294920 | tf_op jit(solution)/shard_map/ppermute | solution.py:422
  60.4 6.2 %collective-permute-start.13 = (f32[64,384]{1,0:T(8,128)S(1)}, f32[64,384]{1,0:T(8,128)S(1)}, u32[]{:S(2)}, u32[]{:S(2)}) collective-permute-start(f32[64,384]{1,0:T(8,128)S(1)} %get-tuple-element.176), channel_id=1, source_target_pairs={{8,0},{16,8},{24,16},{32,24},{40,32},{48,40},{56,48},{64,56},{72,6... | collective-permute-start | bytes 294920 | tf_op jit(solution)/shard_map/ppermute | solution.py:422
  61.7 4.9 %collective-permute-start.14 = (f32[64,384]{1,0:T(8,128)S(1)}, f32[64,384]{1,0:T(8,128)S(1)}, u32[]{:S(2)}, u32[]{:S(2)}) collective-permute-start(f32[64,384]{1,0:T(8,128)S(1)} %get-tuple-element.177), channel_id=1, source_target_pairs={{0,1},{1,2},{2,3},{3,4},{4,5},{5,6},{6,7},{7,0},{8,9},{9,10},{10,1... | collective-permute-start | bytes 294920 | tf_op jit(solution)/shard_map/ppermute | solution.py:422
  63.2 4.3 %collective-permute-start.15 = (f32[64,384]{1,0:T(8,128)S(1)}, f32[64,384]{1,0:T(8,128)S(1)}, u32[]{:S(2)}, u32[]{:S(2)}) collective-permute-start(f32[64,384]{1,0:T(8,128)S(1)} %get-tuple-element.178), channel_id=1, source_target_pairs={{0,7},{1,0},{2,1},{3,2},{4,3},{5,4},{6,5},{7,6},{8,15},{9,8},{10,9... | collective-permute-start | bytes 294920 | tf_op jit(solution)/shard_map/ppermute | solution.py:422
  79.7 10.7 %collective-permute-start.16 = (f32[64,384]{1,0:T(8,128)S(1)}, f32[64,384]{1,0:T(8,128)S(1)}, u32[]{:S(2)}, u32[]{:S(2)}) collective-permute-start(f32[64,384]{1,0:T(8,128)S(1)} %get-tuple-element.186), channel_id=1, source_target_pairs={{0,8},{8,16},{16,24},{24,32},{32,40},{40,48},{48,56},{56,64},{64,7... | collective-permute-start | bytes 294920 | tf_op jit(solution)/shard_map/ppermute | solution.py:422
  83.9 6.5 %collective-permute-start.17 = (f32[64,384]{1,0:T(8,128)S(1)}, f32[64,384]{1,0:T(8,128)S(1)}, u32[]{:S(2)}, u32[]{:S(2)}) collective-permute-start(f32[64,384]{1,0:T(8,128)S(1)} %get-tuple-element.187), channel_id=1, source_target_pairs={{8,0},{16,8},{24,16},{32,24},{40,32},{48,40},{56,48},{64,56},{72,6... | collective-permute-start | bytes 294920 | tf_op jit(solution)/shard_map/ppermute | solution.py:422
  85.5 4.9 %collective-permute-start.18 = (f32[64,384]{1,0:T(8,128)S(1)}, f32[64,384]{1,0:T(8,128)S(1)}, u32[]{:S(2)}, u32[]{:S(2)}) collective-permute-start(f32[64,384]{1,0:T(8,128)S(1)} %get-tuple-element.188), channel_id=1, source_target_pairs={{0,1},{1,2},{2,3},{3,4},{4,5},{5,6},{6,7},{7,0},{8,9},{9,10},{10,1... | collective-permute-start | bytes 294920 | tf_op jit(solution)/shard_map/ppermute | solution.py:422
  87.0 4.3 %collective-permute-start.19 = (f32[64,384]{1,0:T(8,128)S(1)}, f32[64,384]{1,0:T(8,128)S(1)}, u32[]{:S(2)}, u32[]{:S(2)}) collective-permute-start(f32[64,384]{1,0:T(8,128)S(1)} %get-tuple-element.189), channel_id=1, source_target_pairs={{0,7},{1,0},{2,1},{3,2},{4,3},{5,4},{6,5},{7,6},{8,15},{9,8},{10,9... | collective-permute-start | bytes 294920 | tf_op jit(solution)/shard_map/ppermute | solution.py:422
  103.5 10.5 %collective-permute-start.20 = (f32[64,384]{1,0:T(8,128)S(1)}, f32[64,384]{1,0:T(8,128)S(1)}, u32[]{:S(2)}, u32[]{:S(2)}) collective-permute-start(f32[64,384]{1,0:T(8,128)S(1)} %get-tuple-element.197), channel_id=1, source_target_pairs={{0,8},{8,16},{16,24},{24,32},{32,40},{40,48},{48,56},{56,64},{64,7... | collective-permute-start | bytes 294920 | tf_op jit(solution)/shard_map/ppermute | solution.py:422
  107.8 6.9 %collective-permute-start.21 = (f32[64,384]{1,0:T(8,128)S(1)}, f32[64,384]{1,0:T(8,128)S(1)}, u32[]{:S(2)}, u32[]{:S(2)}) collective-permute-start(f32[64,384]{1,0:T(8,128)S(1)} %get-tuple-element.198), channel_id=1, source_target_pairs={{8,0},{16,8},{24,16},{32,24},{40,32},{48,40},{56,48},{64,56},{72,6... | collective-permute-start | bytes 294920 | tf_op jit(solution)/shard_map/ppermute | solution.py:422
  109.1 5.6 %collective-permute-start.22 = (f32[64,384]{1,0:T(8,128)S(1)}, f32[64,384]{1,0:T(8,128)S(1)}, u32[]{:S(2)}, u32[]{:S(2)}) collective-permute-start(f32[64,384]{1,0:T(8,128)S(1)} %get-tuple-element.199), channel_id=1, source_target_pairs={{0,1},{1,2},{2,3},{3,4},{4,5},{5,6},{6,7},{7,0},{8,9},{9,10},{10,1... | collective-permute-start | bytes 294920 | tf_op jit(solution)/shard_map/ppermute | solution.py:422
  110.6 4.3 %collective-permute-start.23 = (f32[64,384]{1,0:T(8,128)S(1)}, f32[64,384]{1,0:T(8,128)S(1)}, u32[]{:S(2)}, u32[]{:S(2)}) collective-permute-start(f32[64,384]{1,0:T(8,128)S(1)} %get-tuple-element.200), channel_id=1, source_target_pairs={{0,7},{1,0},{2,1},{3,2},{4,3},{5,4},{6,5},{7,6},{8,15},{9,8},{10,9... | collective-permute-start | bytes 294920 | tf_op jit(solution)/shard_map/ppermute | solution.py:422
  127.0 9.5 %collective-permute-start.24 = (f32[64,384]{1,0:T(8,128)S(1)}, f32[64,384]{1,0:T(8,128)S(1)}, u32[]{:S(2)}, u32[]{:S(2)}) collective-permute-start(f32[64,384]{1,0:T(8,128)S(1)} %get-tuple-element.215), channel_id=1, source_target_pairs={{0,8},{8,16},{16,24},{24,32},{32,40},{40,48},{48,56},{56,64},{64,7... | collective-permute-start | bytes 294920 | tf_op jit(solution)/shard_map/ppermute | solution.py:422
  132.3 4.2 %collective-permute-start.25 = (f32[64,384]{1,0:T(8,128)S(1)}, f32[64,384]{1,0:T(8,128)S(1)}, u32[]{:S(2)}, u32[]{:S(2)}) collective-permute-start(f32[64,384]{1,0:T(8,128)S(1)} %get-tuple-element.217), channel_id=1, source_target_pairs={{0,1},{1,2},{2,3},{3,4},{4,5},{5,6},{6,7},{7,0},{8,9},{9,10},{10,1... | collective-permute-start | bytes 294920 | tf_op jit(solution)/shard_map/ppermute | solution.py:422
  133.8 50.1 %copy-start.2 = (s32[1,1,4,384]{3,2,1,0:T(4,128)S(1)}, s32[1,1,4,384]{3,2,1,0:T(4,128)}, u32[]{:S(2)}) copy-start(s32[1,1,4,384]{3,2,1,0:T(4,128)} %param.13) | copy-start | bytes 18436
  133.8 50.1 %copy-start.5 = (s32[1,1,4]{2,1,0:T(1,128)S(1)}, s32[1,1,4]{2,1,0:T(1,128)}, u32[]{:S(2)}) copy-start(s32[1,1,4]{2,1,0:T(1,128)} %param.14) | copy-start | bytes 52
  164.9 17.2 %all-to-all-start.6 = ((f32[16,16,128]{2,1,0:T(8,128)}), f32[16,16,128]{2,1,0:T(8,128)S(1)}, u32[]{:S(2)}, u32[]{:S(2)}) async-start(f32[16,16,128]{2,1,0:T(8,128)} %shard_map.92), calls=%async_computation.6 | async-start | bytes 262144 | tf_op jit(solution)/shard_map/all_to_all | solution.py:426
  184.1 0.7 copy-start.6

commit v4 on v3

--- a/solution.py
+++ b/solution.py
@@ -11,7 +11,7 @@
 F32 = jnp.float32
 BF16 = jnp.bfloat16
 PIVOT_FLOOR = 2e-5
-GRAM_ROWS = 16
+GRAM_ROWS = 8
 
 
 def with_halo(block, sides, width):
@@ -133,7 +133,7 @@
 
 
 def setup_kernel(
-    counts, schur, loads, rows, corners, slots, coarse,
+    counts, turn_ref, schur, loads, rows, corners, slots, coarse,
     pick_ref, corner_ref, inv_ref, send_ref, blocks, sems,
 ):
     unknowns = loads.shape[1]
@@ -172,32 +172,41 @@
     picked = mm(loads[...], corner_ref[...])
     cases = picked.shape[0]
     own, total = coarse.shape
+    parts = (send_ref.shape[1] - cases - 8) // own
+    turned = pltpu.roll(coarse[...], turn_ref[0], 1)
     for peer in range(send_ref.shape[0]):
         send_ref[peer, :cases, :] = picked
-        for part in range(total // lanes):
-            send_ref[peer, cases + part * own : cases + (part + 1) * own, :] = coarse[
+        for part in range(parts):
+            send_ref[peer, cases + part * own : cases + (part + 1) * own, :] = turned[
                 :, part * lanes : (part + 1) * lanes
             ]
-        send_ref[peer, cases + own * (total // lanes) :, :] = jnp.broadcast_to(
+        send_ref[peer, cases + own * parts :, :] = jnp.broadcast_to(
             slots[...].astype(F32), (8, lanes)
         )
+
+
+def coarse_parts(own, peers, lanes):
+    return -(-own * (peers // 2 + 1) // lanes)
 
 
 def lift_kernel(slots, got, lift_ref, *, cases, own):
     peers, _, lanes = got.shape
     total = own * peers
-    parts = total // lanes
+    parts = coarse_parts(own, peers, lanes)
     index = lax.broadcasted_iota(jnp.int32, (total, lanes), 0)
     mine = (index == slots[...]).astype(F32).astype(BF16)
-    inverse = jnp.concatenate(
-        [
-            jnp.concatenate(
-                [got[p, cases + q * own : cases + (q + 1) * own, :] for q in range(parts)], axis=1
-            )
-            for p in range(peers)
-        ],
-        axis=0,
-    )
+    lane = lax.broadcasted_iota(jnp.int32, (own, total), 1)
+    reach = own * (peers // 2)
+    weight = jnp.where((lane < own) | (lane >= reach), 0.5, 1.0)
+    weight = jnp.where(lane < reach + own, weight, 0.0)
+    rows = []
+    for p in range(peers):
+        pieces = [got[p, cases + q * own : cases + (q + 1) * own, :] for q in range(parts)]
+        pieces += [jnp.zeros((own, lanes), F32)] * (total // lanes - parts)
+        row = jnp.concatenate(pieces, axis=1) * weight
+        rows.append(pltpu.roll(row, p * own, 1) if p else row)
+    half = jnp.concatenate(rows, axis=0)
+    inverse = half + half.T
     high = inverse.astype(BF16)
     rest = inverse - high.astype(F32)
     middle, low = halves(rest)
@@ -246,7 +255,9 @@
 
 
 def gram_slot(row, col):
-    return col * (col + 1) // 2 + row + 5 if row >= 0 else col
+    if row < 0:
+        return 0 if col == 0 else gram_slot(0, col - 1)
+    return col * (col + 1) // 2 + row + 1
 
 
 def put(total, slot, value):
@@ -261,7 +272,7 @@
 def first_local_kernel(
     field, matrix, corner, pick, inv, loads,
     field_ref, acc_ref, local_ref, local_corner_ref, ahead_ref,
-    arrive_ref, leave_ref, corner_matrix_ref, inv_sent_ref,
+    leave_ref, corner_matrix_ref, inv_sent_ref,
 ):
     cases, unknowns = loads.shape
     local = folded(mm(field[...], matrix[...]))
@@ -285,7 +296,6 @@
         ahead_ref[:, cols] = folded(picked[: 2 * cases])
         parts = picked[2 * cases :]
         inv_sent_ref[:, cols] = parts[0:1] + parts[8:9] + parts[16:17]
-        arrive_ref[cols, :] = mm(pick[:, cols], corner[...], TN).astype(BF16)
         leave_ref[:, cols] = mm(corner[...], pick[:, cols], TN).astype(BF16)
         corner_matrix_ref[:, cols] = mm(corner[...], matrix[:, cols], TN).astype(BF16)
 
@@ -312,7 +322,7 @@
     value = scaled[:cases, :].astype(F32) + scaled[cases:, :].astype(F32) + added
     field_ref[...] = value
     local = folded(mm(scaled[...], matrix[...])) + folded(mm(back[...], corner_matrix[...]))
-    total = put(acc[...], gram_slot(-1, step), product(value, loads[...].astype(F32)))
+    total = acc[...]
     for row in range(step):
         image = image_ref if row == step - 1 else images[row]
         total = put(total, gram_slot(row, step), product(value, image[...]))
@@ -331,12 +341,12 @@
     acc_ref[...] = total
 
 
-def corner_kernel(from0, from1, from2, from3, arrive, local_corner, send_ref):
+def corner_kernel(from0, from1, from2, from3, leave, local_corner, send_ref):
     width = from0.shape[1]
     total = local_corner[...]
     for side, came in enumerate((from0, from1, from2, from3)):
-        rows = slice(side * width, (side + 1) * width)
-        total = total - folded(mm(stacked(came[...]), arrive[rows, :]))
+        cols = slice(side * width, (side + 1) * width)
+        total = total - folded(mm(stacked(came[...]), leave[:, cols], NT))
     for peer in range(send_ref.shape[0]):
         send_ref[peer] = total
 
@@ -451,22 +461,24 @@
     slots = corner_map[0]
 
     tile = 128
+    turn = lax.rem(total - lax.axis_index("chord") * own, total).astype(jnp.int32).reshape(1)
     pick, corner, inv, send = pl.pallas_call(
         setup_kernel,
-        in_specs=[pl.BlockSpec(memory_space=pltpu.SMEM), pl.BlockSpec(memory_space=pl.ANY)]
+        in_specs=[pl.BlockSpec(memory_space=pltpu.SMEM)] * 2
+        + [pl.BlockSpec(memory_space=pl.ANY)]
         + [pl.BlockSpec(memory_space=pltpu.VMEM)] * 5,
         out_shape=(
             shape((unknowns, unknowns), BF16),
             shape((unknowns, lanes), BF16),
             shape((1, unknowns), F32),
-            shape((chord, cases + own * (total // lanes) + 8, lanes), F32),
+            shape((chord, cases + own * coarse_parts(own, chord, lanes) + 8, lanes), F32),
         ),
         scratch_shapes=[
             pltpu.VMEM((unknowns // tile, tile, tile), BF16),
             pltpu.SemaphoreType.DMA((unknowns // tile,)),
         ],
         compiler_params=pltpu.CompilerParams(vmem_limit_bytes=28 * 2**20),
-    )(counts, matrix, rhs, rows, corner_rows[0], slots, block)
+    )(counts, turn, matrix, rhs, rows, corner_rows[0], slots, block)
     got = exchange(send, "chord")
     lift = call(
         functools.partial(lift_kernel, cases=cases, own=own),
@@ -497,11 +509,10 @@
             None if last else shifted(sends[2], "chord", -1, True),
         ]
         if step == 0:
-            field, acc, local, local_corner, ahead, arrive, leave, corner_matrix, inv_sent = call(
+            field, acc, local, local_corner, ahead, leave, corner_matrix, inv_sent = call(
                 first_local_kernel,
                 (
                     full, table, full, corners, full,
-                    shape((unknowns, lanes), BF16),
                     shape((lanes, unknowns), BF16),
                     shape((lanes, unknowns), BF16),
                     shape((1, unknowns), F32),
@@ -524,7 +535,7 @@
         fields.append(field)
         if not last:
             send = call(corner_kernel, shape((chord, cases, lanes), F32))(
-                *came, arrive, local_corner
+                *came, leave, local_corner
             )
             got = exchange(send, "chord")
 

time: 193 us -> 189 us (0.979)
  blocking collectives: 95.7 us -> 91.3 us
    all_to_all x6, blocking collectives: 95.7 us -> 91.3 us  [exchange(): return lax.all_to_all(send, axis, 0, 0, axis_index_groups=groups)]
  transfers between devices with their start and end apart: 19 -> 19, of which waited for: 5 -> 6; matrix products, arithmetic and copies ran while one was open for 0% -> 0% of each run, Pallas kernels for 9% -> 9%
where the time goes in v4:
time: 189 us; the launch traced here: 188 us
  blocking collectives  91.3 us (48%)
  starting transfers between devices  36.9 us (20%)
  Pallas kernels  28.5 us (15%)
  waiting for transfers between devices  15.2 us (8%)
  between operations  14.4 us (8%)
    all_to_all x6, blocking collectives, exchange(): return lax.all_to_all(send, axis, 0, 0, axis_index_groups=groups)  91.3 us
    ppermute x18, starting transfers between devices, shifted(): return lax.ppermute(value, axis, pairs)  31.9 us
    pallas_call x4, Pallas kernels, shards(): call(functools.partial(local_kernel, step=step), (full, full, table) + ((...  13.3 us
    all_to_all x1, waiting for transfers between devices, exchange(): return lax.all_to_all(send, axis, 0, 0, axis_index_groups=groups)  11.6 us
    all_to_all x1, starting transfers between devices, exchange(): return lax.all_to_all(send, axis, 0, 0, axis_index_groups=groups)  5.02 us
  transfers between devices with their start and end apart: 19, of which 6 were waited for; matrix products, arithmetic and copies ran while one was open for 0% of the time, Pallas kernels for 9%

profile of v4, /device:TPU:1, one launch (start us, length us, event | category | flops | bytes accessed | tf_op | source)
XLA Modules:
  0.0 188.0 jit_solution(14774731478743050224)
XLA Ops:
  6.5 2.9 %shard_map.75 = (bf16[1536,1536]{1,0:T(8,128)(2,1)S(1)}, bf16[1536,128]{1,0:T(8,128)(2,1)S(1)}, f32[1,1536]{1,0:T(1,128)S(1)}, f32[8,168,128]{2,1,0:T(8,128)S(1)}) custom-call(s32[4]{0:T(128)} %bitcast.180, s32[1]{0:T(128)} %bitcast.29.turn_ref, bf16[1536,1536]{1,0:T(8,128)(2,1)} %bitcast.150, bf16[64,1536]{1,0:T(8,128)(2,1)} %bitcast.161, ...), custom_call_target="tpu_custom_call" | custom-call | tf_op jit(solution)/shard_map/pallas_call | solution.py:465
  9.5 20.5 %all_to_all.35.got = f32[8,168,128]{2,1,0:T(8,128)S(1)} all-to-all(f32[8,168,128]{2,1,0:T(8,128)S(1)} %get-tuple-element.160), channel_id=1, replica_groups=mesh['span'=64,'chord'=8] {'chord'}, dimensions={0} | all-to-all | bytes 1376256 | tf_op jit(solution)/shard_map/all_to_all | solution.py:436
  30.0 1.7 shard_map.76.lift
  31.7 1.2 shard_map.77
  33.0 1.3 collective-permute-start.8
  34.3 1.3 collective-permute-start.9
  35.6 1.1 collective-permute-start.10
  36.7 3.6 %shard_map.78 = (f32[64,1536]{1,0:T(8,128)S(1)}, f32[64,128]{1,0:T(8,128)S(1)}, f32[64,1536]{1,0:T(8,128)S(1)}, f32[64,128]{1,0:T(8,128)S(1)}, f32[64,1536]{1,0:...) custom-call(bf16[128,1536]{1,0:T(8,128)(2,1)S(1)} %get-tuple-element.168.field, ...), custom_call_target="tpu_custom_call" | custom-call | flops 1000000000 | bytes 1000000 | tf_op jit(solution)/shard_map/pallas_call | solution.py:512
  40.4 0.6 collective-permute-done.11.from3.refs_3_
  41.0 0.3 shard_map.79
  41.3 11.3 %all_to_all.36.got = f32[8,64,128]{2,1,0:T(8,128)S(1)} all-to-all(f32[8,64,128]{2,1,0:T(8,128)S(1)} %shard_map.79), channel_id=1, replica_groups=mesh['span'=64,'chord'=8] {'chord'}, dimensions={0} | all-to-all | bytes 524288 | tf_op jit(solution)/shard_map/all_to_all | solution.py:436
  52.6 0.6 shard_map.80
  53.2 4.3 %collective-permute-start.12 = (f32[64,384]{1,0:T(8,128)S(1)}, f32[64,384]{1,0:T(8,128)S(1)}, u32[]{:S(2)}, u32[]{:S(2)}) collective-permute-start(f32[64,384]{1,0:T(8,128)S(1)} %get-tuple-element.173), channel_id=1, source_target_pairs={{0,8},{8,16},{16,24},{24,32},{32,40},{40,48},{48,56},{56,64},{64,7... | collective-permute-start | bytes 294920 | tf_op jit(solution)/shard_map/ppermute | solution.py:432
  57.5 1.3 collective-permute-start.13
  58.8 1.5 collective-permute-start.14
  60.3 3.3 %shard_map.81 = (f32[64,1536]{1,0:T(8,128)S(1)}, f32[64,1536]{1,0:T(8,128)S(1)}, f32[64,128]{1,0:T(8,128)S(1)}, f32[64,1536]{1,0:T(8,128)S(1)}, f32[64,128]{1,0:T(8,128)S(1)}, /*index=5*/f32[64,1536]{1,0:T(8,128)S(1)}) custom-call(f32[64,384]{1,0:T(8,128)S(1)} %collective-permute-done.8.from0.refs_0_, f32[64,384]{1,0:T(8,128)S(1)} %collective-permute-done.9.from1.refs_1_, ...), custom_call_target="tpu_custom_call" | custom-call | flops 1000000000 | bytes 1000000 | tf_op jit(solution)/shard_map/pallas_call | solution.py:523
  63.6 1.0 collective-permute-done.15.from3.refs_3_
  64.6 0.3 shard_map.82
  64.9 11.3 %all_to_all.37.got = f32[8,64,128]{2,1,0:T(8,128)S(1)} all-to-all(f32[8,64,128]{2,1,0:T(8,128)S(1)} %shard_map.82), channel_id=1, replica_groups=mesh['span'=64,'chord'=8] {'chord'}, dimensions={0} | all-to-all | bytes 524288 | tf_op jit(solution)/shard_map/all_to_all | solution.py:436
  76.2 0.6 shard_map.83
  76.8 4.3 %collective-permute-start.16 = (f32[64,384]{1,0:T(8,128)S(1)}, f32[64,384]{1,0:T(8,128)S(1)}, u32[]{:S(2)}, u32[]{:S(2)}) collective-permute-start(f32[64,384]{1,0:T(8,128)S(1)} %get-tuple-element.184), channel_id=1, source_target_pairs={{0,8},{8,16},{16,24},{24,32},{32,40},{40,48},{48,56},{56,64},{64,7... | collective-permute-start | bytes 294920 | tf_op jit(solution)/shard_map/ppermute | solution.py:432
  81.1 1.6 collective-permute-start.17
  82.7 1.5 collective-permute-start.18
  84.2 3.3 %shard_map.84 = (f32[64,1536]{1,0:T(8,128)S(1)}, f32[64,1536]{1,0:T(8,128)S(1)}, f32[64,128]{1,0:T(8,128)S(1)}, f32[64,1536]{1,0:T(8,128)S(1)}, f32[64,128]{1,0:T(8,128)S(1)}, /*index=5*/f32[64,1536]{1,0:T(8,128)S(1)}) custom-call(f32[64,384]{1,0:T(8,128)S(1)} %collective-permute-done.12.from0.refs_0_, f32[64,384]{1,0:T(8,128)S(1)} %collective-permute-done.13.from1.refs_1_, ...), custom_call_target="tpu_custom_call" | custom-call | flops 1000000000 | bytes 1000000 | tf_op jit(solution)/shard_map/pallas_call | solution.py:523
  87.5 1.0 collective-permute-done.19.from3.refs_3_
  88.5 0.3 shard_map.85
  88.8 11.3 %all_to_all.38.got = f32[8,64,128]{2,1,0:T(8,128)S(1)} all-to-all(f32[8,64,128]{2,1,0:T(8,128)S(1)} %shard_map.85), channel_id=1, replica_groups=mesh['span'=64,'chord'=8] {'chord'}, dimensions={0} | all-to-all | bytes 524288 | tf_op jit(solution)/shard_map/all_to_all | solution.py:436
  100.1 0.6 shard_map.86
  100.7 4.3 %collective-permute-start.20 = (f32[64,384]{1,0:T(8,128)S(1)}, f32[64,384]{1,0:T(8,128)S(1)}, u32[]{:S(2)}, u32[]{:S(2)}) collective-permute-start(f32[64,384]{1,0:T(8,128)S(1)} %get-tuple-element.195), channel_id=1, source_target_pairs={{0,8},{8,16},{16,24},{24,32},{32,40},{40,48},{48,56},{56,64},{64,7... | collective-permute-start | bytes 294920 | tf_op jit(solution)/shard_map/ppermute | solution.py:432
  105.0 1.3 collective-permute-start.21
  106.3 1.5 collective-permute-start.22
  107.8 3.3 %shard_map.87 = (f32[64,1536]{1,0:T(8,128)S(1)}, f32[64,1536]{1,0:T(8,128)S(1)}, f32[64,128]{1,0:T(8,128)S(1)}, f32[64,1536]{1,0:T(8,128)S(1)}, f32[64,128]{1,0:T(8,128)S(1)}, /*index=5*/f32[64,1536]{1,0:T(8,128)S(1)}) custom-call(f32[64,384]{1,0:T(8,128)S(1)} %collective-permute-done.16.from0.refs_0_, f32[64,384]{1,0:T(8,128)S(1)} %collective-permute-done.17.from1.refs_1_, ...), custom_call_target="tpu_custom_call" | custom-call | flops 1000000000 | bytes 1000000 | tf_op jit(solution)/shard_map/pallas_call | solution.py:523
  111.1 0.7 collective-permute-done.21.from1.refs_1_
  111.9 0.2 collective-permute-done.23.from3.refs_3_
  112.1 0.3 shard_map.88
  112.4 11.3 %all_to_all.39.got = f32[8,64,128]{2,1,0:T(8,128)S(1)} all-to-all(f32[8,64,128]{2,1,0:T(8,128)S(1)} %shard_map.88), channel_id=1, replica_groups=mesh['span'=64,'chord'=8] {'chord'}, dimensions={0} | all-to-all | bytes 524288 | tf_op jit(solution)/shard_map/all_to_all | solution.py:436
  123.7 0.6 shard_map.89
  124.3 5.2 %collective-permute-start.24 = (f32[64,384]{1,0:T(8,128)S(1)}, f32[64,384]{1,0:T(8,128)S(1)}, u32[]{:S(2)}, u32[]{:S(2)}) collective-permute-start(f32[64,384]{1,0:T(8,128)S(1)} %get-tuple-element.213), channel_id=1, source_target_pairs={{0,8},{8,16},{16,24},{24,32},{32,40},{40,48},{48,56},{56,64},{64,7... | collective-permute-start | bytes 294920 | tf_op jit(solution)/shard_map/ppermute | solution.py:432
  129.5 1.5 collective-permute-start.25
  131.0 3.3 %shard_map.90 = (f32[64,1536]{1,0:T(8,128)}, f32[64,1536]{1,0:T(8,128)S(1)}, f32[64,128]{1,0:T(8,128)S(1)}) custom-call(f32[64,384]{1,0:T(8,128)S(1)} %collective-permute-done.20.from0.refs_0_, f32[64,384]{1,0:T(8,128)S(1)} %collective-permute-done.21.from1.refs_1_, f32[64,384]{1,0:T(8,128)S(1)} %collective-permute-done.22.from2.refs_2_, ...), custom_call_target="tpu_custom_call" | custom-call | flops 1000000000 | bytes 1000000 | tf_op jit(solution)/shard_map/pallas_call | solution.py:523
  134.3 0.2 shard_map.91
  134.6 25.6 %all_to_all.40.got = f32[32,8,128]{2,1,0:T(8,128)S(1)} all-to-all(f32[32,8,128]{2,1,0:T(8,128)S(1)} %shard_map.91), channel_id=1, replica_groups={{0,1,2,3,4,5,6,7,128,129,130,131,132,133,134,135,256,257,258,259,260,26..., dimensions={0} | all-to-all | bytes 262144 | tf_op jit(solution)/shard_map/all_to_all | solution.py:436
  160.2 0.6 shard_map.92
  160.8 5.0 %all-to-all-start.6 = ((f32[16,8,128]{2,1,0:T(8,128)}), f32[16,8,128]{2,1,0:T(8,128)S(1)}, u32[]{:S(2)}, u32[]{:S(2)}) async-start(f32[16,8,128]{2,1,0:T(8,128)} %shard_map.92), calls=%async_computation.6 | async-start | bytes 131072 | tf_op jit(solution)/shard_map/all_to_all | solution.py:436
  165.9 11.6 %all-to-all-done.6.got = f32[16,8,128]{2,1,0:T(8,128)S(1)} async-done(((f32[16,8,128]{2,1,0:T(8,128)}), f32[16,8,128]{2,1,0:T(8,128)S(1)}, u32[]{:S(2)}, u32[]{:S(2)}) %all-to-all-start.6) | async-done | bytes 65568 | tf_op jit(solution)/shard_map/all_to_all | solution.py:436
  177.5 1.3 shard_map.93
  179.5 1.0 conditional.1
  180.5 0.7 copy-done.6
  (29 shorter events, 0.1 us)
Async XLA Ops:
  6.5 25.2 %copy-start.1 = (bf16[1,1,64,1536]{3,2,1,0:T(8,128)(2,1)S(1)}, bf16[1,1,64,1536]{3,2,1,0:T(8,128)(2,1)}, u32[]{:S(2)}) copy-start(bf16[1,1,64,1536]{3,2,1,0:T(8,128)(2,1)} %param.12) | copy-start | bytes 589828
  6.5 30.2 %slice-start = ((s8[4718592]{0:T(1024)(128)(4,1)}), s8[4194304]{0:T(1024)(128)(4,1)S(1)}, s32[]{:S(2)}) async-start(s8[4718592]{0:T(1024)(128)(4,1)} %bitcast.151), calls=%async_computation.9 | async-start | bytes 8388608
  30.0 6.7 %slice-start.1 = ((s8[4718592]{0:T(1024)(128)(4,1)}), s8[524288]{0:T(1024)(128)(4,1)S(1)}, s32[]{:S(2)}) async-start(s8[4718592]{0:T(1024)(128)(4,1)} %bitcast.151), calls=%async_computation.10 | async-start | bytes 1048576
  33.0 7.4 %collective-permute-start.8 = (f32[64,384]{1,0:T(8,128)S(1)}, f32[64,384]{1,0:T(8,128)S(1)}, u32[]{:S(2)}, u32[]{:S(2)}) collective-permute-start(f32[64,384]{1,0:T(8,128)S(1)} %get-tuple-element.164), channel_id=1, source_target_pairs={{0,8},{8,16},{16,24},{24,32},{32,40},{40,48},{48,56},{56,64},{64,7... | collective-permute-start | bytes 294920 | tf_op jit(solution)/shard_map/ppermute | solution.py:432
  34.3 6.1 %collective-permute-start.9 = (f32[64,384]{1,0:T(8,128)S(1)}, f32[64,384]{1,0:T(8,128)S(1)}, u32[]{:S(2)}, u32[]{:S(2)}) collective-permute-start(f32[64,384]{1,0:T(8,128)S(1)} %get-tuple-element.165), channel_id=1, source_target_pairs={{8,0},{16,8},{24,16},{32,24},{40,32},{48,40},{56,48},{64,56},{72,6... | collective-permute-start | bytes 294920 | tf_op jit(solution)/shard_map/ppermute | solution.py:432
  35.6 4.8 %collective-permute-start.10 = (f32[64,384]{1,0:T(8,128)S(1)}, f32[64,384]{1,0:T(8,128)S(1)}, u32[]{:S(2)}, u32[]{:S(2)}) collective-permute-start(f32[64,384]{1,0:T(8,128)S(1)} %get-tuple-element.166), channel_id=1, source_target_pairs={{0,1},{1,2},{2,3},{3,4},{4,5},{5,6},{6,7},{7,0},{8,9},{9,10},{10,1... | collective-permute-start | bytes 294920 | tf_op jit(solution)/shard_map/ppermute | solution.py:432
  36.7 4.3 %collective-permute-start.11 = (f32[64,384]{1,0:T(8,128)S(1)}, f32[64,384]{1,0:T(8,128)S(1)}, u32[]{:S(2)}, u32[]{:S(2)}) collective-permute-start(f32[64,384]{1,0:T(8,128)S(1)} %get-tuple-element.167), channel_id=1, source_target_pairs={{0,7},{1,0},{2,1},{3,2},{4,3},{5,4},{6,5},{7,6},{8,15},{9,8},{10,9... | collective-permute-start | bytes 294920 | tf_op jit(solution)/shard_map/ppermute | solution.py:432
  53.2 10.4 %collective-permute-start.12 = (f32[64,384]{1,0:T(8,128)S(1)}, f32[64,384]{1,0:T(8,128)S(1)}, u32[]{:S(2)}, u32[]{:S(2)}) collective-permute-start(f32[64,384]{1,0:T(8,128)S(1)} %get-tuple-element.173), channel_id=1, source_target_pairs={{0,8},{8,16},{16,24},{24,32},{32,40},{40,48},{48,56},{56,64},{64,7... | collective-permute-start | bytes 294920 | tf_op jit(solution)/shard_map/ppermute | solution.py:432
  57.5 6.1 %collective-permute-start.13 = (f32[64,384]{1,0:T(8,128)S(1)}, f32[64,384]{1,0:T(8,128)S(1)}, u32[]{:S(2)}, u32[]{:S(2)}) collective-permute-start(f32[64,384]{1,0:T(8,128)S(1)} %get-tuple-element.174), channel_id=1, source_target_pairs={{8,0},{16,8},{24,16},{32,24},{40,32},{48,40},{56,48},{64,56},{72,6... | collective-permute-start | bytes 294920 | tf_op jit(solution)/shard_map/ppermute | solution.py:432
  58.8 4.9 %collective-permute-start.14 = (f32[64,384]{1,0:T(8,128)S(1)}, f32[64,384]{1,0:T(8,128)S(1)}, u32[]{:S(2)}, u32[]{:S(2)}) collective-permute-start(f32[64,384]{1,0:T(8,128)S(1)} %get-tuple-element.175), channel_id=1, source_target_pairs={{0,1},{1,2},{2,3},{3,4},{4,5},{5,6},{6,7},{7,0},{8,9},{9,10},{10,1... | collective-permute-start | bytes 294920 | tf_op jit(solution)/shard_map/ppermute | solution.py:432
  60.3 4.3 %collective-permute-start.15 = (f32[64,384]{1,0:T(8,128)S(1)}, f32[64,384]{1,0:T(8,128)S(1)}, u32[]{:S(2)}, u32[]{:S(2)}) collective-permute-start(f32[64,384]{1,0:T(8,128)S(1)} %get-tuple-element.176), channel_id=1, source_target_pairs={{0,7},{1,0},{2,1},{3,2},{4,3},{5,4},{6,5},{7,6},{8,15},{9,8},{10,9... | collective-permute-start | bytes 294920 | tf_op jit(solution)/shard_map/ppermute | solution.py:432
  76.8 10.7 %collective-permute-start.16 = (f32[64,384]{1,0:T(8,128)S(1)}, f32[64,384]{1,0:T(8,128)S(1)}, u32[]{:S(2)}, u32[]{:S(2)}) collective-permute-start(f32[64,384]{1,0:T(8,128)S(1)} %get-tuple-element.184), channel_id=1, source_target_pairs={{0,8},{8,16},{16,24},{24,32},{32,40},{40,48},{48,56},{56,64},{64,7... | collective-permute-start | bytes 294920 | tf_op jit(solution)/shard_map/ppermute | solution.py:432
  81.1 6.5 %collective-permute-start.17 = (f32[64,384]{1,0:T(8,128)S(1)}, f32[64,384]{1,0:T(8,128)S(1)}, u32[]{:S(2)}, u32[]{:S(2)}) collective-permute-start(f32[64,384]{1,0:T(8,128)S(1)} %get-tuple-element.185), channel_id=1, source_target_pairs={{8,0},{16,8},{24,16},{32,24},{40,32},{48,40},{56,48},{64,56},{72,6... | collective-permute-start | bytes 294920 | tf_op jit(solution)/shard_map/ppermute | solution.py:432
  82.7 4.8 %collective-permute-start.18 = (f32[64,384]{1,0:T(8,128)S(1)}, f32[64,384]{1,0:T(8,128)S(1)}, u32[]{:S(2)}, u32[]{:S(2)}) collective-permute-start(f32[64,384]{1,0:T(8,128)S(1)} %get-tuple-element.186), channel_id=1, source_target_pairs={{0,1},{1,2},{2,3},{3,4},{4,5},{5,6},{6,7},{7,0},{8,9},{9,10},{10,1... | collective-permute-start | bytes 294920 | tf_op jit(solution)/shard_map/ppermute | solution.py:432
  84.2 4.3 %collective-permute-start.19 = (f32[64,384]{1,0:T(8,128)S(1)}, f32[64,384]{1,0:T(8,128)S(1)}, u32[]{:S(2)}, u32[]{:S(2)}) collective-permute-start(f32[64,384]{1,0:T(8,128)S(1)} %get-tuple-element.187), channel_id=1, source_target_pairs={{0,7},{1,0},{2,1},{3,2},{4,3},{5,4},{6,5},{7,6},{8,15},{9,8},{10,9... | collective-permute-start | bytes 294920 | tf_op jit(solution)/shard_map/ppermute | solution.py:432
  100.7 10.4 %collective-permute-start.20 = (f32[64,384]{1,0:T(8,128)S(1)}, f32[64,384]{1,0:T(8,128)S(1)}, u32[]{:S(2)}, u32[]{:S(2)}) collective-permute-start(f32[64,384]{1,0:T(8,128)S(1)} %get-tuple-element.195), channel_id=1, source_target_pairs={{0,8},{8,16},{16,24},{24,32},{32,40},{40,48},{48,56},{56,64},{64,7... | collective-permute-start | bytes 294920 | tf_op jit(solution)/shard_map/ppermute | solution.py:432
  105.0 6.9 %collective-permute-start.21 = (f32[64,384]{1,0:T(8,128)S(1)}, f32[64,384]{1,0:T(8,128)S(1)}, u32[]{:S(2)}, u32[]{:S(2)}) collective-permute-start(f32[64,384]{1,0:T(8,128)S(1)} %get-tuple-element.196), channel_id=1, source_target_pairs={{8,0},{16,8},{24,16},{32,24},{40,32},{48,40},{56,48},{64,56},{72,6... | collective-permute-start | bytes 294920 | tf_op jit(solution)/shard_map/ppermute | solution.py:432
  106.3 5.6 %collective-permute-start.22 = (f32[64,384]{1,0:T(8,128)S(1)}, f32[64,384]{1,0:T(8,128)S(1)}, u32[]{:S(2)}, u32[]{:S(2)}) collective-permute-start(f32[64,384]{1,0:T(8,128)S(1)} %get-tuple-element.197), channel_id=1, source_target_pairs={{0,1},{1,2},{2,3},{3,4},{4,5},{5,6},{6,7},{7,0},{8,9},{9,10},{10,1... | collective-permute-start | bytes 294920 | tf_op jit(solution)/shard_map/ppermute | solution.py:432
  107.8 4.3 %collective-permute-start.23 = (f32[64,384]{1,0:T(8,128)S(1)}, f32[64,384]{1,0:T(8,128)S(1)}, u32[]{:S(2)}, u32[]{:S(2)}) collective-permute-start(f32[64,384]{1,0:T(8,128)S(1)} %get-tuple-element.198), channel_id=1, source_target_pairs={{0,7},{1,0},{2,1},{3,2},{4,3},{5,4},{6,5},{7,6},{8,15},{9,8},{10,9... | collective-permute-start | bytes 294920 | tf_op jit(solution)/shard_map/ppermute | solution.py:432
  124.3 10.1 %collective-permute-start.24 = (f32[64,384]{1,0:T(8,128)S(1)}, f32[64,384]{1,0:T(8,128)S(1)}, u32[]{:S(2)}, u32[]{:S(2)}) collective-permute-start(f32[64,384]{1,0:T(8,128)S(1)} %get-tuple-element.213), channel_id=1, source_target_pairs={{0,8},{8,16},{16,24},{24,32},{32,40},{40,48},{48,56},{56,64},{64,7... | collective-permute-start | bytes 294920 | tf_op jit(solution)/shard_map/ppermute | solution.py:432
  129.5 4.8 %collective-permute-start.25 = (f32[64,384]{1,0:T(8,128)S(1)}, f32[64,384]{1,0:T(8,128)S(1)}, u32[]{:S(2)}, u32[]{:S(2)}) collective-permute-start(f32[64,384]{1,0:T(8,128)S(1)} %get-tuple-element.215), channel_id=1, source_target_pairs={{0,1},{1,2},{2,3},{3,4},{4,5},{5,6},{6,7},{7,0},{8,9},{9,10},{10,1... | collective-permute-start | bytes 294920 | tf_op jit(solution)/shard_map/ppermute | solution.py:432
  131.0 48.4 %copy-start.2 = (s32[1,1,4,384]{3,2,1,0:T(4,128)S(1)}, s32[1,1,4,384]{3,2,1,0:T(4,128)}, u32[]{:S(2)}) copy-start(s32[1,1,4,384]{3,2,1,0:T(4,128)} %param.13) | copy-start | bytes 18436
  131.0 48.4 %copy-start.5 = (s32[1,1,4]{2,1,0:T(1,128)S(1)}, s32[1,1,4]{2,1,0:T(1,128)}, u32[]{:S(2)}) copy-start(s32[1,1,4]{2,1,0:T(1,128)} %param.14) | copy-start | bytes 52
  160.8 16.6 %all-to-all-start.6 = ((f32[16,8,128]{2,1,0:T(8,128)}), f32[16,8,128]{2,1,0:T(8,128)S(1)}, u32[]{:S(2)}, u32[]{:S(2)}) async-start(f32[16,8,128]{2,1,0:T(8,128)} %shard_map.92), calls=%async_computation.6 | async-start | bytes 131072 | tf_op jit(solution)/shard_map/all_to_all | solution.py:436
  180.5 0.7 copy-start.6

commit v5 on v4

--- a/solution.py
+++ b/solution.py
@@ -11,6 +11,8 @@
 F32 = jnp.float32
 BF16 = jnp.bfloat16
 PIVOT_FLOOR = 2e-5
+NOISE_BOUND = 2.5e-4
+ROUNDING = 1.2e-7
 GRAM_ROWS = 8
 
 
@@ -406,6 +408,10 @@
         solved.append(value)
         good = (pivot > PIVOT_FLOOR) & (scale[k] > 0.0) & (scale[k] < 1e30)
         fault = jnp.maximum(fault, jnp.where(good, 0.0, 1.0))
+    parts = [solved[k] * solved[k] / pivots[k] for k in range(n)]
+    noise = tree_sum([parts[k] / (pivots[k] * pivots[k]) for k in range(n)])
+    good = noise < (NOISE_BOUND / ROUNDING) ** 2 * tree_sum(parts)
+    fault = jnp.maximum(fault, jnp.where(good, 0.0, 1.0))
     coeffs = [solved[k] / pivots[k] for k in range(n)]
     for k in reversed(range(n)):
         for m in range(k + 1, n):

time: 189 us -> 188 us (level)
  no operation moved by 1% of the time
where the time goes in v5:
time: 188 us; the launch traced here: 187 us
  blocking collectives  91.2 us (49%)
  starting transfers between devices  37 us (20%)
  Pallas kernels  28.5 us (15%)
  waiting for transfers between devices  15.2 us (8%)
  between operations  14.4 us (8%)
    all_to_all x6, blocking collectives, exchange(): return lax.all_to_all(send, axis, 0, 0, axis_index_groups=groups)  91.2 us
    ppermute x18, starting transfers between devices, shifted(): return lax.ppermute(value, axis, pairs)  32 us
    pallas_call x4, Pallas kernels, shards(): call(functools.partial(local_kernel, step=step), (full, full, table) + ((...  13.3 us
    all_to_all x1, waiting for transfers between devices, exchange(): return lax.all_to_all(send, axis, 0, 0, axis_index_groups=groups)  11.6 us
    all_to_all x1, starting transfers between devices, exchange(): return lax.all_to_all(send, axis, 0, 0, axis_index_groups=groups)  5.04 us
  transfers between devices with their start and end apart: 19, of which 6 were waited for; matrix products, arithmetic and copies ran while one was open for 0% of the time, Pallas kernels for 9%

profile of v5, /device:TPU:1, one launch (start us, length us, event | category | flops | bytes accessed | tf_op | source)
XLA Modules:
  0.0 187.2 jit_solution(7589354686928347949)
XLA Ops:
  6.5 2.9 %shard_map.75 = (bf16[1536,1536]{1,0:T(8,128)(2,1)S(1)}, bf16[1536,128]{1,0:T(8,128)(2,1)S(1)}, f32[1,1536]{1,0:T(1,128)S(1)}, f32[8,168,128]{2,1,0:T(8,128)S(1)}) custom-call(s32[4]{0:T(128)} %bitcast.180, s32[1]{0:T(128)} %bitcast.29.turn_ref, bf16[1536,1536]{1,0:T(8,128)(2,1)} %bitcast.150, bf16[64,1536]{1,0:T(8,128)(2,1)} %bitcast.161, ...), custom_call_target="tpu_custom_call" | custom-call | tf_op jit(solution)/shard_map/pallas_call | solution.py:471
  9.5 20.5 %all_to_all.35.got = f32[8,168,128]{2,1,0:T(8,128)S(1)} all-to-all(f32[8,168,128]{2,1,0:T(8,128)S(1)} %get-tuple-element.160), channel_id=1, replica_groups=mesh['span'=64,'chord'=8] {'chord'}, dimensions={0} | all-to-all | bytes 1376256 | tf_op jit(solution)/shard_map/all_to_all | solution.py:442
  30.0 1.7 shard_map.76.lift
  31.7 1.2 shard_map.77
  33.0 1.3 collective-permute-start.8
  34.3 1.3 collective-permute-start.9
  35.6 1.1 collective-permute-start.10
  36.7 3.7 %shard_map.78 = (f32[64,1536]{1,0:T(8,128)S(1)}, f32[64,128]{1,0:T(8,128)S(1)}, f32[64,1536]{1,0:T(8,128)S(1)}, f32[64,128]{1,0:T(8,128)S(1)}, f32[64,1536]{1,0:...) custom-call(bf16[128,1536]{1,0:T(8,128)(2,1)S(1)} %get-tuple-element.168.field, ...), custom_call_target="tpu_custom_call" | custom-call | flops 1000000000 | bytes 1000000 | tf_op jit(solution)/shard_map/pallas_call | solution.py:518
  40.4 0.6 collective-permute-done.11.from3.refs_3_
  41.0 0.3 shard_map.79
  41.4 11.3 %all_to_all.36.got = f32[8,64,128]{2,1,0:T(8,128)S(1)} all-to-all(f32[8,64,128]{2,1,0:T(8,128)S(1)} %shard_map.79), channel_id=1, replica_groups=mesh['span'=64,'chord'=8] {'chord'}, dimensions={0} | all-to-all | bytes 524288 | tf_op jit(solution)/shard_map/all_to_all | solution.py:442
  52.6 0.6 shard_map.80
  53.2 4.3 %collective-permute-start.12 = (f32[64,384]{1,0:T(8,128)S(1)}, f32[64,384]{1,0:T(8,128)S(1)}, u32[]{:S(2)}, u32[]{:S(2)}) collective-permute-start(f32[64,384]{1,0:T(8,128)S(1)} %get-tuple-element.173), channel_id=1, source_target_pairs={{0,8},{8,16},{16,24},{24,32},{32,40},{40,48},{48,56},{56,64},{64,7... | collective-permute-start | bytes 294920 | tf_op jit(solution)/shard_map/ppermute | solution.py:438
  57.5 1.3 collective-permute-start.13
  58.8 1.5 collective-permute-start.14
  60.3 3.3 %shard_map.81 = (f32[64,1536]{1,0:T(8,128)S(1)}, f32[64,1536]{1,0:T(8,128)S(1)}, f32[64,128]{1,0:T(8,128)S(1)}, f32[64,1536]{1,0:T(8,128)S(1)}, f32[64,128]{1,0:T(8,128)S(1)}, /*index=5*/f32[64,1536]{1,0:T(8,128)S(1)}) custom-call(f32[64,384]{1,0:T(8,128)S(1)} %collective-permute-done.8.from0.refs_0_, f32[64,384]{1,0:T(8,128)S(1)} %collective-permute-done.9.from1.refs_1_, ...), custom_call_target="tpu_custom_call" | custom-call | flops 1000000000 | bytes 1000000 | tf_op jit(solution)/shard_map/pallas_call | solution.py:529
  63.6 1.0 collective-permute-done.15.from3.refs_3_
  64.6 0.3 shard_map.82
  64.9 11.3 %all_to_all.37.got = f32[8,64,128]{2,1,0:T(8,128)S(1)} all-to-all(f32[8,64,128]{2,1,0:T(8,128)S(1)} %shard_map.82), channel_id=1, replica_groups=mesh['span'=64,'chord'=8] {'chord'}, dimensions={0} | all-to-all | bytes 524288 | tf_op jit(solution)/shard_map/all_to_all | solution.py:442
  76.2 0.6 shard_map.83
  76.8 4.3 %collective-permute-start.16 = (f32[64,384]{1,0:T(8,128)S(1)}, f32[64,384]{1,0:T(8,128)S(1)}, u32[]{:S(2)}, u32[]{:S(2)}) collective-permute-start(f32[64,384]{1,0:T(8,128)S(1)} %get-tuple-element.184), channel_id=1, source_target_pairs={{0,8},{8,16},{16,24},{24,32},{32,40},{40,48},{48,56},{56,64},{64,7... | collective-permute-start | bytes 294920 | tf_op jit(solution)/shard_map/ppermute | solution.py:438
  81.0 1.7 collective-permute-start.17
  82.7 1.5 collective-permute-start.18
  84.2 3.3 %shard_map.84 = (f32[64,1536]{1,0:T(8,128)S(1)}, f32[64,1536]{1,0:T(8,128)S(1)}, f32[64,128]{1,0:T(8,128)S(1)}, f32[64,1536]{1,0:T(8,128)S(1)}, f32[64,128]{1,0:T(8,128)S(1)}, /*index=5*/f32[64,1536]{1,0:T(8,128)S(1)}) custom-call(f32[64,384]{1,0:T(8,128)S(1)} %collective-permute-done.12.from0.refs_0_, f32[64,384]{1,0:T(8,128)S(1)} %collective-permute-done.13.from1.refs_1_, ...), custom_call_target="tpu_custom_call" | custom-call | flops 1000000000 | bytes 1000000 | tf_op jit(solution)/shard_map/pallas_call | solution.py:529
  87.6 1.0 collective-permute-done.19.from3.refs_3_
  88.6 0.3 shard_map.85
  88.9 11.3 %all_to_all.38.got = f32[8,64,128]{2,1,0:T(8,128)S(1)} all-to-all(f32[8,64,128]{2,1,0:T(8,128)S(1)} %shard_map.85), channel_id=1, replica_groups=mesh['span'=64,'chord'=8] {'chord'}, dimensions={0} | all-to-all | bytes 524288 | tf_op jit(solution)/shard_map/all_to_all | solution.py:442
  100.1 0.6 shard_map.86
  100.7 4.3 %collective-permute-start.20 = (f32[64,384]{1,0:T(8,128)S(1)}, f32[64,384]{1,0:T(8,128)S(1)}, u32[]{:S(2)}, u32[]{:S(2)}) collective-permute-start(f32[64,384]{1,0:T(8,128)S(1)} %get-tuple-element.195), channel_id=1, source_target_pairs={{0,8},{8,16},{16,24},{24,32},{32,40},{40,48},{48,56},{56,64},{64,7... | collective-permute-start | bytes 294920 | tf_op jit(solution)/shard_map/ppermute | solution.py:438
  105.0 1.3 collective-permute-start.21
  106.3 1.5 collective-permute-start.22
  107.8 3.3 %shard_map.87 = (f32[64,1536]{1,0:T(8,128)S(1)}, f32[64,1536]{1,0:T(8,128)S(1)}, f32[64,128]{1,0:T(8,128)S(1)}, f32[64,1536]{1,0:T(8,128)S(1)}, f32[64,128]{1,0:T(8,128)S(1)}, /*index=5*/f32[64,1536]{1,0:T(8,128)S(1)}) custom-call(f32[64,384]{1,0:T(8,128)S(1)} %collective-permute-done.16.from0.refs_0_, f32[64,384]{1,0:T(8,128)S(1)} %collective-permute-done.17.from1.refs_1_, ...), custom_call_target="tpu_custom_call" | custom-call | flops 1000000000 | bytes 1000000 | tf_op jit(solution)/shard_map/pallas_call | solution.py:529
  111.2 0.8 collective-permute-done.21.from1.refs_1_
  111.9 0.2 collective-permute-done.23.from3.refs_3_
  112.1 0.3 shard_map.88
  112.5 11.3 %all_to_all.39.got = f32[8,64,128]{2,1,0:T(8,128)S(1)} all-to-all(f32[8,64,128]{2,1,0:T(8,128)S(1)} %shard_map.88), channel_id=1, replica_groups=mesh['span'=64,'chord'=8] {'chord'}, dimensions={0} | all-to-all | bytes 524288 | tf_op jit(solution)/shard_map/all_to_all | solution.py:442
  123.7 0.6 shard_map.89
  124.3 5.2 %collective-permute-start.24 = (f32[64,384]{1,0:T(8,128)S(1)}, f32[64,384]{1,0:T(8,128)S(1)}, u32[]{:S(2)}, u32[]{:S(2)}) collective-permute-start(f32[64,384]{1,0:T(8,128)S(1)} %get-tuple-element.213), channel_id=1, source_target_pairs={{0,8},{8,16},{16,24},{24,32},{32,40},{40,48},{48,56},{56,64},{64,7... | collective-permute-start | bytes 294920 | tf_op jit(solution)/shard_map/ppermute | solution.py:438
  129.6 1.5 collective-permute-start.25
  131.1 3.3 %shard_map.90 = (f32[64,1536]{1,0:T(8,128)}, f32[64,1536]{1,0:T(8,128)S(1)}, f32[64,128]{1,0:T(8,128)S(1)}) custom-call(f32[64,384]{1,0:T(8,128)S(1)} %collective-permute-done.20.from0.refs_0_, f32[64,384]{1,0:T(8,128)S(1)} %collective-permute-done.21.from1.refs_1_, f32[64,384]{1,0:T(8,128)S(1)} %collective-permute-done.22.from2.refs_2_, ...), custom_call_target="tpu_custom_call" | custom-call | flops 1000000000 | bytes 1000000 | tf_op jit(solution)/shard_map/pallas_call | solution.py:529
  134.4 0.2 shard_map.91
  134.6 25.6 %all_to_all.40.got = f32[32,8,128]{2,1,0:T(8,128)S(1)} all-to-all(f32[32,8,128]{2,1,0:T(8,128)S(1)} %shard_map.91), channel_id=1, replica_groups={{0,1,2,3,4,5,6,7,128,129,130,131,132,133,134,135,256,257,258,259,260,26..., dimensions={0} | all-to-all | bytes 262144 | tf_op jit(solution)/shard_map/all_to_all | solution.py:442
  160.2 0.6 shard_map.92
  160.9 5.0 %all-to-all-start.6 = ((f32[16,8,128]{2,1,0:T(8,128)}), f32[16,8,128]{2,1,0:T(8,128)S(1)}, u32[]{:S(2)}, u32[]{:S(2)}) async-start(f32[16,8,128]{2,1,0:T(8,128)} %shard_map.92), calls=%async_computation.6 | async-start | bytes 131072 | tf_op jit(solution)/shard_map/all_to_all | solution.py:442
  165.9 11.6 %all-to-all-done.6.got = f32[16,8,128]{2,1,0:T(8,128)S(1)} async-done(((f32[16,8,128]{2,1,0:T(8,128)}), f32[16,8,128]{2,1,0:T(8,128)S(1)}, u32[]{:S(2)}, u32[]{:S(2)}) %all-to-all-start.6) | async-done | bytes 65568 | tf_op jit(solution)/shard_map/all_to_all | solution.py:442
  177.5 1.3 shard_map.93
  179.5 0.1 conditional.1
  179.7 0.7 copy-done.6
  (29 shorter events, 0.1 us)
Async XLA Ops:
  6.5 25.2 %copy-start.1 = (bf16[1,1,64,1536]{3,2,1,0:T(8,128)(2,1)S(1)}, bf16[1,1,64,1536]{3,2,1,0:T(8,128)(2,1)}, u32[]{:S(2)}) copy-start(bf16[1,1,64,1536]{3,2,1,0:T(8,128)(2,1)} %param.12) | copy-start | bytes 589828
  6.5 30.2 %slice-start = ((s8[4718592]{0:T(1024)(128)(4,1)}), s8[4194304]{0:T(1024)(128)(4,1)S(1)}, s32[]{:S(2)}) async-start(s8[4718592]{0:T(1024)(128)(4,1)} %bitcast.151), calls=%async_computation.9 | async-start | bytes 8388608
  30.0 6.7 %slice-start.1 = ((s8[4718592]{0:T(1024)(128)(4,1)}), s8[524288]{0:T(1024)(128)(4,1)S(1)}, s32[]{:S(2)}) async-start(s8[4718592]{0:T(1024)(128)(4,1)} %bitcast.151), calls=%async_computation.10 | async-start | bytes 1048576
  33.0 7.4 %collective-permute-start.8 = (f32[64,384]{1,0:T(8,128)S(1)}, f32[64,384]{1,0:T(8,128)S(1)}, u32[]{:S(2)}, u32[]{:S(2)}) collective-permute-start(f32[64,384]{1,0:T(8,128)S(1)} %get-tuple-element.164), channel_id=1, source_target_pairs={{0,8},{8,16},{16,24},{24,32},{32,40},{40,48},{48,56},{56,64},{64,7... | collective-permute-start | bytes 294920 | tf_op jit(solution)/shard_map/ppermute | solution.py:438
  34.3 6.1 %collective-permute-start.9 = (f32[64,384]{1,0:T(8,128)S(1)}, f32[64,384]{1,0:T(8,128)S(1)}, u32[]{:S(2)}, u32[]{:S(2)}) collective-permute-start(f32[64,384]{1,0:T(8,128)S(1)} %get-tuple-element.165), channel_id=1, source_target_pairs={{8,0},{16,8},{24,16},{32,24},{40,32},{48,40},{56,48},{64,56},{72,6... | collective-permute-start | bytes 294920 | tf_op jit(solution)/shard_map/ppermute | solution.py:438
  35.6 4.8 %collective-permute-start.10 = (f32[64,384]{1,0:T(8,128)S(1)}, f32[64,384]{1,0:T(8,128)S(1)}, u32[]{:S(2)}, u32[]{:S(2)}) collective-permute-start(f32[64,384]{1,0:T(8,128)S(1)} %get-tuple-element.166), channel_id=1, source_target_pairs={{0,1},{1,2},{2,3},{3,4},{4,5},{5,6},{6,7},{7,0},{8,9},{9,10},{10,1... | collective-permute-start | bytes 294920 | tf_op jit(solution)/shard_map/ppermute | solution.py:438
  36.7 4.3 %collective-permute-start.11 = (f32[64,384]{1,0:T(8,128)S(1)}, f32[64,384]{1,0:T(8,128)S(1)}, u32[]{:S(2)}, u32[]{:S(2)}) collective-permute-start(f32[64,384]{1,0:T(8,128)S(1)} %get-tuple-element.167), channel_id=1, source_target_pairs={{0,7},{1,0},{2,1},{3,2},{4,3},{5,4},{6,5},{7,6},{8,15},{9,8},{10,9... | collective-permute-start | bytes 294920 | tf_op jit(solution)/shard_map/ppermute | solution.py:438
  53.2 10.4 %collective-permute-start.12 = (f32[64,384]{1,0:T(8,128)S(1)}, f32[64,384]{1,0:T(8,128)S(1)}, u32[]{:S(2)}, u32[]{:S(2)}) collective-permute-start(f32[64,384]{1,0:T(8,128)S(1)} %get-tuple-element.173), channel_id=1, source_target_pairs={{0,8},{8,16},{16,24},{24,32},{32,40},{40,48},{48,56},{56,64},{64,7... | collective-permute-start | bytes 294920 | tf_op jit(solution)/shard_map/ppermute | solution.py:438
  57.5 6.1 %collective-permute-start.13 = (f32[64,384]{1,0:T(8,128)S(1)}, f32[64,384]{1,0:T(8,128)S(1)}, u32[]{:S(2)}, u32[]{:S(2)}) collective-permute-start(f32[64,384]{1,0:T(8,128)S(1)} %get-tuple-element.174), channel_id=1, source_target_pairs={{8,0},{16,8},{24,16},{32,24},{40,32},{48,40},{56,48},{64,56},{72,6... | collective-permute-start | bytes 294920 | tf_op jit(solution)/shard_map/ppermute | solution.py:438
  58.8 4.9 %collective-permute-start.14 = (f32[64,384]{1,0:T(8,128)S(1)}, f32[64,384]{1,0:T(8,128)S(1)}, u32[]{:S(2)}, u32[]{:S(2)}) collective-permute-start(f32[64,384]{1,0:T(8,128)S(1)} %get-tuple-element.175), channel_id=1, source_target_pairs={{0,1},{1,2},{2,3},{3,4},{4,5},{5,6},{6,7},{7,0},{8,9},{9,10},{10,1... | collective-permute-start | bytes 294920 | tf_op jit(solution)/shard_map/ppermute | solution.py:438
  60.3 4.3 %collective-permute-start.15 = (f32[64,384]{1,0:T(8,128)S(1)}, f32[64,384]{1,0:T(8,128)S(1)}, u32[]{:S(2)}, u32[]{:S(2)}) collective-permute-start(f32[64,384]{1,0:T(8,128)S(1)} %get-tuple-element.176), channel_id=1, source_target_pairs={{0,7},{1,0},{2,1},{3,2},{4,3},{5,4},{6,5},{7,6},{8,15},{9,8},{10,9... | collective-permute-start | bytes 294920 | tf_op jit(solution)/shard_map/ppermute | solution.py:438
  76.8 10.8 %collective-permute-start.16 = (f32[64,384]{1,0:T(8,128)S(1)}, f32[64,384]{1,0:T(8,128)S(1)}, u32[]{:S(2)}, u32[]{:S(2)}) collective-permute-start(f32[64,384]{1,0:T(8,128)S(1)} %get-tuple-element.184), channel_id=1, source_target_pairs={{0,8},{8,16},{16,24},{24,32},{32,40},{40,48},{48,56},{56,64},{64,7... | collective-permute-start | bytes 294920 | tf_op jit(solution)/shard_map/ppermute | solution.py:438
  81.0 6.5 %collective-permute-start.17 = (f32[64,384]{1,0:T(8,128)S(1)}, f32[64,384]{1,0:T(8,128)S(1)}, u32[]{:S(2)}, u32[]{:S(2)}) collective-permute-start(f32[64,384]{1,0:T(8,128)S(1)} %get-tuple-element.185), channel_id=1, source_target_pairs={{8,0},{16,8},{24,16},{32,24},{40,32},{48,40},{56,48},{64,56},{72,6... | collective-permute-start | bytes 294920 | tf_op jit(solution)/shard_map/ppermute | solution.py:438
  82.7 4.8 %collective-permute-start.18 = (f32[64,384]{1,0:T(8,128)S(1)}, f32[64,384]{1,0:T(8,128)S(1)}, u32[]{:S(2)}, u32[]{:S(2)}) collective-permute-start(f32[64,384]{1,0:T(8,128)S(1)} %get-tuple-element.186), channel_id=1, source_target_pairs={{0,1},{1,2},{2,3},{3,4},{4,5},{5,6},{6,7},{7,0},{8,9},{9,10},{10,1... | collective-permute-start | bytes 294920 | tf_op jit(solution)/shard_map/ppermute | solution.py:438
  84.2 4.3 %collective-permute-start.19 = (f32[64,384]{1,0:T(8,128)S(1)}, f32[64,384]{1,0:T(8,128)S(1)}, u32[]{:S(2)}, u32[]{:S(2)}) collective-permute-start(f32[64,384]{1,0:T(8,128)S(1)} %get-tuple-element.187), channel_id=1, source_target_pairs={{0,7},{1,0},{2,1},{3,2},{4,3},{5,4},{6,5},{7,6},{8,15},{9,8},{10,9... | collective-permute-start | bytes 294920 | tf_op jit(solution)/shard_map/ppermute | solution.py:438
  100.7 10.4 %collective-permute-start.20 = (f32[64,384]{1,0:T(8,128)S(1)}, f32[64,384]{1,0:T(8,128)S(1)}, u32[]{:S(2)}, u32[]{:S(2)}) collective-permute-start(f32[64,384]{1,0:T(8,128)S(1)} %get-tuple-element.195), channel_id=1, source_target_pairs={{0,8},{8,16},{16,24},{24,32},{32,40},{40,48},{48,56},{56,64},{64,7... | collective-permute-start | bytes 294920 | tf_op jit(solution)/shard_map/ppermute | solution.py:438
  105.0 6.9 %collective-permute-start.21 = (f32[64,384]{1,0:T(8,128)S(1)}, f32[64,384]{1,0:T(8,128)S(1)}, u32[]{:S(2)}, u32[]{:S(2)}) collective-permute-start(f32[64,384]{1,0:T(8,128)S(1)} %get-tuple-element.196), channel_id=1, source_target_pairs={{8,0},{16,8},{24,16},{32,24},{40,32},{48,40},{56,48},{64,56},{72,6... | collective-permute-start | bytes 294920 | tf_op jit(solution)/shard_map/ppermute | solution.py:438
  106.3 5.6 %collective-permute-start.22 = (f32[64,384]{1,0:T(8,128)S(1)}, f32[64,384]{1,0:T(8,128)S(1)}, u32[]{:S(2)}, u32[]{:S(2)}) collective-permute-start(f32[64,384]{1,0:T(8,128)S(1)} %get-tuple-element.197), channel_id=1, source_target_pairs={{0,1},{1,2},{2,3},{3,4},{4,5},{5,6},{6,7},{7,0},{8,9},{9,10},{10,1... | collective-permute-start | bytes 294920 | tf_op jit(solution)/shard_map/ppermute | solution.py:438
  107.8 4.3 %collective-permute-start.23 = (f32[64,384]{1,0:T(8,128)S(1)}, f32[64,384]{1,0:T(8,128)S(1)}, u32[]{:S(2)}, u32[]{:S(2)}) collective-permute-start(f32[64,384]{1,0:T(8,128)S(1)} %get-tuple-element.198), channel_id=1, source_target_pairs={{0,7},{1,0},{2,1},{3,2},{4,3},{5,4},{6,5},{7,6},{8,15},{9,8},{10,9... | collective-permute-start | bytes 294920 | tf_op jit(solution)/shard_map/ppermute | solution.py:438
  124.3 10.1 %collective-permute-start.24 = (f32[64,384]{1,0:T(8,128)S(1)}, f32[64,384]{1,0:T(8,128)S(1)}, u32[]{:S(2)}, u32[]{:S(2)}) collective-permute-start(f32[64,384]{1,0:T(8,128)S(1)} %get-tuple-element.213), channel_id=1, source_target_pairs={{0,8},{8,16},{16,24},{24,32},{32,40},{40,48},{48,56},{56,64},{64,7... | collective-permute-start | bytes 294920 | tf_op jit(solution)/shard_map/ppermute | solution.py:438
  129.6 4.8 %collective-permute-start.25 = (f32[64,384]{1,0:T(8,128)S(1)}, f32[64,384]{1,0:T(8,128)S(1)}, u32[]{:S(2)}, u32[]{:S(2)}) collective-permute-start(f32[64,384]{1,0:T(8,128)S(1)} %get-tuple-element.215), channel_id=1, source_target_pairs={{0,1},{1,2},{2,3},{3,4},{4,5},{5,6},{6,7},{7,0},{8,9},{9,10},{10,1... | collective-permute-start | bytes 294920 | tf_op jit(solution)/shard_map/ppermute | solution.py:438
  131.1 48.4 %copy-start.2 = (s32[1,1,4,384]{3,2,1,0:T(4,128)S(1)}, s32[1,1,4,384]{3,2,1,0:T(4,128)}, u32[]{:S(2)}) copy-start(s32[1,1,4,384]{3,2,1,0:T(4,128)} %param.13) | copy-start | bytes 18436
  131.1 48.5 %copy-start.5 = (s32[1,1,4]{2,1,0:T(1,128)S(1)}, s32[1,1,4]{2,1,0:T(1,128)}, u32[]{:S(2)}) copy-start(s32[1,1,4]{2,1,0:T(1,128)} %param.14) | copy-start | bytes 52
  160.9 16.6 %all-to-all-start.6 = ((f32[16,8,128]{2,1,0:T(8,128)}), f32[16,8,128]{2,1,0:T(8,128)S(1)}, u32[]{:S(2)}, u32[]{:S(2)}) async-start(f32[16,8,128]{2,1,0:T(8,128)} %shard_map.92), calls=%async_computation.6 | async-start | bytes 131072 | tf_op jit(solution)/shard_map/all_to_all | solution.py:442
  179.7 0.7 copy-start.6

commit v6 on v5

--- a/solution.py
+++ b/solution.py
@@ -377,11 +377,9 @@
         send_ref[peer] = total
 
 
-def solve_kernel(got, *refs):
-    fields = refs[:ITERS]
-    out_ref, fault_ref = refs[ITERS:]
+def solve_kernel(got, coeff_ref, fault_ref):
     total = tree_sum([got[p] for p in range(got.shape[0])])
-    cases = out_ref.shape[0]
+    cases = coeff_ref.shape[0]
 
     def entry(row, col):
         slot = gram_slot(row, col)
@@ -423,6 +421,13 @@
     fault_ref[0, 0] = jnp.max(fault)
     spread = jnp.concatenate(coeffs + [jnp.zeros_like(coeffs[0])] * (8 - n), axis=0)
     spread = jnp.concatenate([spread, jnp.zeros_like(spread)], axis=1).T[:cases]
+    coeff_ref[...] = jnp.concatenate([spread, jnp.zeros((cases, 120), F32)], axis=1)
+
+
+def combine_kernel(coeff, *refs):
+    fields, out_ref = refs[:-1], refs[-1]
+    n = ITERS
+    spread = coeff[...]
     width = out_ref.shape[1] // 4
     for part in range(4):
         cols = slice(part * width, (part + 1) * width)
@@ -553,21 +558,21 @@
     got = exchange(send, ("span", "chord"), first)
     send = call(relay_kernel, shape((inner, GRAM_ROWS, 128), F32))(got)
     got = exchange(send, "span", second)
-    answer, fault = pl.pallas_call(
+    coeffs, fault = pl.pallas_call(
         solve_kernel,
-        out_shape=(shape((cases, unknowns), BF16), shape((1, 1), F32)),
+        out_shape=(table, shape((1, 1), F32)),
         out_specs=(
             pl.BlockSpec(memory_space=pltpu.VMEM),
             pl.BlockSpec(memory_space=pltpu.SMEM),
         ),
         compiler_params=pltpu.CompilerParams(vmem_limit_bytes=28 * 2**20),
-    )(got, *fields)
+    )(got)
     answer = lax.cond(
         fault[0, 0] > 0.0,
-        lambda answer, *arrays: plain_recurrence(*arrays),
-        lambda answer, *arrays: answer,
-        answer,
-        *originals,
+        lambda parts, arrays: plain_recurrence(*arrays),
+        lambda parts, arrays: call(combine_kernel, shape((cases, unknowns), BF16))(*parts),
+        (coeffs, *fields),
+        originals,
     )
     return answer[None, None]
 

time: 188 us -> 188 us (level)
  no operation moved by 1% of the time
where the time goes in v6:
time: 188 us; the launch traced here: 187 us
  blocking collectives  91.2 us (49%)
  starting transfers between devices  37 us (20%)
  Pallas kernels  28.8 us (15%)
  waiting for transfers between devices  15.2 us (8%)
  between operations  14.4 us (8%)
    all_to_all x6, blocking collectives, exchange(): return lax.all_to_all(send, axis, 0, 0, axis_index_groups=groups)  91.2 us
    ppermute x18, starting transfers between devices, shifted(): return lax.ppermute(value, axis, pairs)  32 us
    pallas_call x4, Pallas kernels, shards(): call(functools.partial(local_kernel, step=step), (full, full, table) + ((...  13.3 us
    all_to_all x1, waiting for transfers between devices, exchange(): return lax.all_to_all(send, axis, 0, 0, axis_index_groups=groups)  11.6 us
    all_to_all x1, starting transfers between devices, exchange(): return lax.all_to_all(send, axis, 0, 0, axis_index_groups=groups)  5.04 us
  transfers between devices with their start and end apart: 19, of which 6 were waited for; matrix products, arithmetic and copies ran while one was open for 0% of the time, Pallas kernels for 9%

profile of v6, /device:TPU:1, one launch (start us, length us, event | category | flops | bytes accessed | tf_op | source)
XLA Modules:
  0.0 187.4 jit_solution(6969845803941772041)
XLA Ops:
  6.5 2.9 %shard_map.75 = (bf16[1536,1536]{1,0:T(8,128)(2,1)S(1)}, bf16[1536,128]{1,0:T(8,128)(2,1)S(1)}, f32[1,1536]{1,0:T(1,128)S(1)}, f32[8,168,128]{2,1,0:T(8,128)S(1)}) custom-call(s32[4]{0:T(128)} %bitcast.181, s32[1]{0:T(128)} %bitcast.29.turn_ref, bf16[1536,1536]{1,0:T(8,128)(2,1)} %bitcast.150, bf16[64,1536]{1,0:T(8,128)(2,1)} %bitcast.161, ...), custom_call_target="tpu_custom_call" | custom-call | tf_op jit(solution)/shard_map/pallas_call | solution.py:476
  9.5 20.5 %all_to_all.35.got = f32[8,168,128]{2,1,0:T(8,128)S(1)} all-to-all(f32[8,168,128]{2,1,0:T(8,128)S(1)} %get-tuple-element.176), channel_id=1, replica_groups=mesh['span'=64,'chord'=8] {'chord'}, dimensions={0} | all-to-all | bytes 1376256 | tf_op jit(solution)/shard_map/all_to_all | solution.py:447
  30.0 1.7 shard_map.76.lift
  31.7 1.2 shard_map.77
  33.0 1.3 collective-permute-start.8
  34.3 1.3 collective-permute-start.9
  35.6 1.1 collective-permute-start.10
  36.7 3.7 %shard_map.78 = (f32[64,1536]{1,0:T(8,128)S(1)}, f32[64,128]{1,0:T(8,128)S(1)}, f32[64,1536]{1,0:T(8,128)S(1)}, f32[64,128]{1,0:T(8,128)S(1)}, f32[64,1536]{1,0:...) custom-call(bf16[128,1536]{1,0:T(8,128)(2,1)S(1)} %get-tuple-element.184.field, ...), custom_call_target="tpu_custom_call" | custom-call | flops 1000000000 | bytes 1000000 | tf_op jit(solution)/shard_map/pallas_call | solution.py:523
  40.4 0.6 collective-permute-done.11.from3.refs_3_
  41.0 0.3 shard_map.79
  41.4 11.3 %all_to_all.36.got = f32[8,64,128]{2,1,0:T(8,128)S(1)} all-to-all(f32[8,64,128]{2,1,0:T(8,128)S(1)} %shard_map.79), channel_id=1, replica_groups=mesh['span'=64,'chord'=8] {'chord'}, dimensions={0} | all-to-all | bytes 524288 | tf_op jit(solution)/shard_map/all_to_all | solution.py:447
  52.6 0.6 shard_map.80
  53.2 4.3 %collective-permute-start.12 = (f32[64,384]{1,0:T(8,128)S(1)}, f32[64,384]{1,0:T(8,128)S(1)}, u32[]{:S(2)}, u32[]{:S(2)}) collective-permute-start(f32[64,384]{1,0:T(8,128)S(1)} %get-tuple-element.189), channel_id=1, source_target_pairs={{0,8},{8,16},{16,24},{24,32},{32,40},{40,48},{48,56},{56,64},{64,7... | collective-permute-start | bytes 294920 | tf_op jit(solution)/shard_map/ppermute | solution.py:443
  57.5 1.3 collective-permute-start.13
  58.8 1.5 collective-permute-start.14
  60.3 3.3 %shard_map.81 = (f32[64,1536]{1,0:T(8,128)S(1)}, f32[64,1536]{1,0:T(8,128)S(1)}, f32[64,128]{1,0:T(8,128)S(1)}, f32[64,1536]{1,0:T(8,128)S(1)}, f32[64,128]{1,0:T(8,128)S(1)}, /*index=5*/f32[64,1536]{1,0:T(8,128)S(1)}) custom-call(f32[64,384]{1,0:T(8,128)S(1)} %collective-permute-done.8.from0.refs_0_, f32[64,384]{1,0:T(8,128)S(1)} %collective-permute-done.9.from1.refs_1_, ...), custom_call_target="tpu_custom_call" | custom-call | flops 1000000000 | bytes 1000000 | tf_op jit(solution)/shard_map/pallas_call | solution.py:534
  63.6 1.0 collective-permute-done.15.from3.refs_3_
  64.6 0.3 shard_map.82
  64.9 11.3 %all_to_all.37.got = f32[8,64,128]{2,1,0:T(8,128)S(1)} all-to-all(f32[8,64,128]{2,1,0:T(8,128)S(1)} %shard_map.82), channel_id=1, replica_groups=mesh['span'=64,'chord'=8] {'chord'}, dimensions={0} | all-to-all | bytes 524288 | tf_op jit(solution)/shard_map/all_to_all | solution.py:447
  76.2 0.6 shard_map.83
  76.8 4.3 %collective-permute-start.16 = (f32[64,384]{1,0:T(8,128)S(1)}, f32[64,384]{1,0:T(8,128)S(1)}, u32[]{:S(2)}, u32[]{:S(2)}) collective-permute-start(f32[64,384]{1,0:T(8,128)S(1)} %get-tuple-element.200), channel_id=1, source_target_pairs={{0,8},{8,16},{16,24},{24,32},{32,40},{40,48},{48,56},{56,64},{64,7... | collective-permute-start | bytes 294920 | tf_op jit(solution)/shard_map/ppermute | solution.py:443
  81.0 1.7 collective-permute-start.17
  82.7 1.5 collective-permute-start.18
  84.2 3.3 %shard_map.84 = (f32[64,1536]{1,0:T(8,128)S(1)}, f32[64,1536]{1,0:T(8,128)S(1)}, f32[64,128]{1,0:T(8,128)S(1)}, f32[64,1536]{1,0:T(8,128)S(1)}, f32[64,128]{1,0:T(8,128)S(1)}, /*index=5*/f32[64,1536]{1,0:T(8,128)S(1)}) custom-call(f32[64,384]{1,0:T(8,128)S(1)} %collective-permute-done.12.from0.refs_0_, f32[64,384]{1,0:T(8,128)S(1)} %collective-permute-done.13.from1.refs_1_, ...), custom_call_target="tpu_custom_call" | custom-call | flops 1000000000 | bytes 1000000 | tf_op jit(solution)/shard_map/pallas_call | solution.py:534
  87.6 1.0 collective-permute-done.19.from3.refs_3_
  88.6 0.3 shard_map.85
  88.9 11.3 %all_to_all.38.got = f32[8,64,128]{2,1,0:T(8,128)S(1)} all-to-all(f32[8,64,128]{2,1,0:T(8,128)S(1)} %shard_map.85), channel_id=1, replica_groups=mesh['span'=64,'chord'=8] {'chord'}, dimensions={0} | all-to-all | bytes 524288 | tf_op jit(solution)/shard_map/all_to_all | solution.py:447
  100.1 0.6 shard_map.86
  100.7 4.3 %collective-permute-start.20 = (f32[64,384]{1,0:T(8,128)S(1)}, f32[64,384]{1,0:T(8,128)S(1)}, u32[]{:S(2)}, u32[]{:S(2)}) collective-permute-start(f32[64,384]{1,0:T(8,128)S(1)} %get-tuple-element.211), channel_id=1, source_target_pairs={{0,8},{8,16},{16,24},{24,32},{32,40},{40,48},{48,56},{56,64},{64,7... | collective-permute-start | bytes 294920 | tf_op jit(solution)/shard_map/ppermute | solution.py:443
  105.0 1.3 collective-permute-start.21
  106.3 1.5 collective-permute-start.22
  107.8 3.3 %shard_map.87 = (f32[64,1536]{1,0:T(8,128)S(1)}, f32[64,1536]{1,0:T(8,128)S(1)}, f32[64,128]{1,0:T(8,128)S(1)}, f32[64,1536]{1,0:T(8,128)S(1)}, f32[64,128]{1,0:T(8,128)S(1)}, /*index=5*/f32[64,1536]{1,0:T(8,128)S(1)}) custom-call(f32[64,384]{1,0:T(8,128)S(1)} %collective-permute-done.16.from0.refs_0_, f32[64,384]{1,0:T(8,128)S(1)} %collective-permute-done.17.from1.refs_1_, ...), custom_call_target="tpu_custom_call" | custom-call | flops 1000000000 | bytes 1000000 | tf_op jit(solution)/shard_map/pallas_call | solution.py:534
  111.2 0.8 collective-permute-done.21.from1.refs_1_
  111.9 0.2 collective-permute-done.23.from3.refs_3_
  112.1 0.3 shard_map.88
  112.5 11.3 %all_to_all.39.got = f32[8,64,128]{2,1,0:T(8,128)S(1)} all-to-all(f32[8,64,128]{2,1,0:T(8,128)S(1)} %shard_map.88), channel_id=1, replica_groups=mesh['span'=64,'chord'=8] {'chord'}, dimensions={0} | all-to-all | bytes 524288 | tf_op jit(solution)/shard_map/all_to_all | solution.py:447
  123.7 0.6 shard_map.89
  124.3 5.2 %collective-permute-start.24 = (f32[64,384]{1,0:T(8,128)S(1)}, f32[64,384]{1,0:T(8,128)S(1)}, u32[]{:S(2)}, u32[]{:S(2)}) collective-permute-start(f32[64,384]{1,0:T(8,128)S(1)} %get-tuple-element.229), channel_id=1, source_target_pairs={{0,8},{8,16},{16,24},{24,32},{32,40},{40,48},{48,56},{56,64},{64,7... | collective-permute-start | bytes 294920 | tf_op jit(solution)/shard_map/ppermute | solution.py:443
  129.6 1.5 collective-permute-start.25
  131.1 3.3 %shard_map.90 = (f32[64,1536]{1,0:T(8,128)}, f32[64,1536]{1,0:T(8,128)S(1)}, f32[64,128]{1,0:T(8,128)S(1)}) custom-call(f32[64,384]{1,0:T(8,128)S(1)} %collective-permute-done.20.from0.refs_0_, f32[64,384]{1,0:T(8,128)S(1)} %collective-permute-done.21.from1.refs_1_, f32[64,384]{1,0:T(8,128)S(1)} %collective-permute-done.22.from2.refs_2_, ...), custom_call_target="tpu_custom_call" | custom-call | flops 1000000000 | bytes 1000000 | tf_op jit(solution)/shard_map/pallas_call | solution.py:534
  134.6 25.6 %all_to_all.40.got = f32[32,8,128]{2,1,0:T(8,128)S(1)} all-to-all(f32[32,8,128]{2,1,0:T(8,128)S(1)} %shard_map.91), channel_id=1, replica_groups={{0,1,2,3,4,5,6,7,128,129,130,131,132,133,134,135,256,257,258,259,260,26..., dimensions={0} | all-to-all | bytes 262144 | tf_op jit(solution)/shard_map/all_to_all | solution.py:447
  160.2 0.6 shard_map.92
  160.9 5.0 %all-to-all-start.6 = ((f32[16,8,128]{2,1,0:T(8,128)}), f32[16,8,128]{2,1,0:T(8,128)S(1)}, u32[]{:S(2)}, u32[]{:S(2)}) async-start(f32[16,8,128]{2,1,0:T(8,128)} %shard_map.92), calls=%async_computation.6 | async-start | bytes 131072 | tf_op jit(solution)/shard_map/all_to_all | solution.py:447
  165.9 11.6 %all-to-all-done.6.got = f32[16,8,128]{2,1,0:T(8,128)S(1)} async-done(((f32[16,8,128]{2,1,0:T(8,128)}), f32[16,8,128]{2,1,0:T(8,128)S(1)}, u32[]{:S(2)}, u32[]{:S(2)}) %all-to-all-start.6) | async-done | bytes 65568 | tf_op jit(solution)/shard_map/all_to_all | solution.py:447
  177.5 1.3 shard_map.93
  179.5 0.4 conditional.1
  179.5 0.2 branch_0_fun.1
  179.9 0.7 copy-done.3
  (30 shorter events, 0.2 us)
Async XLA Ops:
  6.5 25.2 %copy-start.1 = (bf16[1,1,64,1536]{3,2,1,0:T(8,128)(2,1)S(1)}, bf16[1,1,64,1536]{3,2,1,0:T(8,128)(2,1)}, u32[]{:S(2)}) copy-start(bf16[1,1,64,1536]{3,2,1,0:T(8,128)(2,1)} %param.12) | copy-start | bytes 589828
  6.5 30.2 %slice-start = ((s8[4718592]{0:T(1024)(128)(4,1)}), s8[4194304]{0:T(1024)(128)(4,1)S(1)}, s32[]{:S(2)}) async-start(s8[4718592]{0:T(1024)(128)(4,1)} %bitcast.151), calls=%async_computation.9 | async-start | bytes 8388608
  30.0 6.7 %slice-start.1 = ((s8[4718592]{0:T(1024)(128)(4,1)}), s8[524288]{0:T(1024)(128)(4,1)S(1)}, s32[]{:S(2)}) async-start(s8[4718592]{0:T(1024)(128)(4,1)} %bitcast.151), calls=%async_computation.10 | async-start | bytes 1048576
  33.0 7.4 %collective-permute-start.8 = (f32[64,384]{1,0:T(8,128)S(1)}, f32[64,384]{1,0:T(8,128)S(1)}, u32[]{:S(2)}, u32[]{:S(2)}) collective-permute-start(f32[64,384]{1,0:T(8,128)S(1)} %get-tuple-element.180), channel_id=1, source_target_pairs={{0,8},{8,16},{16,24},{24,32},{32,40},{40,48},{48,56},{56,64},{64,7... | collective-permute-start | bytes 294920 | tf_op jit(solution)/shard_map/ppermute | solution.py:443
  34.3 6.1 %collective-permute-start.9 = (f32[64,384]{1,0:T(8,128)S(1)}, f32[64,384]{1,0:T(8,128)S(1)}, u32[]{:S(2)}, u32[]{:S(2)}) collective-permute-start(f32[64,384]{1,0:T(8,128)S(1)} %get-tuple-element.181), channel_id=1, source_target_pairs={{8,0},{16,8},{24,16},{32,24},{40,32},{48,40},{56,48},{64,56},{72,6... | collective-permute-start | bytes 294920 | tf_op jit(solution)/shard_map/ppermute | solution.py:443
  35.6 4.8 %collective-permute-start.10 = (f32[64,384]{1,0:T(8,128)S(1)}, f32[64,384]{1,0:T(8,128)S(1)}, u32[]{:S(2)}, u32[]{:S(2)}) collective-permute-start(f32[64,384]{1,0:T(8,128)S(1)} %get-tuple-element.182), channel_id=1, source_target_pairs={{0,1},{1,2},{2,3},{3,4},{4,5},{5,6},{6,7},{7,0},{8,9},{9,10},{10,1... | collective-permute-start | bytes 294920 | tf_op jit(solution)/shard_map/ppermute | solution.py:443
  36.7 4.3 %collective-permute-start.11 = (f32[64,384]{1,0:T(8,128)S(1)}, f32[64,384]{1,0:T(8,128)S(1)}, u32[]{:S(2)}, u32[]{:S(2)}) collective-permute-start(f32[64,384]{1,0:T(8,128)S(1)} %get-tuple-element.183), channel_id=1, source_target_pairs={{0,7},{1,0},{2,1},{3,2},{4,3},{5,4},{6,5},{7,6},{8,15},{9,8},{10,9... | collective-permute-start | bytes 294920 | tf_op jit(solution)/shard_map/ppermute | solution.py:443
  53.2 10.4 %collective-permute-start.12 = (f32[64,384]{1,0:T(8,128)S(1)}, f32[64,384]{1,0:T(8,128)S(1)}, u32[]{:S(2)}, u32[]{:S(2)}) collective-permute-start(f32[64,384]{1,0:T(8,128)S(1)} %get-tuple-element.189), channel_id=1, source_target_pairs={{0,8},{8,16},{16,24},{24,32},{32,40},{40,48},{48,56},{56,64},{64,7... | collective-permute-start | bytes 294920 | tf_op jit(solution)/shard_map/ppermute | solution.py:443
  57.5 6.1 %collective-permute-start.13 = (f32[64,384]{1,0:T(8,128)S(1)}, f32[64,384]{1,0:T(8,128)S(1)}, u32[]{:S(2)}, u32[]{:S(2)}) collective-permute-start(f32[64,384]{1,0:T(8,128)S(1)} %get-tuple-element.190), channel_id=1, source_target_pairs={{8,0},{16,8},{24,16},{32,24},{40,32},{48,40},{56,48},{64,56},{72,6... | collective-permute-start | bytes 294920 | tf_op jit(solution)/shard_map/ppermute | solution.py:443
  58.8 4.9 %collective-permute-start.14 = (f32[64,384]{1,0:T(8,128)S(1)}, f32[64,384]{1,0:T(8,128)S(1)}, u32[]{:S(2)}, u32[]{:S(2)}) collective-permute-start(f32[64,384]{1,0:T(8,128)S(1)} %get-tuple-element.191), channel_id=1, source_target_pairs={{0,1},{1,2},{2,3},{3,4},{4,5},{5,6},{6,7},{7,0},{8,9},{9,10},{10,1... | collective-permute-start | bytes 294920 | tf_op jit(solution)/shard_map/ppermute | solution.py:443
  60.3 4.3 %collective-permute-start.15 = (f32[64,384]{1,0:T(8,128)S(1)}, f32[64,384]{1,0:T(8,128)S(1)}, u32[]{:S(2)}, u32[]{:S(2)}) collective-permute-start(f32[64,384]{1,0:T(8,128)S(1)} %get-tuple-element.192), channel_id=1, source_target_pairs={{0,7},{1,0},{2,1},{3,2},{4,3},{5,4},{6,5},{7,6},{8,15},{9,8},{10,9... | collective-permute-start | bytes 294920 | tf_op jit(solution)/shard_map/ppermute | solution.py:443
  76.8 10.8 %collective-permute-start.16 = (f32[64,384]{1,0:T(8,128)S(1)}, f32[64,384]{1,0:T(8,128)S(1)}, u32[]{:S(2)}, u32[]{:S(2)}) collective-permute-start(f32[64,384]{1,0:T(8,128)S(1)} %get-tuple-element.200), channel_id=1, source_target_pairs={{0,8},{8,16},{16,24},{24,32},{32,40},{40,48},{48,56},{56,64},{64,7... | collective-permute-start | bytes 294920 | tf_op jit(solution)/shard_map/ppermute | solution.py:443
  81.0 6.5 %collective-permute-start.17 = (f32[64,384]{1,0:T(8,128)S(1)}, f32[64,384]{1,0:T(8,128)S(1)}, u32[]{:S(2)}, u32[]{:S(2)}) collective-permute-start(f32[64,384]{1,0:T(8,128)S(1)} %get-tuple-element.201), channel_id=1, source_target_pairs={{8,0},{16,8},{24,16},{32,24},{40,32},{48,40},{56,48},{64,56},{72,6... | collective-permute-start | bytes 294920 | tf_op jit(solution)/shard_map/ppermute | solution.py:443
  82.7 4.8 %collective-permute-start.18 = (f32[64,384]{1,0:T(8,128)S(1)}, f32[64,384]{1,0:T(8,128)S(1)}, u32[]{:S(2)}, u32[]{:S(2)}) collective-permute-start(f32[64,384]{1,0:T(8,128)S(1)} %get-tuple-element.202), channel_id=1, source_target_pairs={{0,1},{1,2},{2,3},{3,4},{4,5},{5,6},{6,7},{7,0},{8,9},{9,10},{10,1... | collective-permute-start | bytes 294920 | tf_op jit(solution)/shard_map/ppermute | solution.py:443
  84.2 4.3 %collective-permute-start.19 = (f32[64,384]{1,0:T(8,128)S(1)}, f32[64,384]{1,0:T(8,128)S(1)}, u32[]{:S(2)}, u32[]{:S(2)}) collective-permute-start(f32[64,384]{1,0:T(8,128)S(1)} %get-tuple-element.203), channel_id=1, source_target_pairs={{0,7},{1,0},{2,1},{3,2},{4,3},{5,4},{6,5},{7,6},{8,15},{9,8},{10,9... | collective-permute-start | bytes 294920 | tf_op jit(solution)/shard_map/ppermute | solution.py:443
  100.7 10.4 %collective-permute-start.20 = (f32[64,384]{1,0:T(8,128)S(1)}, f32[64,384]{1,0:T(8,128)S(1)}, u32[]{:S(2)}, u32[]{:S(2)}) collective-permute-start(f32[64,384]{1,0:T(8,128)S(1)} %get-tuple-element.211), channel_id=1, source_target_pairs={{0,8},{8,16},{16,24},{24,32},{32,40},{40,48},{48,56},{56,64},{64,7... | collective-permute-start | bytes 294920 | tf_op jit(solution)/shard_map/ppermute | solution.py:443
  105.0 6.9 %collective-permute-start.21 = (f32[64,384]{1,0:T(8,128)S(1)}, f32[64,384]{1,0:T(8,128)S(1)}, u32[]{:S(2)}, u32[]{:S(2)}) collective-permute-start(f32[64,384]{1,0:T(8,128)S(1)} %get-tuple-element.212), channel_id=1, source_target_pairs={{8,0},{16,8},{24,16},{32,24},{40,32},{48,40},{56,48},{64,56},{72,6... | collective-permute-start | bytes 294920 | tf_op jit(solution)/shard_map/ppermute | solution.py:443
  106.3 5.6 %collective-permute-start.22 = (f32[64,384]{1,0:T(8,128)S(1)}, f32[64,384]{1,0:T(8,128)S(1)}, u32[]{:S(2)}, u32[]{:S(2)}) collective-permute-start(f32[64,384]{1,0:T(8,128)S(1)} %get-tuple-element.213), channel_id=1, source_target_pairs={{0,1},{1,2},{2,3},{3,4},{4,5},{5,6},{6,7},{7,0},{8,9},{9,10},{10,1... | collective-permute-start | bytes 294920 | tf_op jit(solution)/shard_map/ppermute | solution.py:443
  107.8 4.3 %collective-permute-start.23 = (f32[64,384]{1,0:T(8,128)S(1)}, f32[64,384]{1,0:T(8,128)S(1)}, u32[]{:S(2)}, u32[]{:S(2)}) collective-permute-start(f32[64,384]{1,0:T(8,128)S(1)} %get-tuple-element.214), channel_id=1, source_target_pairs={{0,7},{1,0},{2,1},{3,2},{4,3},{5,4},{6,5},{7,6},{8,15},{9,8},{10,9... | collective-permute-start | bytes 294920 | tf_op jit(solution)/shard_map/ppermute | solution.py:443
  124.3 10.1 %collective-permute-start.24 = (f32[64,384]{1,0:T(8,128)S(1)}, f32[64,384]{1,0:T(8,128)S(1)}, u32[]{:S(2)}, u32[]{:S(2)}) collective-permute-start(f32[64,384]{1,0:T(8,128)S(1)} %get-tuple-element.229), channel_id=1, source_target_pairs={{0,8},{8,16},{16,24},{24,32},{32,40},{40,48},{48,56},{56,64},{64,7... | collective-permute-start | bytes 294920 | tf_op jit(solution)/shard_map/ppermute | solution.py:443
  129.6 4.8 %collective-permute-start.25 = (f32[64,384]{1,0:T(8,128)S(1)}, f32[64,384]{1,0:T(8,128)S(1)}, u32[]{:S(2)}, u32[]{:S(2)}) collective-permute-start(f32[64,384]{1,0:T(8,128)S(1)} %get-tuple-element.231), channel_id=1, source_target_pairs={{0,1},{1,2},{2,3},{3,4},{4,5},{5,6},{6,7},{7,0},{8,9},{9,10},{10,1... | collective-permute-start | bytes 294920 | tf_op jit(solution)/shard_map/ppermute | solution.py:443
  131.1 48.4 %copy-start.2 = (s32[1,1,4,384]{3,2,1,0:T(4,128)S(1)}, s32[1,1,4,384]{3,2,1,0:T(4,128)}, u32[]{:S(2)}) copy-start(s32[1,1,4,384]{3,2,1,0:T(4,128)} %param.13) | copy-start | bytes 18436
  131.1 48.4 %copy-start.6 = (s32[1,1,4]{2,1,0:T(1,128)S(1)}, s32[1,1,4]{2,1,0:T(1,128)}, u32[]{:S(2)}) copy-start(s32[1,1,4]{2,1,0:T(1,128)} %param.14) | copy-start | bytes 52
  160.9 16.6 %all-to-all-start.6 = ((f32[16,8,128]{2,1,0:T(8,128)}), f32[16,8,128]{2,1,0:T(8,128)S(1)}, u32[]{:S(2)}, u32[]{:S(2)}) async-start(f32[16,8,128]{2,1,0:T(8,128)} %shard_map.92), calls=%async_computation.6 | async-start | bytes 131072 | tf_op jit(solution)/shard_map/all_to_all | solution.py:447
  179.9 0.7 copy-start.3
